TPU v7x, 32 devices: a whole 2x2x4 slice. The times are simulated.
32 devices in a mesh: clip: 8 (over z, y), chan: 4 (over x, core).
Axes of the slice: x: 2, y: 2, z: 4, core: 2. Of those that a mesh axis runs over, the one named last changes fastest.
Arguments:
- frames_in: bfloat16 [16, 16, 49, 2048], P('clip', None, None, 'chan'), may hold values from -15 to 15
- seg_counts: int32 [16], replicated, may hold values from 8 to 16, as said below
- w_reduce: bfloat16 [2048, 512], P(None, 'chan'), may hold values from -0.125 to 0.125
- gain_one: float32 [512], P('chan'), may hold values from 0.5 to 1.5
- shift_one: float32 [512], P('chan'), may hold values from -3 to 3
- w_spatial: bfloat16 [9, 512, 512], P(None, None, 'chan'), may hold values from -0.09375 to 0.09375
- gain_two: float32 [512], P('chan'), may hold values from 0.5 to 1.5
- shift_two: float32 [512], P('chan'), may hold values from -3 to 3
- near_kern: float32 [9, 512], P(None, 'chan'), may hold values from -2 to 2
- far_kern: float32 [9, 512], P(None, 'chan'), may hold values from -2 to 2
- w_expand: bfloat16 [512, 2048], P(None, 'chan'), may hold values from -0.25 to 0.25
- gain_three: float32 [2048], P('chan'), may hold values from 0.5 to 1.5
- shift_three: float32 [2048], P('chan'), may hold values from -3 to 3
- w_classes: bfloat16 [2048, 174], P('chan'), may hold values from -0.125 to 0.125
- class_bias: float32 [174], replicated, may hold values from -3 to 3
- out_grad: bfloat16 [16, 16, 49, 2048], P('clip', None, None, 'chan'), may hold values from -6 to 6
- logit_grad: bfloat16 [16, 174], P('clip'), may hold values from -6 to 6
Outputs:
- output: bfloat16 [16, 16, 49, 2048], P('clip', None, None, 'chan')
- logits: float32 [16, 174], P('clip')
- grad_frames: float32 [16, 16, 49, 2048], P('clip', None, None, 'chan')
- grad_w_reduce: float32 [2048, 512], P(None, 'chan')
- grad_gain_one: float32 [512], P('chan')
- grad_shift_one: float32 [512], P('chan')
- grad_w_spatial: float32 [9, 512, 512], P(None, None, 'chan')
- grad_gain_two: float32 [512], P('chan')
- grad_shift_two: float32 [512], P('chan')
- grad_near: float32 [9, 512], P(None, 'chan')
- grad_far: float32 [9, 512], P(None, 'chan')
- grad_w_expand: float32 [512, 2048], P(None, 'chan')
- grad_gain_three: float32 [2048], P('chan')
- grad_shift_three: float32 [2048], P('chan')
- grad_w_classes: float32 [2048, 174], P('chan')
- grad_class_bias: float32 [174], replicated
Inputs may be any that keep to these rules, and one draw needn't show every extreme that they name: Each clip's valid segments are the first seg_counts of its 16 slots, either 8 or 16; clip 0 has 16 and clip 1 has 8.
All inputs are finite; a program needn't handle non-finite values.
Results may differ from a plain program's by a relative error of at most 0.024.
Values may be sent and summed in bfloat16 or wider, within the bound.
No kernel may reach another device: no remote copies, remote signals or barrier semaphores. Data moves between devices by JAX's collectives and lax.ppermute only.
A program may use at most 192 MiB of HBM per device.

v0:
```python
import jax
import jax.numpy as jnp
from jax import lax
from jax.sharding import PartitionSpec as P

SIDE = 7


EPSILON = 1e-05


def shifted_columns(frames, dilate, frame_side):
    padded = jnp.pad(frames, ((0, 0), (dilate, dilate), (dilate, dilate), (0, 0)))
    pieces = [
        padded[
            :,
            row_off * dilate : row_off * dilate + frame_side,
            col_off * dilate : col_off * dilate + frame_side,
            :,
        ]
        for row_off in range(3)
        for col_off in range(3)
    ]
    return jnp.stack(pieces, axis=3)


def temporal_gate(features, seg_mask, near_kern, far_kern):
    clip_count, seg_count, pixel_count, chan_count = features.shape
    following = jnp.concatenate([features[:, 1:], jnp.zeros_like(features[:, :1])], axis=1)
    next_valid = jnp.concatenate([seg_mask[:, 1:], jnp.zeros_like(seg_mask[:, :1])], axis=1)
    differ = next_valid[:, :, None, None] * (following - features)
    frames = differ.reshape(clip_count * seg_count, SIDE, SIDE, chan_count)
    near_sum = jnp.sum(shifted_columns(frames, 1, SIDE) * near_kern[None, None, None], axis=3)
    far_sum = jnp.sum(shifted_columns(frames, 2, SIDE) * far_kern[None, None, None], axis=3)
    gate_value = jax.nn.sigmoid(near_sum + far_sum).reshape(features.shape)
    return features * (1.0 + gate_value)


def normalize(activation, mask_rows, valid_total):
    sums, squares = lax.psum(
        (
            jnp.sum(activation * mask_rows, axis=0),
            jnp.sum(activation * activation * mask_rows, axis=0),
        ),
        "clip",
    )
    average = sums / valid_total
    inv_std = lax.rsqrt(squares / valid_total - average * average + EPSILON)
    return ((activation - average) * inv_std, inv_std)


def norm_back(grad_norm, normed, inv_std, gain_vec, mask_rows, valid_total):
    grad_gain, grad_shift = lax.psum(
        (jnp.sum(grad_norm * normed, axis=0), jnp.sum(grad_norm, axis=0)), "clip"
    )
    grad_act = (
        gain_vec
        * inv_std
        * (grad_norm - mask_rows * (grad_shift + normed * grad_gain) / valid_total)
    )
    return (grad_act, grad_gain, grad_shift)


def silu_slope(pre_act):
    logistic = jax.nn.sigmoid(pre_act)
    return logistic * (1.0 + pre_act * (1.0 - logistic))


def per_device(
    frames_in,
    seg_counts,
    w_reduce,
    gain_one,
    shift_one,
    w_spatial,
    gain_two,
    shift_two,
    near_kern,
    far_kern,
    w_expand,
    gain_three,
    shift_three,
    w_classes,
    class_bias,
    out_grad,
    logit_grad,
):
    clip_count, seg_count, pixel_count, chan_local = frames_in.shape
    mid_local = w_reduce.shape[1]
    mid_width = w_spatial.shape[1]
    row_count = clip_count * seg_count * pixel_count
    own_counts = lax.dynamic_slice_in_dim(
        seg_counts, lax.axis_index("clip") * clip_count, clip_count
    )
    seg_mask = (jnp.arange(seg_count)[None, :] < own_counts[:, None]).astype(jnp.float32)
    mask_rows = jnp.broadcast_to(
        seg_mask[:, :, None], (clip_count, seg_count, pixel_count)
    ).reshape(row_count, 1)
    valid_total = jnp.sum(seg_counts).astype(jnp.float32) * pixel_count
    count_scale = (1.0 / (own_counts.astype(jnp.float32) * pixel_count))[:, None]
    x_rows = frames_in.reshape(row_count, chan_local)
    x_whole = lax.all_gather(x_rows, "chan", axis=1, tiled=True)
    act_one = jnp.dot(x_whole, w_reduce, preferred_element_type=jnp.float32)
    normed_one, inv_one = normalize(act_one, mask_rows, valid_total)
    pre_one = gain_one * normed_one + shift_one
    hid_one = jax.nn.silu(pre_one).astype(jnp.bfloat16)
    full_one = lax.all_gather(hid_one, "chan", axis=1, tiled=True)
    columns = shifted_columns(
        full_one.reshape(clip_count * seg_count, SIDE, SIDE, mid_width), 1, SIDE
    ).reshape(row_count, 9 * mid_width)
    spatial_flat = w_spatial.reshape(9 * mid_width, mid_local)
    act_two = jnp.dot(columns, spatial_flat, preferred_element_type=jnp.float32)
    normed_two, inv_two = normalize(act_two, mask_rows, valid_total)
    pre_two = gain_two * normed_two + shift_two
    hid_two = jax.nn.silu(pre_two)

    def gate_local(features, near_weights, far_weights):
        return temporal_gate(features, seg_mask, near_weights, far_weights)

    gated, gate_back = jax.vjp(
        gate_local,
        hid_two.reshape(clip_count, seg_count, pixel_count, mid_local),
        near_kern,
        far_kern,
    )
    gated_low = gated.reshape(row_count, mid_local).astype(jnp.bfloat16)
    full_two = lax.all_gather(gated_low, "chan", axis=1, tiled=True)
    act_three = jnp.dot(full_two, w_expand, preferred_element_type=jnp.float32)
    normed_three, inv_three = normalize(act_three, mask_rows, valid_total)
    resid = x_rows.astype(jnp.float32) + gain_three * normed_three + shift_three
    output = mask_rows * jax.nn.silu(resid)
    pooled = (
        jnp.sum(output.reshape(clip_count, seg_count * pixel_count, chan_local), axis=1)
        * count_scale
    ).astype(jnp.bfloat16)
    logits = (
        lax.psum(jnp.dot(pooled, w_classes, preferred_element_type=jnp.float32), "chan")
        + class_bias
    )
    grad_classes = jnp.dot(pooled.T, logit_grad, preferred_element_type=jnp.float32)
    grad_bias = jnp.sum(logit_grad.astype(jnp.float32), axis=0)
    grad_pooled = jnp.dot(logit_grad, w_classes.T, preferred_element_type=jnp.float32) * count_scale
    spread_pooled = jnp.broadcast_to(
        grad_pooled[:, None, :], (clip_count, seg_count * pixel_count, chan_local)
    ).reshape(row_count, chan_local)
    grad_output = out_grad.reshape(row_count, chan_local).astype(jnp.float32) + spread_pooled
    grad_resid = grad_output * mask_rows * silu_slope(resid)
    grad_act_three, grad_gain_three, grad_shift_three = norm_back(
        grad_resid, normed_three, inv_three, gain_three, mask_rows, valid_total
    )
    low_three = grad_act_three.astype(jnp.bfloat16)
    grad_expand = jnp.dot(full_two.T, low_three, preferred_element_type=jnp.float32)
    grad_gated = lax.psum_scatter(
        jnp.dot(low_three, w_expand.T, preferred_element_type=jnp.float32).astype(jnp.bfloat16),
        "chan",
        scatter_dimension=1,
        tiled=True,
    ).astype(jnp.float32)
    grad_hid_two, grad_near, grad_far = gate_back(
        grad_gated.reshape(clip_count, seg_count, pixel_count, mid_local)
    )
    grad_pre_two = grad_hid_two.reshape(row_count, mid_local) * silu_slope(pre_two)
    grad_act_two, grad_gain_two, grad_shift_two = norm_back(
        grad_pre_two, normed_two, inv_two, gain_two, mask_rows, valid_total
    )
    low_two = grad_act_two.astype(jnp.bfloat16)
    grad_spatial = jnp.dot(columns.T, low_two, preferred_element_type=jnp.float32).reshape(
        9, mid_width, mid_local
    )
    grad_columns = jnp.dot(low_two, spatial_flat.T, preferred_element_type=jnp.float32)

    def to_columns(grid_in):
        return shifted_columns(grid_in, 1, SIDE).reshape(row_count, 9 * mid_width)

    unused_cols, column_back = jax.vjp(
        to_columns, jnp.zeros((clip_count * seg_count, SIDE, SIDE, mid_width), jnp.float32)
    )
    grad_field = column_back(grad_columns)[0].reshape(row_count, mid_width)
    grad_hid_one = lax.psum_scatter(
        grad_field.astype(jnp.bfloat16), "chan", scatter_dimension=1, tiled=True
    ).astype(jnp.float32)
    grad_pre_one = grad_hid_one * silu_slope(pre_one)
    grad_act_one, grad_gain_one, grad_shift_one = norm_back(
        grad_pre_one, normed_one, inv_one, gain_one, mask_rows, valid_total
    )
    low_one = grad_act_one.astype(jnp.bfloat16)
    grad_reduce = jnp.dot(x_whole.T, low_one, preferred_element_type=jnp.float32)
    grad_through = lax.psum_scatter(
        jnp.dot(low_one, w_reduce.T, preferred_element_type=jnp.float32).astype(jnp.bfloat16),
        "chan",
        scatter_dimension=1,
        tiled=True,
    ).astype(jnp.float32)
    grad_input = grad_resid + grad_through
    summed = lax.psum(
        (grad_reduce, grad_spatial, grad_near, grad_far, grad_expand, grad_classes, grad_bias),
        "clip",
    )
    return (
        output.reshape(frames_in.shape).astype(jnp.bfloat16),
        logits,
        grad_input.reshape(frames_in.shape),
        summed[0],
        grad_gain_one,
        grad_shift_one,
        summed[1],
        grad_gain_two,
        grad_shift_two,
        summed[2],
        summed[3],
        summed[4],
        grad_gain_three,
        grad_shift_three,
        summed[5],
        summed[6],
    )


def solution(mesh):
    in_specs = (
        P("clip", None, None, "chan"),
        P(),
        P(None, "chan"),
        P("chan"),
        P("chan"),
        P(None, None, "chan"),
        P("chan"),
        P("chan"),
        P(None, "chan"),
        P(None, "chan"),
        P(None, "chan"),
        P("chan"),
        P("chan"),
        P("chan", None),
        P(),
        P("clip", None, None, "chan"),
        P("clip", None),
    )
    out_specs = (
        P("clip", None, None, "chan"),
        P("clip", None),
        P("clip", None, None, "chan"),
        P(None, "chan"),
        P("chan"),
        P("chan"),
        P(None, None, "chan"),
        P("chan"),
        P("chan"),
        P(None, "chan"),
        P(None, "chan"),
        P(None, "chan"),
        P("chan"),
        P("chan"),
        P("chan", None),
        P(),
    )
    return jax.shard_map(
        per_device, mesh=mesh, in_specs=in_specs, out_specs=out_specs, check_vma=False
    )
```

profile of v0, /device:TPU:0, one launch (start us, length us, event | category | flops | bytes accessed | tf_op | source)
XLA Modules:
  0.0 746.7 jit_solution(10301680562772278200)
XLA Ops:
  12.8 48.3 %all-gather.4.cloned.1.call-done = bf16[1568,2048]{1,0:T(8,128)(2,1)} async-done(((bf16[1568,512]{1,0:T(8,128)(2,1)}), bf16[1568,2048]{1,0:T(8,128)(2,1)}) %all-gather.4.cloned.1.call-update) | async-done | bytes 6422544 | tf_op jit(solution)/shard_map/all_gather | solution.py:102
  61.1 4.7 multiply_reduce_fusion.11
  65.8 21.4 %all-reduce.38 = (f32[128]{0:T(128)S(1)}, f32[128]{0:T(128)S(1)}) all-reduce(f32[128]{0:T(128)S(1)} %get-tuple-element.73, f32[128]{0:T(128)S(1)} %get-tuple-element.72), channel_id=1, replica_groups=mesh['clip'=8,'chan'=4] {'clip'}, use_global_device_ids=true, to_apply=%region_1.0 | all-reduce | flops 256 | bytes 2048 | tf_op jit(solution)/shard_map/psum | solution.py:40
  88.9 16.4 %all-gather.6.cloned.1.call-done = bf16[1568,512]{1,0:T(8,128)(2,1)} async-done(((bf16[1568,128]{1,0:T(8,128)(2,1)}), bf16[1568,512]{1,0:T(8,128)(2,1)}) %all-gather.6.cloned.1.call-update) | async-done | bytes 1605648 | tf_op jit(solution)/shard_map/all_gather | solution.py:107
  128.1 15.8 %copy.73 = bf16[32,7,7,9,512]{4,3,2,1,0:T(8,128)(2,1)} copy(bf16[32,7,7,9,512]{4,2,1,0,3:T(8,128)(2,1)} %fusion.18) | data formatting | bytes 28901376 | tf_op jit(solution)/shard_map/stack | solution.py:24
  143.9 25.9 %copy.113 = bf16[196,8,9,512]{3,1,2,0:T(8,128)(2,1)S(1)} copy(bf16[196,8,9,512]{3,2,1,0:T(8,128)(2,1)} %bitcast.234) | data formatting | bytes 28901376
  169.8 4.0 multiply_reduce_fusion.9
  174.9 21.5 %all-reduce.37 = (f32[128]{0:T(128)S(1)}, f32[128]{0:T(128)S(1)}) all-reduce(f32[128]{0:T(128)S(1)} %get-tuple-element.71, f32[128]{0:T(128)S(1)} %get-tuple-element.70), channel_id=1, replica_groups=mesh['clip'=8,'chan'=4] {'clip'}, use_global_device_ids=true, to_apply=%region_6.7 | all-reduce | flops 256 | bytes 2048 | tf_op jit(solution)/shard_map/psum | solution.py:40
  214.2 4.2 copy.77
  218.4 3.7 reshape.175
  222.1 8.5 %all-gather.8.cloned.1.call-done = bf16[1568,512]{1,0:T(8,128)(2,1)} async-done(((bf16[1568,128]{1,0:T(8,128)(2,1)}), bf16[1568,512]{1,0:T(8,128)(2,1)}) %all-gather.8.cloned.1.call-update) | async-done | bytes 1605648 | tf_op jit(solution)/shard_map/all_gather | solution.py:127
  230.6 4.3 multiply_reduce_fusion.6
  234.9 21.3 %all-reduce.36 = (f32[512]{0:T(512)S(1)}, f32[512]{0:T(512)S(1)}) all-reduce(f32[512]{0:T(512)S(1)} %get-tuple-element.65, f32[512]{0:T(512)S(1)} %get-tuple-element.64), channel_id=1, replica_groups=mesh['clip'=8,'chan'=4] {'clip'}, use_global_device_ids=true, to_apply=%region_14.15 | all-reduce | flops 1024 | bytes 8192 | tf_op jit(solution)/shard_map/psum | solution.py:40
  256.3 6.7 fusion.64
  263.0 17.1 %all-reduce.35 = (f32[512]{0:T(512)S(1)}, f32[512]{0:T(512)S(1)}) all-reduce(f32[512]{0:T(512)S(1)} %get-tuple-element.67, f32[512]{0:T(512)S(1)} %get-tuple-element.66), channel_id=1, replica_groups=mesh['clip'=8,'chan'=4] {'clip'}, use_global_device_ids=true, to_apply=%region_20.21 | all-reduce | flops 1024 | bytes 8192 | tf_op jit(solution)/shard_map/psum | solution.py:53
  280.1 3.9 multiply_convert_fusion
  291.4 26.5 %reduce-scatter.10.cloned.1.call-done = bf16[128,1568]{1,0:T(8,128)(2,1)} async-done(((bf16[512,1568]{1,0:T(8,128)(2,1)}), bf16[128,1568]{1,0:T(8,128)(2,1)}) %reduce-scatter.10.cloned.1.call-update) | async-done | bytes 401424
  325.2 6.5 multiply_reduce_fusion
  341.7 21.5 %all-reduce.34 = (f32[128]{0:T(128)S(1)}, f32[128]{0:T(128)S(1)}) all-reduce(f32[128]{0:T(128)S(1)} %get-tuple-element.77, f32[128]{0:T(128)S(1)} %get-tuple-element.76), channel_id=1, replica_groups=mesh['clip'=8,'chan'=4] {'clip'}, use_global_device_ids=true, to_apply=%region_25.26 | all-reduce | flops 256 | bytes 2048 | tf_op jit(solution)/shard_map/psum | solution.py:53
  363.7 13.5 %fusion.19 = f32[32,7,7,9,512]{4,0,3,2,1:T(8,128)} fusion(bf16[9,512,128]{2,1,0:T(8,128)(2,1)S(1)} %copy-done, bf16[32,7,7,128,1]{3,2,1,0,4:T(8,128)(2,1)S(1)} %bitcast.244), kind=kOutput, calls=%fused_computation.80 | convolution fusion | flops 1849688064 | bytes 30482432 | tf_op jit(solution)/shard_map/dot_general | solution.py:170
  377.2 18.3 %slice_bitcast_fusion.8 = (f32[32,7,7,512]{3,0,2,1:T(8,128)}, f32[32,7,7,512]{3,0,2,1:T(8,128)}, f32[32,7,7,512]{3,0,2,1:T(8,128)}, f32[32,7,7,512]{3,0,2,1:T(8,...) fusion(f32[32,7,7,9,512]{4,0,3,2,1:T(8,128)} %fusion.19), kind=kLoop, calls=%fused_computation.38 | loop fusion | bytes 57802752 | tf_op jit(solution)/shard_map/transpose(jvp())/unstack | solution.py:24
  395.5 5.7 pad_add_fusion
  412.7 20.1 %copy.91 = bf16[4608,1568]{1,0:T(8,128)(2,1)} copy(bf16[4608,1568]{0,1:T(8,128)(2,1)} %bitcast.237) | data formatting | bytes 28901376 | tf_op jit(solution)/shard_map/dot_general | solution.py:167
  439.7 11.0 %fusion.58 = f32[9,512,128]{2,1,0:T(8,128)} fusion(bf16[9,512,1568]{2,1,0:T(8,128)(2,1)} %bitcast.235, bf16[1568,128]{1,0:T(8,128)(2,1)S(1)} %multiply_convert_fusion.2), kind=kOutput, calls=%fused_computation.172 | convolution fusion | flops 1849688064 | bytes 17211392 | tf_op jit(solution)/shard_map/dot_general | solution.py:167
  452.5 33.6 %all-reduce.33 = (f32[128]{0:T(128)S(1)}, f32[128]{0:T(128)S(1)}, f32[9,128]{1,0:T(8,128)}, f32[9,128]{1,0:T(8,128)}, f32[174]{0:T(256)}) all-reduce(f32[128]{0:T(128)S(1)} %get-tuple-element.69, f32[128]{0:T(128)S(1)} %get-tuple-element.68, f32[9,128]{1,0:T(8,128)S(1)} %get-tuple-element.75, ...), channel_id=1, replica_groups=mesh['clip'=8,'chan'=4] {'clip'}, use_global_device_ids=true, to_apply=%region_30.31 | all-reduce | flops 2734 | bytes 21872 | tf_op jit(solution)/shard_map/psum | solution.py:53
  486.1 5.5 convolution_bitcast_fusion
  492.6 4.7 convolution_convert_fusion
  500.9 6.3 psum.146
  507.8 153.2 %all-reduce.42.cloned.1.call-done = (f32[2048,128]{0,1:T(8,128)}, f32[9,512,128]{2,1,0:T(8,128)}, f32[512,512]{1,0:T(8,128)}, f32[512,174]{0,1:T(8,128)}) async-done(((f32[2048,128]{0,1:T(8,128)}, f32[9,512,128]{2,1,0:T(8,128)}, f32[512,512]{1,0:T(8,128)}, f32[512,174]{0,1:T(8,128)}), (f32[2048,128]{0,1:T(8,128)}, f32[9,512,128]{2,1,0:T(8,128)}, f32[512,512]{1,0:T(8,128)}, ...) | async-done | bytes 4812816 | tf_op jit(solution)/shard_map/psum | solution.py:195
  663.6 58.4 %reduce-scatter.8.cloned.1.call-done = bf16[1568,512]{1,0:T(8,128)(2,1)} async-done(((bf16[1568,2048]{1,0:T(8,128)(2,1)}), bf16[1568,512]{1,0:T(8,128)(2,1)}) %reduce-scatter.8.cloned.1.call-update) | async-done | bytes 1605648 | tf_op jit(solution)/shard_map/reduce_scatter | solution.py:188
  721.9 4.6 convert_add_fusion
  729.9 5.7 copy.94
  (204 shorter events, 108.2 us)
Async XLA Ops:
  7.2 162.6 %copy-start = (bf16[9,512,128]{2,1,0:T(8,128)(2,1)S(1)}, bf16[9,512,128]{2,1,0:T(8,128)(2,1)}, u32[]{:S(2)}) copy-start(bf16[9,512,128]{2,1,0:T(8,128)(2,1)} %param.22) | copy-start | bytes 3538948
  7.2 53.9 %all-gather.4.cloned.1.call-start = ((), (), s32[]{:S(2)}) async-start(), calls=%async_computation.3 | async-start | bytes 8028160 | tf_op jit(solution)/shard_map/all_gather | solution.py:102
  11.1 94.2 %all-gather.6.cloned.1.call-start = ((), (), s32[]{:S(2)}) async-start(), calls=%async_computation.4 | async-start | bytes 2007040 | tf_op jit(solution)/shard_map/all_gather | solution.py:107
  12.8 74.4 %copy-start.27 = (f32[128]{0:T(128)S(1)}, f32[128]{0:T(128)}, u32[]{:S(2)}) copy-start(f32[128]{0:T(128)} %param.20) | copy-start | bytes 1540
  12.8 74.9 %copy-start.37 = (f32[128]{0:T(128)S(1)}, f32[128]{0:T(128)}, u32[]{:S(2)}) copy-start(f32[128]{0:T(128)} %param.21) | copy-start | bytes 1540
  65.8 23.1 %copy-start.17 = (f32[1568,128]{1,0:T(8,128)}, f32[1568,128]{1,0:T(8,128)S(1)}, u32[]{:S(2)}) copy-start(f32[1568,128]{1,0:T(8,128)S(1)} %get-tuple-element.147) | copy-start | bytes 2408452
  88.8 141.8 %all-gather.8.cloned.1.call-start = ((), (), s32[]{:S(2)}) async-start(), calls=%async_computation.5 | async-start | bytes 2007040 | tf_op jit(solution)/shard_map/all_gather | solution.py:127
  169.8 26.7 %copy-start.24 = (f32[128]{0:T(128)S(1)}, f32[128]{0:T(128)}, u32[]{:S(2)}) copy-start(f32[128]{0:T(128)} %param.23) | copy-start | bytes 1540
  169.8 26.7 %copy-start.25 = (f32[128]{0:T(128)S(1)}, f32[128]{0:T(128)}, u32[]{:S(2)}) copy-start(f32[128]{0:T(128)} %param.24) | copy-start | bytes 1540
  214.1 103.7 %reduce-scatter.10.cloned.1.call-start = ((), (), s32[]{:S(2)}) async-start(), calls=%async_computation.7 | async-start | bytes 2129920
  222.1 34.2 %copy-start.26 = (f32[512]{0:T(512)S(1)}, f32[512]{0:T(512)}, u32[]{:S(2)}) copy-start(f32[512]{0:T(512)} %param.28) | copy-start | bytes 6148
  222.1 34.2 %copy-start.34 = (f32[512]{0:T(512)S(1)}, f32[512]{0:T(512)}, u32[]{:S(2)}) copy-start(f32[512]{0:T(512)} %param.29) | copy-start | bytes 6148
  290.9 159.8 %reduce-scatter.12.cloned.1.call-start = ((), (), s32[]{:S(2)}) async-start(), calls=%async_computation.8 | async-start | bytes 2129920
  363.3 13.9 %copy-start.40 = (f32[128]{0:T(128)}, f32[128]{0:T(128)S(1)}, u32[]{:S(2)}) copy-start(f32[128]{0:T(128)S(1)} %get-tuple-element.159) | copy-start | bytes 1540
  363.3 13.9 %copy-start.41 = (f32[128]{0:T(128)}, f32[128]{0:T(128)S(1)}, u32[]{:S(2)}) copy-start(f32[128]{0:T(128)S(1)} %get-tuple-element.160) | copy-start | bytes 1540
  395.4 5.8 copy-start.5
  395.4 6.6 copy-start.6
  395.5 7.6 %copy-start.7 = (f32[32,7,7,512]{3,0,2,1:T(8,128)S(1)}, f32[32,7,7,512]{3,0,2,1:T(8,128)}, u32[]{:S(2)}) copy-start(f32[32,7,7,512]{3,0,2,1:T(8,128)} %get-tuple-element.114) | copy-start | bytes 9633796
  395.5 8.5 %copy-start.8 = (f32[32,7,7,512]{3,0,2,1:T(8,128)S(1)}, f32[32,7,7,512]{3,0,2,1:T(8,128)}, u32[]{:S(2)}) copy-start(f32[32,7,7,512]{3,0,2,1:T(8,128)} %get-tuple-element.118) | copy-start | bytes 9633796
  395.5 9.4 %copy-start.9 = (f32[32,7,7,512]{3,0,2,1:T(8,128)S(1)}, f32[32,7,7,512]{3,0,2,1:T(8,128)}, u32[]{:S(2)}) copy-start(f32[32,7,7,512]{3,0,2,1:T(8,128)} %get-tuple-element.119) | copy-start | bytes 9633796
  412.5 248.6 %all-reduce.42.cloned.1.call-start = ((), (), s32[]{:S(2)}) async-start(), calls=%async_computation.9 | async-start | bytes 9633792 | tf_op jit(solution)/shard_map/psum | solution.py:195
  439.7 12.3 %copy-start.18 = (f32[1568,128]{1,0:T(8,128)S(1)}, f32[1568,128]{1,0:T(8,128)}, u32[]{:S(2)}) copy-start(f32[1568,128]{1,0:T(8,128)} %copy-done.17) | copy-start | bytes 2408452
  439.7 12.3 %copy-start.28 = (f32[128]{0:T(128)S(1)}, f32[128]{0:T(128)}, u32[]{:S(2)}) copy-start(f32[128]{0:T(128)} %param.20) | copy-start | bytes 1540
  439.7 12.3 %copy-start.30 = (f32[128]{0:T(128)S(1)}, f32[128]{0:T(128)}, u32[]{:S(2)}) copy-start(f32[128]{0:T(128)} %copy-done.29) | copy-start | bytes 1540
  439.7 12.3 %copy-start.32 = (f32[128]{0:T(128)S(1)}, f32[128]{0:T(128)}, u32[]{:S(2)}) copy-start(f32[128]{0:T(128)} %copy-done.31) | copy-start | bytes 1540
  439.7 12.3 %copy-start.38 = (f32[128]{0:T(128)S(1)}, f32[128]{0:T(128)}, u32[]{:S(2)}) copy-start(f32[128]{0:T(128)} %param.21) | copy-start | bytes 1540
  439.7 46.4 %copy-start.42 = (f32[128]{0:T(128)S(1)}, f32[128]{0:T(128)}, u32[]{:S(2)}) copy-start(f32[128]{0:T(128)} %get-tuple-element.97) | copy-start | bytes 1540
  486.1 5.6 copy-start.48
  486.1 5.6 copy-start.49
  491.6 230.4 %reduce-scatter.8.cloned.1.call-start = ((), (), s32[]{:S(2)}) async-start(), calls=%async_computation.6 | async-start | bytes 8028160 | tf_op jit(solution)/shard_map/reduce_scatter | solution.py:188
  497.3 9.9 %copy-start.39 = (f32[174]{0:T(256)S(1)}, f32[174]{0:T(256)}, u32[]{:S(2)}) copy-start(f32[174]{0:T(256)} %param.31) | copy-start | bytes 2092
  729.9 5.7 copy-start.19
  (25 other events, 67.0 us)
Sparse Core Ops, SparseCore 0:
  11.2 49.8 all-gather.3
  88.9 16.3 all-gather.5
  214.2 16.3 all-gather.7
  291.0 26.7 reduce-scatter.9
  412.6 25.2 reduce-scatter.11
  491.7 169.3 all-reduce.41
  663.8 58.1 reduce-scatter.7
where the time goes:
time: 752 us; the launch traced here: 747 us
  waiting for transfers between devices  311 us (41%)
  local copies, waits for them, and re-layouts  171 us (23%)
  blocking collectives  143 us (19%)
  matrix products  54.7 us (7%)
  other arithmetic  50.6 us (7%)
  between operations  15.8 us (2%)
    psum x1, waiting for transfers between devices, per_device(): lax.psum((grad_reduce, grad_spatial, grad_near, grad_far, grad_expand, gr...  153 us
    unnamed x134, local copies, waits for them, and re-layouts  78.8 us
    psum x3, blocking collectives, norm_back(): lax.psum((jnp.sum(grad_norm * normed, axis=0), jnp.sum(grad_norm, axis=0)...  72.3 us
    psum x3, blocking collectives, normalize(): lax.psum((jnp.sum(activation * mask_rows, axis=0), jnp.sum(activation * a...  64.2 us
    reduce_scatter x1, waiting for transfers between devices, per_device(): lax.psum_scatter(jnp.dot(low_one, w_reduce.T, preferred_element_type=jnp....  58.4 us
    all_gather x1, waiting for transfers between devices, per_device(): x_whole = lax.all_gather(x_rows, 'chan', axis=1, tiled=True)  48.3 us
    another operation x8, local copies, waits for them, and re-layouts, shifted_columns(): return jnp.stack(pieces, axis=3)  42.8 us
    unnamed x9, waiting for transfers between devices  26.6 us
  transfers between devices with their start and end apart: 7, of which 6 were waited for; matrix products, arithmetic and copies ran while one was open for 8% of the time, Pallas kernels for 0%

commit v1 on v0

v1 whole, which is shorter than its diff:
```python
import functools

import jax
import jax.numpy as jnp
from jax import lax
from jax.experimental import pallas as pl
from jax.experimental.pallas import tpu as pltpu
from jax.sharding import PartitionSpec as P

SIDE = 7
WIDE = SIDE + 1
EDGE = SIDE + 4
EPSILON = 1e-05
LANES = 128
F32 = jnp.float32
BF16 = jnp.bfloat16
VMEM_BYTES = 20 * 1024 * 1024


def silu_slope(pre_act):
    logistic = jax.nn.sigmoid(pre_act)
    return logistic * (1.0 + pre_act * (1.0 - logistic))


def seg_index(row_count, seg_count):
    return lax.broadcasted_iota(jnp.int32, (row_count, 1), 0) % seg_count


def dot32(left, right, dims=((1,), (0,))):
    return lax.dot_general(left, right, (dims, ((), ())), preferred_element_type=F32)


class Pick:
    def __init__(self, array, index):
        self.array = array
        self.index = index


class Free:
    def __init__(self, array):
        self.array = array


class Near:
    def __init__(self, array):
        self.array = array


class Arriving:
    def __init__(self, copy, ref):
        self.copy = copy
        self.ref = ref
        self.shape = ref.shape

    def __getitem__(self, index):
        if self.copy is not None:
            self.copy.wait()
            self.copy = None
        return self.ref[index]


def near(shape, kind):
    return pltpu.VMEM(shape, kind)


def call(body, out_shape, scratch=(), deps=(), ints=None, floats=None):
    single = not isinstance(out_shape, (tuple, list))
    shapes = (out_shape,) if single else tuple(out_shape)
    away = [isinstance(out, jax.ShapeDtypeStruct) for out in shapes]
    outs = tuple(pltpu.HBM(out.shape, out.dtype) if far else out for out, far in zip(shapes, away))
    scalars = [array for array in (ints, floats) if array is not None]

    def bare(arg):
        while isinstance(arg, (Pick, Free, Near)):
            arg = arg.array
        return arg

    def placed(arg):
        inner = arg.array if isinstance(arg, Pick) else arg
        if isinstance(inner, Free):
            return inner.array
        if isinstance(inner, Near):
            return pltpu.with_memory_space_constraint(inner.array, pltpu.VMEM)
        return pltpu.with_memory_space_constraint(inner, pltpu.HBM)

    def run(*args):
        fetched = [isinstance(arg, Pick) and not isinstance(arg.array, Near) for arg in args]
        buffers = [pltpu.VMEM(arg.array.shape[1:], arg.array.dtype) for arg, own in zip(args, fetched) if own]
        if buffers:
            buffers.append(pltpu.SemaphoreType.DMA((len(buffers),)))

        def kernel(*refs):
            first = refs[: len(scalars)]
            inputs = refs[len(scalars) : len(scalars) + len(args)]
            rest = refs[len(scalars) + len(args) + len(deps) :]
            results, local = rest[: len(outs)], rest[len(outs) : len(outs) + len(buffers)]
            rest = rest[len(outs) + len(buffers) :]
            passed = []
            for arg, ref, own in zip(args, inputs, fetched):
                if isinstance(arg, Pick):
                    ref = ref.at[arg.index if isinstance(arg.index, int) else arg.index(first[0])]
                if own:
                    place = sum(isinstance(each, Arriving) for each in passed)
                    copy = pltpu.make_async_copy(ref, local[place], local[-1].at[place])
                    copy.start()
                    ref = Arriving(copy, local[place])
                passed.append(ref)
            body(*first, *passed, *results, *rest)

        kernel.__name__ = getattr(body, "func", body).__name__
        anywhere = pl.BlockSpec(memory_space=pl.ANY)
        results = pl.pallas_call(
            kernel,
            out_shape=outs,
            in_specs=[SMEM] * len(scalars)
            + [anywhere if own else VMEM for own in fetched]
            + [anywhere] * len(deps),
            out_specs=[VMEM] * len(outs),
            scratch_shapes=buffers + list(scratch),
            compiler_params=pltpu.CompilerParams(vmem_limit_bytes=VMEM_BYTES),
        )(*scalars, *[placed(arg) for arg in args], *[bare(dep) for dep in deps])
        results = tuple(result if far else Near(result) for result, far in zip(results, away))
        return results[0] if single else results

    return run


SMEM = pl.BlockSpec(memory_space=pltpu.SMEM)
VMEM = pl.BlockSpec(memory_space=pltpu.VMEM)


def store_taps(cat_ref, line, values, line_rows, seg_count):
    depth = values.shape[1]
    for tap in range(3):
        start = ((line + 1) * WIDE + 1 - tap) * seg_count
        cat_ref[start : start + line_rows, tap * depth : (tap + 1) * depth] = values


def line_sums(values, row_of):
    return jnp.sum(values.reshape(-1, 8, values.shape[1]), axis=0) + row_of


def send_sums(sent_ref, total, cross):
    sums = jnp.concatenate([jnp.sum(total, axis=0, keepdims=True), jnp.sum(cross, axis=0, keepdims=True)], axis=0)
    if len(sent_ref.shape) == 2:
        sent_ref[0:2, :] = sums
        return
    for peer in range(sent_ref.shape[0]):
        sent_ref[peer, 0:2, :] = sums


def side_sums(got_ref, side):
    total = jnp.zeros((2, got_ref.shape[3]), F32)
    for clip in range(got_ref.shape[0]):
        for core in range(2):
            total += got_ref[clip, side * 2 + core, 0:2, :]
    return total


def norm_rows(sums, gain_vec, shift_vec, count):
    average = sums[0:1, :] / count
    inv_std = lax.rsqrt(sums[1:2, :] / count - average * average + EPSILON)
    return average, gain_vec * inv_std, shift_vec, inv_std


def line_mask(line_rows, seg_count, count):
    return (seg_index(line_rows, seg_count) < count).astype(F32)


def split_blocks(ints_ref, w_ref, *refs):
    size = refs[0].shape[0]
    for bits, ref in enumerate(refs):
        start = (ints_ref[0] ^ bits) * size
        ref[...] = w_ref[pl.ds(pl.multiple_of(start, size), size), :]


def reduce_other(ints_ref, own_ref, near_ref, far_ref, cross_ref, x_ref, part_ref, w_ref):
    core = ints_ref[3]
    size = own_ref.shape[1]
    for place, (first, second) in enumerate(((own_ref, near_ref), (far_ref, cross_ref))):
        for index, ref in ((core, first), (1 - core, second)):
            start = pl.multiple_of((2 * place + index) * size, size)
            w_ref[:, pl.ds(start, size)] = ref[...]
    part_ref[...] = dot32(x_ref[...], w_ref[...]).astype(BF16)


def add_low(near_ref, far_ref, out_ref):
    half = out_ref.shape[1]
    out_ref[...] = (far_ref[...] + near_ref[:, half:].astype(F32)).astype(BF16)


def pack_small(gain_one_ref, shift_one_ref, gain_two_ref, shift_two_ref, near_ref, far_ref, out_ref):
    out_ref[...] = jnp.zeros_like(out_ref)
    for row, ref in enumerate((gain_one_ref, shift_one_ref, gain_two_ref, shift_two_ref)):
        out_ref[row : row + 1, :] = ref[...]
    out_ref[4:13, :] = near_ref[...]
    out_ref[13:22, :] = far_ref[...]


def join_small(ints_ref, own_ref, near_ref, far_ref, cross_ref, out_ref):
    chan = 2 * ints_ref[1] + ints_ref[3]
    for bits, ref in enumerate((own_ref, near_ref, far_ref, cross_ref)):
        out_ref[chan ^ bits] = ref[...]


def small_row(small_ref, side, row):
    return jnp.concatenate([small_ref[2 * side + core, row : row + 1, :] for core in range(2)], axis=1)


def reduce_own(ints_ref, near_ref, w_ref, x_ref, part_ref, send_ref):
    half = w_ref.shape[1] // 2
    send = dot32(x_ref[...], w_ref[:, half:]) + near_ref[:, half:].astype(F32)
    send_ref[...] = send.astype(BF16)
    part_ref[...] = dot32(x_ref[...], w_ref[:, :half]) + near_ref[:, :half].astype(F32)


def first_sums(seg_count, ints_ref, part_ref, far_ref, act_ref, low_ref, sent_ref):
    line_rows = SIDE * seg_count
    mask = line_mask(line_rows, seg_count, ints_ref[0])
    total = cross = jnp.zeros((8, act_ref.shape[1]), F32)
    for line in range(SIDE):
        rows = slice(line * line_rows, (line + 1) * line_rows)
        act = part_ref[rows, :] + far_ref[rows, :].astype(F32)
        act_ref[rows, :] = act
        low_ref[rows, :] = act.astype(BF16)
        kept = act * mask
        total = line_sums(kept, total)
        cross = line_sums(kept * act, cross)
    send_sums(sent_ref, total, cross)


def conv_forward(
    seg_count, ints_ref, floats_ref, own_ref, oth_ref, got_ref, small_ref, w_ref,
    act_ref, low_ref, sent_ref, hid_ref, cat_ref, acc_ref,
):
    line_rows = SIDE * seg_count
    half = own_ref.shape[1]
    side = ints_ref[1]
    cat_ref[...] = jnp.zeros_like(cat_ref)
    own, oth = [
        norm_rows(side_sums(got_ref, index), small_row(small_ref, index, 0), small_row(small_ref, index, 1), floats_ref[0])
        for index in (side, 1 - side)
    ]
    average, scale, shift, _ = [jnp.concatenate(pieces, axis=1) for pieces in zip(own, oth)]
    for line in range(SIDE):
        rows = slice(line * line_rows, (line + 1) * line_rows)
        act = jnp.concatenate([own_ref[rows, :], oth_ref[rows, :].astype(F32)], axis=1)
        pre = (act - average) * scale + shift
        hid = (pre * jax.nn.sigmoid(pre)).astype(BF16)
        hid_ref[rows, :] = hid
        store_taps(cat_ref, line, hid, line_rows, seg_count)
    span = SIDE * WIDE * seg_count
    step = WIDE * seg_count
    for row_off in range(3):
        part = dot32(cat_ref[row_off * step : row_off * step + span, :], w_ref[row_off])
        if row_off == 0:
            acc_ref[...] = part
        else:
            acc_ref[...] += part
    mask = line_mask(line_rows, seg_count, ints_ref[0])
    total = cross = jnp.zeros((8, half), F32)
    for line in range(SIDE):
        rows = slice(line * line_rows, (line + 1) * line_rows)
        act = acc_ref[line * step : line * step + line_rows, :]
        act_ref[rows, :] = act
        low_ref[rows, :] = act.astype(BF16)
        kept = act * mask
        total = line_sums(kept, total)
        cross = line_sums(kept * act, cross)
    send_sums(sent_ref, total, cross)


def store_frames(pad_ref, line, values, line_rows, seg_count):
    start = ((line + 2) * EDGE + 2) * seg_count
    pad_ref[start : start + line_rows, :] = values


def load_frames(pad_ref, line, row_off, col_off, line_rows, seg_count):
    start = ((line + 2 + row_off) * EDGE + 2 + col_off) * seg_count
    return pad_ref[start : start + line_rows, :]


def tap_offsets():
    for index in range(9):
        yield index, index // 3 - 1, index % 3 - 1
    for index in range(9):
        yield 9 + index, 2 * (index // 3 - 1), 2 * (index % 3 - 1)


def next_mask(line_rows, seg_count, count):
    seg = seg_index(line_rows, seg_count)
    return (seg + 1 < jnp.minimum(count, seg_count)).astype(F32)


def gate_forward(
    seg_count, other, ints_ref, floats_ref, act_ref, got_ref, small_ref, gated_ref, *rest,
):
    hid_ref, gate_ref = (None, None) if other else rest[:2]
    roll_ref, pad_ref = rest[-2:]
    line_rows = SIDE * seg_count
    pad_ref[...] = jnp.zeros_like(pad_ref)
    roll_ref[...] = jnp.zeros_like(roll_ref)
    side = 1 - ints_ref[1] if other else ints_ref[1]
    sums = side_sums(got_ref, side)
    follows = next_mask(line_rows, seg_count, ints_ref[0])
    for core in range(act_ref.shape[1] // LANES):
        lanes = slice(core * LANES, (core + 1) * LANES)
        rows_for = small_ref.at[2 * side + core]
        average, scale, shift, _ = norm_rows(sums[:, lanes], rows_for[2:3, :], rows_for[3:4, :], floats_ref[0])
        for line in range(SIDE):
            rows = slice(line * line_rows, (line + 1) * line_rows)
            act = act_ref[rows, lanes].astype(F32)
            pre = (act - average) * scale + shift
            roll_ref[rows, :] = pre * jax.nn.sigmoid(pre)
        for line in range(SIDE):
            first = line * line_rows
            here = roll_ref[first : first + line_rows, :]
            after = roll_ref[first + 1 : first + 1 + line_rows, :]
            store_frames(pad_ref, line, follows * (after - here), line_rows, seg_count)
        for line in range(SIDE):
            rows = slice(line * line_rows, (line + 1) * line_rows)
            total = jnp.zeros((line_rows, LANES), F32)
            for index, row_off, col_off in tap_offsets():
                kern = rows_for[4 + index : 5 + index, :]
                total += load_frames(pad_ref, line, row_off, col_off, line_rows, seg_count) * kern
            gate = jax.nn.sigmoid(total)
            hid = roll_ref[rows, :]
            gated_ref[rows, lanes] = (hid * (1.0 + gate)).astype(BF16)
            if not other:
                hid_ref[rows, lanes] = hid
                gate_ref[rows, lanes] = gate


def expand(
    seg_count, ints_ref, own_ref, oth_ref, near_own_ref, near_oth_ref, w_ref, bias_ref, act_ref, sent_ref,
):
    half = own_ref.shape[1]
    row_count = own_ref.shape[0]
    line_rows = SIDE * seg_count
    side = ints_ref[1]
    w_own = w_ref[pl.ds(pl.multiple_of(side * half, half), half), :]
    w_oth = w_ref[pl.ds(pl.multiple_of((1 - side) * half, half), half), :]
    total = cross = jnp.zeros((8, w_ref.shape[1]), F32)
    for clip, (left, right) in enumerate(((own_ref, oth_ref), (near_own_ref, near_oth_ref))):
        act_ref[clip] = dot32(left[...], w_own) + dot32(right[...], w_oth)
        mask = line_mask(line_rows, seg_count, ints_ref[2 * clip])
        for line in range(SIDE):
            act = act_ref[clip, line * line_rows : (line + 1) * line_rows, :]
            kept = act * mask
            total = line_sums(kept, total)
            cross = line_sums(kept * act, cross)
    send_sums(sent_ref, total, cross)
    sent_ref[2:3, :] = bias_ref[...]


def finish(
    seg_count, ints_ref, floats_ref, got_ref, gain_ref, shift_ref, flat_ref, act_own_ref, x_own_ref, grad_own_ref,
    act_oth_ref, x_oth_ref, grad_oth_ref, out_ref, resid_ref, pooled_ref, sent_ref,
):
    line_rows = SIDE * seg_count
    width = act_own_ref.shape[1]
    average, _, shift, inv_std = norm_rows(got_ref, gain_ref[...], shift_ref[...], floats_ref[0])
    gain = gain_ref[...]
    total = cross = jnp.zeros((8, width), F32)
    own, oth = (act_own_ref, x_own_ref, grad_own_ref), (act_oth_ref, x_oth_ref, grad_oth_ref)
    for clip, (act_ref, x_ref, grad_ref) in enumerate((own, oth)):
        place = ints_ref[3] if clip == 0 else 1 - ints_ref[3]
        mask = line_mask(line_rows, seg_count, ints_ref[2 * clip])
        flat = flat_ref[clip : clip + 1, :]
        pool = jnp.zeros((8, width), F32)
        for line in range(SIDE):
            rows = slice(line * line_rows, (line + 1) * line_rows)
            normed = (act_ref[rows, :] - average) * inv_std
            resid = x_ref[rows, :].astype(F32) + gain * normed + shift
            logistic = jax.nn.sigmoid(resid)
            output = mask * resid * logistic
            out_ref[place, rows, :] = output.astype(BF16)
            pool = line_sums(output, pool)
            grad = (grad_ref[rows, :].astype(F32) + flat) * mask
            grad = grad * (logistic * (1.0 + resid * (1.0 - logistic)))
            resid_ref[clip, rows, :] = grad
            total = line_sums(grad, total)
            cross = line_sums(grad * normed, cross)
        pooled_ref[clip : clip + 1, :] = jnp.sum(pool, axis=0, keepdims=True) * floats_ref[1 + clip]
    send_sums(sent_ref, total, cross)


def expand_backward(
    seg_count, clip, ints_ref, floats_ref, got_ref, back_ref, gain_ref, resid_ref, act_ref, w_ref,
    low_ref, *part_refs,
):
    line_rows = SIDE * seg_count
    half = w_ref.shape[0] // 2
    side = ints_ref[1]
    average, scale, _, inv_std = norm_rows(got_ref, gain_ref[...], gain_ref[...], floats_ref[0])
    back = back_ref[0:2, :] / floats_ref[0]
    mask = line_mask(line_rows, seg_count, ints_ref[2 * clip])
    for line in range(SIDE):
        rows = slice(line * line_rows, (line + 1) * line_rows)
        normed = (act_ref[rows, :] - average) * inv_std
        grad = scale * (resid_ref[rows, :] - mask * (back[0:1, :] + normed * back[1:2, :]))
        low_ref[rows, :] = grad.astype(BF16)
    for place, index in enumerate((side, 1 - side)):
        w_side = w_ref[pl.ds(pl.multiple_of(index * half, half), half), :]
        part = dot32(low_ref[...], w_side, ((1,), (1,)))
        if clip == 0:
            part_refs[place][...] = part
        else:
            part_refs[0][:, place * half : (place + 1) * half] = part.astype(BF16)


def gate_backward(
    seg_count, ints_ref, floats_ref, grad_ref, near_ref, far_ref, hid_ref, gate_ref, act_ref, got_ref, small_ref,
    logit_ref, slope_ref, low_ref, sent_ref, kern_grad_ref, field_ref, pad_ref, back_ref,
):
    line_rows = SIDE * seg_count
    pad_ref[...] = jnp.zeros_like(pad_ref)
    field_ref[...] = jnp.zeros_like(field_ref)
    back_ref[...] = jnp.zeros_like(back_ref)
    kern_grad_ref[...] = jnp.zeros_like(kern_grad_ref)
    side = ints_ref[1]
    sums = side_sums(got_ref, side)
    follows = next_mask(line_rows, seg_count, ints_ref[0])
    totals_all, cross_all = [], []
    for core in range(act_ref.shape[1] // LANES):
        lanes = slice(core * LANES, (core + 1) * LANES)
        rows_for = small_ref.at[2 * side + core]
        average, scale, shift, inv_std = norm_rows(sums[:, lanes], rows_for[2:3, :], rows_for[3:4, :], floats_ref[0])

        def whole_grad(rows):
            return grad_ref[rows, lanes] + near_ref[rows, lanes].astype(F32) + far_ref[rows, lanes].astype(F32)

        for line in range(SIDE):
            first = line * line_rows
            rows = slice(first, first + line_rows)
            here = hid_ref[rows, lanes]
            if line < SIDE - 1:
                after = hid_ref[first + 1 : first + 1 + line_rows, lanes]
            else:
                after = jnp.concatenate([hid_ref[first + 1 : first + line_rows, lanes], here[:1, :]], axis=0)
            store_frames(pad_ref, line, follows * (after - here), line_rows, seg_count)
            gate = gate_ref[rows, lanes]
            store_frames(field_ref, line, whole_grad(rows) * here * gate * (1.0 - gate), line_rows, seg_count)
        totals = [jnp.zeros((8, LANES), F32) for _ in range(18)]
        for line in range(SIDE):
            field = load_frames(field_ref, line, 0, 0, line_rows, seg_count)
            back = jnp.zeros((line_rows, LANES), F32)
            for index, row_off, col_off in tap_offsets():
                shifted = load_frames(pad_ref, line, row_off, col_off, line_rows, seg_count)
                totals[index] = line_sums(field * shifted, totals[index])
                kern = rows_for[4 + index : 5 + index, :]
                back += load_frames(field_ref, line, -row_off, -col_off, line_rows, seg_count) * kern
            start = 8 + line * line_rows
            back_ref[start : start + line_rows, :] = follows * back
        kern_grad_ref[0:18, lanes] = jnp.concatenate(
            [jnp.sum(each, axis=0, keepdims=True) for each in totals], axis=0
        )
        total = cross = jnp.zeros((8, LANES), F32)
        for line in range(SIDE):
            first = line * line_rows
            rows = slice(first, first + line_rows)
            before = back_ref[first + 7 : first + 7 + line_rows, :]
            here = back_ref[first + 8 : first + 8 + line_rows, :]
            grad = whole_grad(rows) * (1.0 + gate_ref[rows, lanes]) + before - here
            centred = act_ref[rows, lanes] - average
            grad = grad * silu_slope(centred * scale + shift)
            slope_ref[rows, lanes] = grad
            low_ref[rows, lanes] = grad.astype(BF16)
            total = line_sums(grad, total)
            cross = line_sums(grad * (centred * inv_std), cross)
        totals_all.append(total)
        cross_all.append(cross)
    send_sums(sent_ref, jnp.concatenate(totals_all, axis=1), jnp.concatenate(cross_all, axis=1))
    for peer in range(sent_ref.shape[0]):
        sent_ref[peer, 2:4, :] = logit_ref[...]


def back_rows(got_ref, back_ref, small_ref, row, side, count):
    average, scale, shift, inv_std = norm_rows(
        side_sums(got_ref, side), small_row(small_ref, side, row), small_row(small_ref, side, row + 1), count
    )
    back = side_sums(back_ref, side) / count
    return average, inv_std, scale, back[0:1, :], back[1:2, :], shift


def conv_backward(
    seg_count, ints_ref, floats_ref, grad_ref, more_ref, act_ref, oth_ref, got_ref, back_ref, first_ref, got_one_ref,
    small_ref, w_ref, from_ref, pair_ref, slope_ref, low_ref, sent_ref, field_ref, cat_ref, acc_ref, w_all_ref,
):
    line_rows = SIDE * seg_count
    half = grad_ref.shape[1]
    step = WIDE * seg_count
    span = SIDE * step
    side = ints_ref[1]
    count = floats_ref[0]
    mask = line_mask(line_rows, seg_count, ints_ref[0])
    cat_ref[...] = jnp.zeros_like(cat_ref)
    field_ref[...] = jnp.zeros_like(field_ref)
    own = back_rows(got_ref, back_ref, small_ref, 2, side, count)
    oth = back_rows(got_ref, back_ref, small_ref, 2, 1 - side, count)
    average, inv_std, scale, mean, mix, _ = [jnp.concatenate(pieces, axis=1) for pieces in zip(own, oth)]
    for line in range(SIDE):
        rows = slice(line * line_rows, (line + 1) * line_rows)
        act = jnp.concatenate([act_ref[rows, :], oth_ref[rows, :].astype(F32)], axis=1)
        grad = jnp.concatenate([grad_ref[rows, :], more_ref[rows, :].astype(F32)], axis=1)
        normed = (act - average) * inv_std
        low = (scale * (grad - mask * (mean + normed * mix))).astype(BF16)
        store_taps(cat_ref, line, low, line_rows, seg_count)
        field_ref[line * step : line * step + line_rows, :] = low[:, :half]
    core = ints_ref[3]
    size = half // 2
    depth = 2 * half
    for tap in range(9):
        w_all_ref[tap, :, :half] = w_ref[tap // 3, (tap % 3) * depth : (tap % 3) * depth + half, :]
        for index, ref in ((core, from_ref), (1 - core, pair_ref)):
            w_all_ref[tap, :, pl.ds(pl.multiple_of(half + index * size, size), size)] = ref[tap]
    for row_off in range(3):
        rows = slice(row_off * step, row_off * step + span)
        part = sum(
            dot32(cat_ref[rows, tap * depth : (tap + 1) * depth], w_all_ref[8 - 3 * row_off - tap], ((1,), (1,)))
            for tap in range(3)
        )
        if row_off == 0:
            acc_ref[...] = part
        else:
            acc_ref[...] += part
    average, scale, shift, inv_std = norm_rows(
        side_sums(got_one_ref, side), small_row(small_ref, side, 0), small_row(small_ref, side, 1), count
    )
    total = cross = jnp.zeros((8, half), F32)
    for line in range(SIDE):
        rows = slice(line * line_rows, (line + 1) * line_rows)
        centred = first_ref[rows, :] - average
        grad = acc_ref[line * step : line * step + line_rows, :]
        grad = grad * silu_slope(centred * scale + shift)
        slope_ref[rows, :] = grad
        low_ref[rows, :] = grad.astype(BF16)
        total = line_sums(grad, total)
        cross = line_sums(grad * (centred * inv_std), cross)
    send_sums(sent_ref, total, cross)


def split_rows(rows_ref, index, keep_ref, send_ref):
    size = keep_ref.shape[0]
    keep_ref[...] = rows_ref[pl.ds(pl.multiple_of(index * size, 16), size), :]
    send_ref[...] = rows_ref[pl.ds(pl.multiple_of((1 - index) * size, 16), size), :]


def taps_gradient(seg_count, ints_ref, hid_ref, field_ref, kern_grad_ref, keep_ref, send_ref, taps_ref):
    line_rows = SIDE * seg_count
    taps_ref[...] = jnp.zeros_like(taps_ref)
    for line in range(SIDE):
        rows = slice(line * line_rows, (line + 1) * line_rows)
        store_taps(taps_ref, line, hid_ref[rows, :], line_rows, seg_count)
    step = WIDE * seg_count
    span = SIDE * step
    depth = taps_ref.shape[1] // 3
    lanes_of = [pl.ds(pl.multiple_of(index * LANES, LANES), LANES) for index in (ints_ref[3], 1 - ints_ref[3])]
    fields = jnp.concatenate([field_ref[:, lanes] for lanes in lanes_of], axis=1)
    for tap in range(9):
        start = (tap // 3) * step
        left = taps_ref[start : start + span, (tap % 3) * depth : (tap % 3 + 1) * depth]
        part = dot32(left, fields, ((0,), (0,))).astype(BF16)
        for place, ref in enumerate((keep_ref, send_ref)):
            ref[tap * depth : (tap + 1) * depth, :] = part[:, place * LANES : (place + 1) * LANES]
    rest = keep_ref.shape[0] - 9 * depth
    count = kern_grad_ref.shape[0]
    for lanes, ref in zip(lanes_of, (keep_ref, send_ref)):
        ref[9 * depth : 9 * depth + count, :] = kern_grad_ref[:, lanes].astype(BF16)
        ref[9 * depth + count :, :] = jnp.zeros((rest - count, LANES), BF16)


def sum_into(sum_ref, *refs):
    total = refs[0][...].astype(F32)
    for ref in refs[1:]:
        total += ref[...].astype(F32)
    sum_ref[...] = total.astype(sum_ref.dtype)


def store_blocks(ints_ref, rows_ref, refs):
    size = refs[0].shape[0]
    for bits, ref in enumerate(refs):
        start = pl.multiple_of((ints_ref[5] ^ bits) * size, 8)
        ref[...] = rows_ref[pl.ds(start, size), :].astype(ref.dtype)


def join_blocks(ints_ref, refs, out_ref):
    size = refs[0].shape[0]
    for bits, ref in enumerate(refs):
        start = pl.multiple_of((ints_ref[5] ^ bits) * size, 8)
        out_ref[pl.ds(start, size), :] = ref[...]


def sum_split(ints_ref, own_ref, got_ref, keep_ref, send_ref, sum_ref):
    sum_into(sum_ref, own_ref, got_ref)
    split_rows(sum_ref, ints_ref[4], keep_ref, send_ref)


def sum_blocks(ints_ref, own_ref, got_ref, *refs):
    sum_into(refs[-1], own_ref, got_ref)
    store_blocks(ints_ref, refs[-1], refs[:-1])


def sum_parts(*refs):
    sum_into(refs[-1], *refs[:-1])


def join_pair(ints_ref, own_ref, got_ref, out_ref):
    size = own_ref.shape[0]
    for index, ref in ((ints_ref[4], own_ref), (1 - ints_ref[4], got_ref)):
        out_ref[pl.ds(pl.multiple_of(index * size, 16), size), :] = ref[...]


def stage_one(places, ints_ref, pack_ref, pack_got_ref, reduce_ref, *refs):
    wide, refs = refs[:places], refs[places:]
    blocks, (keep_ref, send_ref, join_ref, sum_ref) = refs[:places], refs[places:]
    sum_into(sum_ref, pack_ref, pack_got_ref)
    store_blocks(ints_ref, sum_ref, blocks)
    split_rows(reduce_ref, ints_ref[4], keep_ref, send_ref)
    join_blocks(ints_ref, wide, join_ref)


def stage_two(places, ints_ref, keep_ref, got_ref, *refs):
    pack, (part_ref, *blocks, sum_ref) = refs[:places], refs[places:]
    sum_into(part_ref, *pack)
    sum_into(sum_ref, keep_ref, got_ref)
    store_blocks(ints_ref, sum_ref, blocks)


def stage_three(places, ints_ref, *refs):
    pack, reduce, (join_ref, columns_ref) = refs[:places], refs[places : 2 * places], refs[2 * places :]
    join_blocks(ints_ref, pack, join_ref)
    total = reduce[0][...].astype(F32)
    for ref in reduce[1:]:
        total += ref[...].astype(F32)
    total = total.astype(BF16)
    size = columns_ref.shape[2]
    for place, side in enumerate((ints_ref[1], 1 - ints_ref[1])):
        for core in range(2):
            start = (2 * place + core) * size
            for clip in range(columns_ref.shape[0] // 4):
                columns_ref[clip * 4 + 2 * side + core] = total[:, start : start + size]


def unpack_spatial(ints_ref, own_ref, got_ref, out_ref, near_ref, far_ref, rows_ref):
    join_pair(ints_ref, own_ref, got_ref, rows_ref)
    depth = out_ref.shape[1]
    half = depth // 2
    side = ints_ref[1]
    for tap in range(9):
        for place, index in enumerate((side, 1 - side)):
            start = tap * depth + place * half
            target = pl.ds(pl.multiple_of(index * half, half), half)
            out_ref[tap, target, :] = rows_ref[start : start + half, :].astype(F32)
    rest = rows_ref[9 * depth : 9 * depth + 32, :].astype(F32)
    near_ref[...] = rest[0:9, :]
    far_ref[...] = rest[9:18, :]


def unpack_wide(ints_ref, own_ref, got_ref, out_ref, classes_ref, rows_ref):
    join_pair(ints_ref, own_ref, got_ref, rows_ref)
    half = out_ref.shape[0] // 2
    for place, index in enumerate((ints_ref[1], 1 - ints_ref[1])):
        target = pl.ds(pl.multiple_of(index * half, half), half)
        out_ref[target, :] = rows_ref[place * half : (place + 1) * half, :].astype(F32)
    classes_ref[...] = rows_ref[2 * half :, :].astype(F32)


def last_norm(
    seg_count, ints_ref, floats_ref, grad_ref, more_ref, act_ref, oth_ref, got_ref, back_ref, small_ref, low_ref,
):
    line_rows = SIDE * seg_count
    side = ints_ref[1]
    mask = line_mask(line_rows, seg_count, ints_ref[0])
    half = grad_ref.shape[1]
    for place, (grads, acts) in enumerate(((grad_ref, act_ref), (more_ref, oth_ref))):
        index = side if place == 0 else 1 - side
        average, inv_std, scale, mean, mix, _ = back_rows(
            got_ref, back_ref, small_ref, 0, index, floats_ref[0]
        )
        for line in range(SIDE):
            rows = slice(line * line_rows, (line + 1) * line_rows)
            normed = (acts[rows, :].astype(F32) - average) * inv_std
            grad = scale * (grads[rows, :].astype(F32) - mask * (mean + normed * mix))
            low_ref[rows, place * half : (place + 1) * half] = grad.astype(BF16)


def pick_rows(ints_ref, w_ref, out_ref):
    size = out_ref.shape[1]
    out_ref[...] = w_ref[:, pl.ds(pl.multiple_of((1 - ints_ref[1]) * size, size), size), :]


def expand_gradient(
    ints_ref, own_ref, oth_ref, near_own_ref, near_oth_ref, low_ref, near_low_ref, classes_ref,
    keep_ref, send_ref, out_ref,
):
    half = own_ref.shape[1]
    for place, (first, second) in enumerate(((own_ref, near_own_ref), (oth_ref, near_oth_ref))):
        part = dot32(first[...], low_ref[...], ((0,), (0,))) + dot32(second[...], near_low_ref[...], ((0,), (0,)))
        out_ref[place * half : (place + 1) * half, :] = part.astype(BF16)
    rest = out_ref.shape[0] - 2 * half
    out_ref[2 * half :, :] = jnp.zeros((rest, out_ref.shape[1]), BF16)
    count = classes_ref.shape[0]
    out_ref[2 * half : 2 * half + count, :] = classes_ref[...].astype(BF16)
    split_rows(out_ref, ints_ref[4], keep_ref, send_ref)


def reduce_gradient(ints_ref, x_own_ref, low_ref, x_oth_ref, near_ref, out_ref):
    part = dot32(x_own_ref[...], low_ref[...], ((0,), (0,)))
    out_ref[...] = (part + dot32(x_oth_ref[...], near_ref[...], ((0,), (0,)))).astype(BF16)


def input_gradient(ints_ref, low_ref, w_ref, resid_ref, near_ref, out_ref):
    core = ints_ref[3]
    out_ref[core] = resid_ref[0] + dot32(low_ref[...], w_ref[...], ((1,), (1,)))
    out_ref[1 - core] = resid_ref[1] + dot32(near_ref[...], w_ref[...], ((1,), (1,)))


def per_device(
    clip_size,
    chan_size,
    frames_in,
    seg_counts,
    w_reduce,
    gain_one,
    shift_one,
    w_spatial,
    gain_two,
    shift_two,
    near_kern,
    far_kern,
    w_expand,
    gain_three,
    shift_three,
    w_classes,
    class_bias,
    out_grad,
    logit_grad,
):
    clip_count, seg_count, pixel_count, chan_local = frames_in.shape
    mid_local = w_reduce.shape[1]
    mid_width = w_spatial.shape[1]
    half = mid_width // 2
    row_count = seg_count * pixel_count
    class_count = w_classes.shape[1]
    chan_index = lax.axis_index("chan")
    clip_index = lax.axis_index("clip")
    side_index = chan_index // 2
    core_index = chan_index % 2
    everyone = clip_size * chan_size
    sds = jax.ShapeDtypeStruct

    def swap(array, bits):
        array = array.array if isinstance(array, Near) else array
        return lax.ppermute(array, "chan", [(i, i ^ bits) for i in range(chan_size)])

    def own_first(array, index, size, axis):
        own = lax.dynamic_slice_in_dim(array, index * size, size, axis)
        oth = lax.dynamic_slice_in_dim(array, (1 - index) * size, size, axis)
        return own, oth

    def pair(own, oth):
        flip = core_index == 1
        return jnp.where(flip, oth, own), jnp.where(flip, own, oth)

    def swap_clip(array, bits):
        array = array.array if isinstance(array, Near) else array
        return lax.ppermute(array, "clip", [(i, i ^ bits) for i in range(clip_size)])

    parity, place = clip_index % 2, clip_index // 2
    places = clip_size // 2
    groups = [list(range(first, clip_size, 2)) for first in range(2)]

    def sum_places(values):
        if places > 4:
            return lax.psum(values, "clip", axis_index_groups=groups)
        return sum([values] + [swap_clip(values, 2 * bits) for bits in range(1, places)])

    def share_all(sent):
        got = lax.all_to_all(sent, ("clip", "chan"), 0, 0)
        return got.reshape((clip_size, chan_size) + sent.shape[1:])

    def share_clip(sent):
        sent = sent.array
        return sum_places(sent + swap_clip(sent, 1))

    own_counts = lax.dynamic_slice_in_dim(seg_counts, clip_index * clip_count, clip_count)
    count_pair = jnp.concatenate(own_first(own_counts, core_index, 1, 0))
    valid_total = jnp.sum(seg_counts).astype(F32) * pixel_count
    count_scale = 1.0 / (count_pair.astype(F32) * pixel_count)
    ints = jnp.stack([count_pair[0], side_index, count_pair[1], core_index, parity, place])
    floats = jnp.concatenate([valid_total[None], count_scale])

    x_all = frames_in.transpose(0, 2, 1, 3).reshape(clip_count, row_count, chan_local)
    grad_all = out_grad.transpose(0, 2, 1, 3).reshape(clip_count, row_count, chan_local)
    x_own, x_oth = Pick(x_all, lambda ints: ints[3]), Pick(x_all, lambda ints: 1 - ints[3])
    grad_own, grad_oth = Pick(grad_all, lambda ints: ints[3]), Pick(grad_all, lambda ints: 1 - ints[3])
    half_f32, near_f32 = sds((row_count, half), F32), near((row_count, half), F32)
    half_low, near_low_half = sds((row_count, half), BF16), near((row_count, half), BF16)
    sums_shape = sds((everyone, 2, half), F32)
    pad_rows = 9 * WIDE * seg_count
    span = SIDE * WIDE * seg_count
    edge_rows = EDGE * EDGE * seg_count

    block_shape = sds((chan_local, mid_local), BF16)
    chan = chan_index.astype(jnp.int32)[None]
    sent_blocks = call(split_blocks, (block_shape,) * chan_size, ints=chan)(w_reduce)
    got_blocks = {bits: swap(sent_blocks[bits], bits) for bits in (2, 3, 1)}

    small_own = call(pack_small, sds((24, mid_local), F32))(
        gain_one[None], shift_one[None], gain_two[None], shift_two[None], near_kern, far_kern
    )
    small = call(join_small, sds((chan_size, 24, mid_local), F32), ints=ints)(
        small_own, *[swap(small_own, bits) for bits in (1, 2, 3)]
    )

    part_oth, w_rows = call(
        reduce_other,
        (near((row_count, mid_width), BF16), sds((chan_local, mid_width), BF16)),
        deps=(small,),
        ints=ints,
    )(sent_blocks[0], got_blocks[1], got_blocks[2], got_blocks[3], x_oth)
    near_one = swap(part_oth, 1)
    part_own, far_send = call(
        reduce_own,
        (near((row_count, half), F32), near((row_count, half), BF16)),
        ints=ints,
    )(near_one, w_rows, x_own)
    far_one = swap(far_send, 2)

    w_pair = jnp.concatenate(pair(w_spatial, swap(w_spatial, 1)), axis=2)
    w_fwd_own, w_fwd_oth = own_first(w_pair, side_index, half, 1)
    w_fwd = jnp.concatenate([w_fwd_own, w_fwd_oth], axis=1).reshape(3, 3 * mid_width, half)

    act_one, act_one_low, sent_one = call(
        functools.partial(first_sums, seg_count), (half_f32, half_low, sums_shape), deps=(w_fwd,), ints=ints,
    )(part_own, far_one)
    act_one_oth = swap(act_one_low, 2)
    got_one = share_all(sent_one)

    act_two, act_two_low, sent_two, hid_one = call(
        functools.partial(conv_forward, seg_count),
        (half_f32, half_low, sums_shape, sds((row_count, mid_width), BF16)),
        [pltpu.VMEM((pad_rows, 3 * mid_width), BF16), pltpu.VMEM((span, half), F32)],
        ints=ints,
        floats=floats,
    )(act_one, act_one_oth, got_one, small, w_fwd)
    act_two_oth = swap(act_two_low, 2)
    got_two = share_all(sent_two)

    def gate_call(act, other):
        return call(
            functools.partial(gate_forward, seg_count, other),
            (near_low_half,) if other else (near_low_half, near_f32, near_f32),
            [pltpu.VMEM((row_count + 8, LANES), F32), pltpu.VMEM((edge_rows, LANES), F32)],
            ints=ints,
            floats=floats,
        )(act, got_two, small)

    gated_own, hid_two, gate = gate_call(act_two, False)
    near_own = swap(gated_own, 1)
    gated_oth = gate_call(act_two_oth, True)[0]
    near_oth = swap(gated_oth, 1)

    bias_row = jnp.sum(logit_grad.astype(F32), axis=0)
    bias_row = jnp.pad(bias_row, (0, chan_local - class_count))[None]
    act_three, sent_three = call(
        functools.partial(expand, seg_count),
        (near((2, row_count, chan_local), F32), near((3, chan_local), F32)),
        ints=ints,
    )(gated_own, gated_oth, near_own, near_oth, w_expand, bias_row)
    got_three = share_clip(sent_three)

    to_side = call(pick_rows, sds((9, half, mid_local), BF16), deps=(sent_three,), ints=ints)(Free(w_spatial))
    from_side = swap(to_side, 2)
    from_pair = swap(from_side, 1)


    logit_pair = jnp.concatenate(own_first(logit_grad, core_index, 1, 0))
    grad_pooled = dot32(logit_pair, w_classes, ((1,), (1,))) * count_scale[:, None]
    output, grad_resid, pooled, sent_back = call(
        functools.partial(finish, seg_count),
        (
            sds((2, row_count, chan_local), BF16),
            near((2, row_count, chan_local), F32),
            near((2, chan_local), F32),
            near((2, chan_local), F32),
        ),
        ints=ints,
        floats=floats,
    )(
        got_three, gain_three[None], shift_three[None], grad_pooled,
        Pick(act_three, 0), x_own, grad_own, Pick(act_three, 1), x_oth, grad_oth,
    )
    got_back = share_clip(sent_back)
    pooled = pooled.array.astype(BF16)

    def back_call(clip):
        outs = [near((row_count, chan_local), BF16)]
        if clip == 0:
            outs += [near((row_count, half), F32)] * 2
        else:
            outs += [near((row_count, mid_width), BF16)]
        return call(
            functools.partial(expand_backward, seg_count, clip), tuple(outs), deps=(from_side,), ints=ints, floats=floats,
        )(got_three, got_back, gain_three[None], Pick(grad_resid, clip), Pick(act_three, clip), w_expand)

    low_three_oth, back_oth = back_call(1)
    near_back = swap(back_oth, 1)
    low_three_own, back_own, back_far = back_call(0)

    unit = 16 * clip_size
    def halves(rows, width):
        return (sds((rows // 2, width), BF16),) * 2

    def to_places(blocks):
        if places > 4:
            order = place ^ jnp.arange(places)
            sent = jnp.stack(blocks)[order]
            return list(lax.all_to_all(sent, "clip", 0, 0, axis_index_groups=groups)[order])
        return [blocks[0]] + [swap_clip(blocks[bits], 2 * bits) for bits in range(1, places)]

    def blocks_of(rows, width):
        return (sds((rows // places, width), BF16),) * places

    grad_classes = dot32(logit_pair, pooled, ((0,), (0,)))
    wide_rows = -(-(mid_width + class_count) // unit) * unit
    wide_keep, wide_send = call(
        expand_gradient, halves(wide_rows, chan_local), [pltpu.VMEM((wide_rows, chan_local), BF16)], ints=ints,
    )(gated_own, gated_oth, near_own, near_oth, low_three_own, low_three_oth, grad_classes)

    far_back = swap(call(add_low, near_low_half, deps=())(near_back, back_far), 2)
    wide_blocks = call(
        sum_blocks,
        blocks_of(wide_rows // 2, chan_local),
        [pltpu.VMEM((wide_rows // 2, chan_local), BF16)],
        ints=ints,
    )(wide_keep, swap_clip(wide_send, 1))
    wide_got = to_places(wide_blocks)

    logits_part = jnp.concatenate(own_first(dot32(pooled, w_classes), core_index, 1, 0))
    logits_wide = jnp.pad(logits_part, ((0, 0), (0, half - class_count)))
    slope_two, slope_two_low, sent_back_two, kern_grad = call(
        functools.partial(gate_backward, seg_count),
        (half_f32, half_low, sds((everyone, 4, half), F32), sds((32, half), F32)),
        [
            pltpu.VMEM((edge_rows, LANES), F32),
            pltpu.VMEM((edge_rows, LANES), F32),
            pltpu.VMEM((row_count + 8, LANES), F32),
        ],
        deps=(wide_send,),
        ints=ints,
        floats=floats,
    )(back_own, near_back, far_back, hid_two, gate, act_two, got_two, small, logits_wide)
    slope_two_oth = swap(slope_two_low, 2)
    got_back_two = share_all(sent_back_two)
    slope_one, slope_one_low, sent_back_one, field_two = call(
        functools.partial(conv_backward, seg_count),
        (half_f32, half_low, sums_shape, sds((span, half), BF16)),
        [
            pltpu.VMEM((pad_rows, 3 * mid_width), BF16),
            pltpu.VMEM((span, half), F32),
            pltpu.VMEM((9, half, mid_width), BF16),
        ],
        deps=(wide_blocks[0],),
        ints=ints,
        floats=floats,
    )(
        slope_two, slope_two_oth, act_two, act_two_oth, got_two, got_back_two, act_one, got_one, small, w_fwd,
        from_side, from_pair,
    )
    slope_one_oth = swap(slope_one_low, 2)
    got_back_one = share_all(sent_back_one)

    pack_rows = -(-(9 * mid_width + 32) // unit) * unit
    pack_own, pack_send = call(
        functools.partial(taps_gradient, seg_count),
        (sds((pack_rows, mid_local), BF16),) * 2,
        [pltpu.VMEM((pad_rows, 3 * mid_width), BF16)],
        ints=ints,
    )(hid_one, field_two, kern_grad)
    pack_keep, pack_pair = call(
        sum_split, halves(pack_rows, mid_local), [pltpu.VMEM((pack_rows, mid_local), BF16)], ints=ints,
    )(pack_own, swap(pack_send, 1))
    wide_part = call(sum_parts, sds((wide_rows // clip_size, chan_local), BF16))(*wide_got)

    low_one = call(
        functools.partial(last_norm, seg_count),
        sds((row_count, mid_width), BF16),
        deps=(pack_pair, wide_part),
        ints=ints,
        floats=floats,
    )(slope_one, slope_one_oth, act_one, act_one_oth, got_one, got_back_one, small)
    near_low = swap(low_one, 1)
    reduce_all = call(reduce_gradient, sds((chan_local, mid_width), BF16), ints=ints)(
        x_own, low_one, x_oth, near_low
    )

    share = chan_local // clip_size
    stage = call(
        functools.partial(stage_one, places),
        blocks_of(pack_rows // 2, mid_local) + halves(chan_local, mid_width) + (sds((wide_rows // 2, chan_local), BF16),),
        [pltpu.VMEM((pack_rows // 2, mid_local), BF16)],
        ints=ints,
    )(pack_keep, swap_clip(pack_pair, 1), reduce_all, *to_places([wide_part] * places))
    pack_blocks, (reduce_keep, reduce_send, wide_join) = stage[:places], stage[places:]
    grad_frames = call(
        input_gradient, sds((2, row_count, chan_local), F32), deps=(pack_blocks[0],), ints=ints,
    )(low_one, w_rows, grad_resid, near_low)
    wide_other = swap_clip(wide_join, 1)
    pack_part, *reduce_blocks = call(
        functools.partial(stage_two, places),
        (sds((pack_rows // clip_size, mid_local), BF16),) + blocks_of(chan_local // 2, mid_width),
        [pltpu.VMEM((chan_local // 2, mid_width), F32)],
        deps=(grad_frames, wide_other),
        ints=ints,
    )(reduce_keep, swap_clip(reduce_send, 1), *to_places(pack_blocks))
    grad_w_expand, classes_got = call(
        unpack_wide,
        (sds((mid_width, chan_local), F32), sds((wide_rows - mid_width, chan_local), F32)),
        [pltpu.VMEM((wide_rows, chan_local), BF16)],
        deps=(pack_part,),
        ints=ints,
    )(wide_join, wide_other)
    grad_w_classes = classes_got[:class_count].T
    pack_join, columns = call(
        functools.partial(stage_three, places),
        (sds((pack_rows // 2, mid_local), BF16), sds((everyone, share, mid_local), BF16)),
        deps=(grad_w_expand,),
        ints=ints,
    )(*to_places([pack_part] * places), *to_places(reduce_blocks))
    reduce_got = lax.all_to_all(columns, ("clip", "chan"), 0, 0)
    reduce_got = reduce_got.reshape(places, 2, chan_size, share, mid_local).transpose(2, 1, 0, 3, 4)
    grad_w_reduce = reduce_got.reshape(chan_size * chan_local, mid_local).astype(F32)
    grad_spatial, grad_near, grad_far = call(
        unpack_spatial,
        (sds((9, mid_width, mid_local), F32),) + (sds((9, mid_local), F32),) * 2,
        [pltpu.VMEM((pack_rows, mid_local), BF16)],
        ints=ints,
    )(pack_join, swap_clip(pack_join, 1))

    mine = lax.dynamic_index_in_dim(got_back_two, clip_index, 0, keepdims=False)
    logits = jnp.sum(mine, axis=0)[2:, :class_count] + class_bias

    def own_sums(got):
        sums = jnp.sum(got.reshape((clip_size, 2, 2) + got.shape[2:]), axis=(0, 2))
        sums = lax.dynamic_index_in_dim(sums, side_index, 0, keepdims=False)
        return lax.dynamic_slice_in_dim(sums[:2], core_index * mid_local, mid_local, 1)

    grads_one = own_sums(got_back_one)
    grads_two = own_sums(got_back_two)
    grads_three = got_back
    grad_bias = got_three[2, :class_count]

    def whole(array):
        return array.reshape(2, pixel_count, seg_count, chan_local).transpose(0, 2, 1, 3)

    return (
        whole(output),
        logits,
        whole(grad_frames),
        grad_w_reduce,
        grads_one[1],
        grads_one[0],
        grad_spatial,
        grads_two[1],
        grads_two[0],
        grad_near,
        grad_far,
        grad_w_expand,
        grads_three[1],
        grads_three[0],
        grad_w_classes,
        grad_bias,
    )


def solution(mesh):
    in_specs = (
        P("clip", None, None, "chan"),
        P(),
        P(None, "chan"),
        P("chan"),
        P("chan"),
        P(None, None, "chan"),
        P("chan"),
        P("chan"),
        P(None, "chan"),
        P(None, "chan"),
        P(None, "chan"),
        P("chan"),
        P("chan"),
        P("chan", None),
        P(),
        P("clip", None, None, "chan"),
        P("clip", None),
    )
    out_specs = (
        P("clip", None, None, "chan"),
        P("clip", None),
        P("clip", None, None, "chan"),
        P(None, "chan"),
        P("chan"),
        P("chan"),
        P(None, None, "chan"),
        P("chan"),
        P("chan"),
        P(None, "chan"),
        P(None, "chan"),
        P(None, "chan"),
        P("chan"),
        P("chan"),
        P("chan", None),
        P(),
    )
    body = functools.partial(per_device, mesh.shape["clip"], mesh.shape["chan"])
    return jax.shard_map(
        body, mesh=mesh, in_specs=in_specs, out_specs=out_specs, check_vma=False
    )
```

time: 752 us -> 299 us (0.40)
  waiting for transfers between devices: 311 us -> 86 us
  local copies, waits for them, and re-layouts: 171 us -> 27.9 us
  blocking collectives: 143 us -> 11.9 us
  Pallas kernels: 0 us -> 90.1 us
  starting transfers between devices: 0.91 us -> 72.3 us
  matrix products: 54.7 us -> 1.86 us
  other arithmetic: 50.6 us -> 5.33 us
  between operations: 15.8 us -> 1.78 us
    psum x1 -> x0, waiting for transfers between devices: 153 us -> none  [per_device(): lax.psum((grad_reduce, grad_spatial, grad_near, grad_far, grad_expand, gr...]
    psum x7 -> x0, blocking collectives: 143 us -> none  [the longest x3 72.3 us: norm_back(): lax.psum((jnp.sum(grad_norm * normed, axis=0), jnp.sum(grad_norm, axis=0)...]
    pallas_call x0 -> x30, Pallas kernels: none -> 90.1 us  [run(): pl.pallas_call(kernel, out_shape=outs, in_specs=[SMEM] * len(scalars) + [...]
    ppermute x0 -> x49, waiting for transfers between devices: none -> 81.3 us  [the longest x28 59.3 us: swap_clip(): lax.ppermute(array, 'clip', [(i, i ^ bits) for i in range(clip_size)])]
    all_gather x3 -> x0, waiting for transfers between devices: 73.1 us -> none  [the longest x1 48.3 us: per_device(): x_whole = lax.all_gather(x_rows, 'chan', axis=1, tiled=True)]
    unnamed x134 -> x114, local copies, waits for them, and re-layouts: 78.8 us -> 20.3 us
    reduce_scatter x1 -> x0, waiting for transfers between devices: 58.4 us -> none  [per_device(): lax.psum_scatter(jnp.dot(low_one, w_reduce.T, preferred_element_type=jnp....]
    ppermute x0 -> x49, starting transfers between devices: none -> 54.4 us  [the longest x28 40.6 us: swap_clip(): lax.ppermute(array, 'clip', [(i, i ^ bits) for i in range(clip_size)])]
  transfers between devices with their start and end apart: 7 -> 53, of which waited for: 6 -> 23; matrix products, arithmetic and copies ran while one was open for 8% -> 5% of each run, Pallas kernels for 0% -> 18%
where the time goes in v1:
time: 299 us; the launch traced here: 297 us
  Pallas kernels  90.1 us (30%)
  waiting for transfers between devices  86 us (29%)
  starting transfers between devices  72.3 us (24%)
  local copies, waits for them, and re-layouts  27.9 us (9%)
  blocking collectives  11.9 us (4%)
  other arithmetic  5.33 us (2%)
    pallas_call x30, Pallas kernels, run(): pl.pallas_call(kernel, out_shape=outs, in_specs=[SMEM] * len(scalars) + [...  90.1 us
    ppermute x28, waiting for transfers between devices, swap_clip(): lax.ppermute(array, 'clip', [(i, i ^ bits) for i in range(clip_size)])  59.3 us
    ppermute x28, starting transfers between devices, swap_clip(): lax.ppermute(array, 'clip', [(i, i ^ bits) for i in range(clip_size)])  40.6 us
    ppermute x21, waiting for transfers between devices, swap(): lax.ppermute(array, 'chan', [(i, i ^ bits) for i in range(chan_size)])  22 us
    unnamed x114, local copies, waits for them, and re-layouts  20.3 us
    ppermute x21, starting transfers between devices, swap(): lax.ppermute(array, 'chan', [(i, i ^ bits) for i in range(chan_size)])  13.8 us
    all_to_all x3, starting transfers between devices, share_all(): got = lax.all_to_all(sent, ('clip', 'chan'), 0, 0)  13.6 us
    all_to_all x1, blocking collectives, share_all(): got = lax.all_to_all(sent, ('clip', 'chan'), 0, 0)  11.9 us
  transfers between devices with their start and end apart: 53, of which 23 were waited for; matrix products, arithmetic and copies ran while one was open for 5% of the time, Pallas kernels for 18%

profile of v1, /device:TPU:0, one launch (start us, length us, event | category | flops | bytes accessed | tf_op | source)
XLA Modules:
  0.0 297.2 jit_solution(8369294450337856836)
XLA Ops:
  3.1 2.9 collective-permute-start.1
  19.9 3.1 %shard_map.291 = (bf16[784,512]{1,0:T(8,128)(2,1)S(1)}, bf16[512,512]{1,0:T(8,128)(2,1)}) custom-call(s32[6]{0:T(128)S(1)} %stack.19.refs_0_, bf16[512,128]{1,0:T(8,128)(2,1)} %get-tuple-element.82.refs_1_, bf16[512,128]{1,0:T(8,128)(2,1)} %copy-done.37, bf16[512,128]{1,0:T(8,128)(2,1)} %copy-done.38, bf16[512,128]{1,0:T(8,128)(2,1)} %copy-done.39, ...), custom_call_target="tpu_custom_call" | custom-call | tf_op jit(solution)/shard_map/pallas_call | solution.py:112
  26.4 3.0 %shard_map.292 = (f32[784,256]{1,0:T(8,128)S(1)}, bf16[784,256]{1,0:T(8,128)(2,1)S(1)}) custom-call(s32[6]{0:T(128)S(1)} %stack.19.refs_0_, bf16[784,512]{1,0:T(8,128)(2,1)} %collective-permute-done.6.refs_1_, bf16[512,512]{1,0:T(8,128)(2,1)} %get-tuple-element.87.refs_2_, bf16[2,784,512]{2,1,0:T(8,128)(2,1)} %bitcast.57), custom_call_target="tpu_custom_call" | custom-call | tf_op jit(solution)/shard_map/pallas_call | solution.py:112
  31.1 10.0 %collective-permute-done.7.refs_2_ = bf16[784,256]{1,0:T(8,128)(2,1)S(1)} collective-permute-done((bf16[784,256]{1,0:T(8,128)(2,1)S(1)}, bf16[784,256]{1,0:T(8,128)(2,1)S(1)}, u32[]{:S(2)}, u32[]{:S(2)}) %collective-permute-start.7) | collective-permute-done | bytes 401440 | tf_op jit(solution)/shard_map/ppermute | solution.py:755
  44.7 5.7 %all-to-all-start = ((f32[32,2,256]{2,1,0:T(2,128)}), f32[32,2,256]{2,1,0:T(2,128)S(1)}, u32[]{:S(2)}, u32[]{:S(2)}) async-start(f32[32,2,256]{2,1,0:T(2,128)} %get-tuple-element.92), calls=%async_computation | async-start | bytes 131072 | tf_op jit(solution)/shard_map/all_to_all | solution.py:780
  53.1 4.7 %all-to-all-done = f32[32,2,256]{2,1,0:T(2,128)S(1)} async-done(((f32[32,2,256]{2,1,0:T(2,128)}), f32[32,2,256]{2,1,0:T(2,128)S(1)}, u32[]{:S(2)}, u32[]{:S(2)}) %all-to-all-start) | async-done | bytes 65568 | tf_op jit(solution)/shard_map/all_to_all | solution.py:780
  58.6 5.6 %shard_map.294 = (f32[784,256]{1,0:T(8,128)}, bf16[784,256]{1,0:T(8,128)(2,1)}, f32[32,2,256]{2,1,0:T(2,128)}, bf16[784,512]{1,0:T(8,128)(2,1)}) custom-call(s32[6]{0:T(128)S(1)} %stack.19.refs_0_, f32[3]{0:T(128)S(1)} %pad_maximum_fusion.2.refs_1_, f32[784,256]{1,0:T(8,128)} %get-tuple-element.90.refs_2_.refs_8_.refs_4_, bf16[784,256]{1,0:T(8,128)(2,1)} %copy-done.16, ...), custom_call_target="tpu_custom_call" | custom-call | tf_op jit(solution)/shard_map/pallas_call | solution.py:112
  64.6 11.9 %all_to_all.25 = f32[32,2,256]{2,1,0:T(2,128)} all-to-all(f32[32,2,256]{2,1,0:T(2,128)} %get-tuple-element.94), channel_id=1, replica_groups=mesh['clip'=8,'chan'=4] {'clip','chan'}, dimensions={0} | all-to-all | bytes 131072 | tf_op jit(solution)/shard_map/all_to_all | solution.py:780
  96.0 3.3 %collective-permute-done.16 = f32[3,512]{1,0:T(4,128)S(1)} collective-permute-done((f32[3,512]{1,0:T(4,128)S(1)}, f32[3,512]{1,0:T(4,128)S(1)}, u32[]{:S(2)}, u32[]{:S(2)}) %collective-permute-start.16) | collective-permute-done | bytes 6176 | tf_op jit(solution)/shard_map/ppermute | solution.py:768
  99.9 5.1 %shard_map.298 = (bf16[2,784,512]{2,1,0:T(8,128)(2,1)}, f32[2,784,512]{2,1,0:T(8,128)S(1)}, f32[2,512]{1,0:T(2,128)S(1)}, f32[2,512]{1,0:T(2,128)S(1)}) custom-call(s32[6]{0:T(128)S(1)} %stack.19.refs_0_, f32[3]{0:T(128)S(1)} %pad_maximum_fusion.2.refs_1_, f32[3,512]{1,0:T(4,128)} %add_add_fusion.refs_2_, f32[1,512]{1,0:T(1,128)} %bitcast.78, ...), custom_call_target="tpu_custom_call" | custom-call | tf_op jit(solution)/shard_map/pallas_call | solution.py:112
  113.3 2.8 collective-permute-done.20
  125.9 3.4 %shard_map.303 = (bf16[384,512]{1,0:T(8,128)(2,1)}, bf16[384,512]{1,0:T(8,128)(2,1)}) custom-call(s32[6]{0:T(128)S(1)} %stack.19.refs_0_, bf16[784,256]{1,0:T(8,128)(2,1)S(1)} %get-tuple-element.95.refs_1_, bf16[784,256]{1,0:T(8,128)(2,1)S(1)} %shard_map.296.refs_2_, bf16[784,256]{1,0:T(8,128)(2,1)} %copy-done.17, bf16[784,256]{1,0:T(8,128)(2,1)} %copy-done.18, ...), custom_call_target="tpu_custom_call" | custom-call | tf_op jit(solution)/shard_map/pallas_call | solution.py:112
  129.3 5.0 %collective-permute-done.23.refs_4_ = bf16[784,256]{1,0:T(8,128)(2,1)S(1)} collective-permute-done((bf16[784,256]{1,0:T(8,128)(2,1)S(1)}, bf16[784,256]{1,0:T(8,128)(2,1)S(1)}, u32[]{:S(2)}, u32[]{:S(2)}) %collective-permute-start.23) | collective-permute-done | bytes 401440 | tf_op jit(solution)/shard_map/ppermute | solution.py:755
  135.1 5.2 %shard_map.304 = (f32[784,256]{1,0:T(8,128)}, bf16[784,256]{1,0:T(8,128)(2,1)}, f32[32,4,256]{2,1,0:T(4,128)}, f32[32,256]{1,0:T(8,128)}) custom-call(s32[6]{0:T(128)S(1)} %stack.19.refs_0_, f32[3]{0:T(128)S(1)} %pad_maximum_fusion.2.refs_1_, f32[784,256]{1,0:T(8,128)S(1)} %get-tuple-element.102.refs_2_, bf16[784,512]{1,0:T(8,128)(2,1)} %copy-done.14, ...), custom_call_target="tpu_custom_call" | custom-call | tf_op jit(solution)/shard_map/pallas_call | solution.py:112
  142.2 3.8 %all-to-all-start.2 = ((f32[32,4,256]{2,1,0:T(4,128)}), f32[32,4,256]{2,1,0:T(4,128)S(1)}, u32[]{:S(2)}, u32[]{:S(2)}) async-start(f32[32,4,256]{2,1,0:T(4,128)} %get-tuple-element.111), calls=%async_computation.2 | async-start | bytes 262144 | tf_op jit(solution)/shard_map/all_to_all | solution.py:780
  146.0 6.9 %collective-permute-done.26.refs_2_ = bf16[384,512]{1,0:T(8,128)(2,1)} collective-permute-done((bf16[384,512]{1,0:T(8,128)(2,1)}, bf16[384,512]{1,0:T(8,128)(2,1)}, u32[]{:S(2)}, u32[]{:S(2)}) %collective-permute-start.26) | collective-permute-done | bytes 393248 | tf_op jit(solution)/shard_map/ppermute | solution.py:768
  156.7 7.1 %shard_map.306 = (f32[784,256]{1,0:T(8,128)}, bf16[784,256]{1,0:T(8,128)(2,1)}, f32[32,2,256]{2,1,0:T(2,128)}, bf16[896,256]{1,0:T(8,128)(2,1)}) custom-call(s32[6]{0:T(128)S(1)} %stack.19.refs_0_, f32[3]{0:T(128)S(1)} %pad_maximum_fusion.2.refs_1_, f32[784,256]{1,0:T(8,128)} %get-tuple-element.112.refs_2_, ...), custom_call_target="tpu_custom_call" | custom-call | tf_op jit(solution)/shard_map/pallas_call | solution.py:112
  163.8 5.4 %shard_map.307 = (bf16[4736,128]{1,0:T(8,128)(2,1)}, bf16[4736,128]{1,0:T(8,128)(2,1)}) custom-call(s32[6]{0:T(128)S(1)} %stack.19.refs_0_, bf16[784,512]{1,0:T(8,128)(2,1)} %get-tuple-element.119.refs_1_, bf16[896,256]{1,0:T(8,128)(2,1)} %get-tuple-element.120.refs_2_, f32[32,256]{1,0:T(8,128)} %get-tuple-element.121.refs_3_), custom_call_target="tpu_custom_call" | custom-call | tf_op jit(solution)/shard_map/pallas_call | solution.py:112
  169.9 4.0 %all-to-all-start.3 = ((f32[32,2,256]{2,1,0:T(2,128)}), f32[32,2,256]{2,1,0:T(2,128)S(1)}, u32[]{:S(2)}, u32[]{:S(2)}) async-start(f32[32,2,256]{2,1,0:T(2,128)} %get-tuple-element.118), calls=%async_computation.3 | async-start | bytes 131072 | tf_op jit(solution)/shard_map/all_to_all | solution.py:780
  178.3 2.9 collective-permute-done.29.refs_1_
  181.3 5.2 %collective-permute-done.30.refs_2_ = bf16[96,512]{1,0:T(8,128)(2,1)S(1)} collective-permute-done((bf16[96,512]{1,0:T(8,128)(2,1)}, bf16[96,512]{1,0:T(8,128)(2,1)S(1)}, u32[]{:S(2)}, u32[]{:S(2)}) %collective-permute-start.30) | collective-permute-done | bytes 98336 | tf_op jit(solution)/shard_map/ppermute | solution.py:768
  189.5 3.4 %shard_map.308 = (bf16[2368,128]{1,0:T(8,128)(2,1)}, bf16[2368,128]{1,0:T(8,128)(2,1)}) custom-call(s32[6]{0:T(128)S(1)} %stack.19.refs_0_, bf16[4736,128]{1,0:T(8,128)(2,1)} %get-tuple-element.122.refs_1_, bf16[4736,128]{1,0:T(8,128)(2,1)} %collective-permute-done.28.refs_2_), custom_call_target="tpu_custom_call" | custom-call | tf_op jit(solution)/shard_map/pallas_call | solution.py:112
  194.6 3.0 %shard_map.310.refs_2_.refs_1_ = bf16[784,512]{1,0:T(8,128)(2,1)} custom-call(s32[6]{0:T(128)S(1)} %stack.19.refs_0_, f32[3]{0:T(128)S(1)} %pad_maximum_fusion.2.refs_1_, f32[784,256]{1,0:T(8,128)} %get-tuple-element.116.refs_2_, bf16[784,256]{1,0:T(8,128)(2,1)} %collective-permute-done.27.refs_3_, f32[784,256]{1,0:T(8,128)} %get-tuple-element.90.refs_2_.refs_8_.refs_4_, ...), custom_call_target="tpu_custom_call" | custom-call | tf_op jit(solution)/shard_map/pallas_call | solution.py:112
  204.4 4.9 %shard_map.311.refs_3_ = bf16[512,512]{1,0:T(8,128)(2,1)} custom-call(s32[6]{0:T(128)S(1)} %stack.19.refs_0_, bf16[2,784,512]{2,1,0:T(8,128)(2,1)} %bitcast.60, bf16[784,512]{1,0:T(8,128)(2,1)} %shard_map.310.refs_2_.refs_1_, bf16[2,784,512]{2,1,0:T(8,128)(2,1)} %bitcast.61, bf16[784,512]{1,0:T(8,128)(2,1)} %copy-done.15), custom_call_target="tpu_custom_call" | custom-call | tf_op jit(solution)/shard_map/pallas_call | solution.py:112
  211.0 2.7 collective-permute-done.33.refs_2_
  214.5 2.8 shard_map.312
  224.7 4.3 %shard_map.313.refs_7_ = f32[2,784,512]{2,1,0:T(8,128)} custom-call(s32[6]{0:T(128)S(1)} %stack.19.refs_0_, bf16[784,512]{1,0:T(8,128)(2,1)} %shard_map.310.refs_2_.refs_1_, bf16[512,512]{1,0:T(8,128)(2,1)} %get-tuple-element.87.refs_2_, f32[2,784,512]{2,1,0:T(8,128)S(1)} %get-tuple-element.101.refs_5_.refs_3_, bf16[784,512]{1,0:T(8,128)(2,1)} %copy-done.15, ...), custom_call_target="tpu_custom_call" | custom-call | tf_op jit(solution)/shard_map/pallas_call | solution.py:112
  228.9 5.5 %collective-permute-done.39.refs_5_ = bf16[592,128]{1,0:T(8,128)(2,1)S(1)} collective-permute-done((bf16[592,128]{1,0:T(8,128)(2,1)}, bf16[592,128]{1,0:T(8,128)(2,1)S(1)}, u32[]{:S(2)}, u32[]{:S(2)}) %collective-permute-start.39) | collective-permute-done | bytes 151584 | tf_op jit(solution)/shard_map/ppermute | solution.py:768
  246.7 6.1 %collective-permute-done.45.refs_6_ = bf16[64,512]{1,0:T(8,128)(2,1)S(1)} collective-permute-done((bf16[64,512]{1,0:T(8,128)(2,1)}, bf16[64,512]{1,0:T(8,128)(2,1)S(1)}, u32[]{:S(2)}, u32[]{:S(2)}) %collective-permute-start.45) | collective-permute-done | bytes 65568 | tf_op jit(solution)/shard_map/ppermute | solution.py:768
  266.0 4.3 %all-to-all-start.4 = ((bf16[32,64,128]{2,1,0:T(8,128)(2,1)}), bf16[32,64,128]{2,1,0:T(8,128)(2,1)S(1)}, u32[]{:S(2)}, u32[]{:S(2)}) async-start(bf16[32,64,128]{2,1,0:T(8,128)(2,1)} %get-tuple-element.142), calls=%async_computation.4 | async-start | bytes 1048576 | tf_op jit(solution)/shard_map/all_to_all | solution.py:1032
  274.8 17.4 %collective-permute-done.48.refs_2_ = bf16[2368,128]{1,0:T(8,128)(2,1)S(1)} collective-permute-done((bf16[2368,128]{1,0:T(8,128)(2,1)}, bf16[2368,128]{1,0:T(8,128)(2,1)S(1)}, u32[]{:S(2)}, u32[]{:S(2)}) %collective-permute-start.48) | collective-permute-done | bytes 606240 | tf_op jit(solution)/shard_map/ppermute | solution.py:768
  293.0 2.9 shard_map.317
  (251 shorter events, 130.8 us)
Async XLA Ops:
  0.7 29.7 %collective-permute-start.8 = (bf16[9,512,128]{2,1,0:T(8,128)(2,1)}, bf16[9,512,128]{2,1,0:T(8,128)(2,1)S(1)}, u32[]{:S(2)}, u32[]{:S(2)}) collective-permute-start(bf16[9,512,128]{2,1,0:T(8,128)(2,1)} %refs_1_.3), channel_id=1, source_target_pairs={{0,1},{1,0},{2,3},{3,2},{4,5},{5,4},{6,7},{7,6},{8,9},{9,8},{10,11... | collective-permute-start | bytes 3538952 | tf_op jit(solution)/shard_map/ppermute | solution.py:755
  3.0 15.3 %collective-permute-start = (bf16[512,128]{1,0:T(8,128)(2,1)}, bf16[512,128]{1,0:T(8,128)(2,1)S(1)}, u32[]{:S(2)}, u32[]{:S(2)}) collective-permute-start(bf16[512,128]{1,0:T(8,128)(2,1)} %get-tuple-element.83), channel_id=1, source_target_pairs={{0,1},{1,0},{2,3},{3,2},{4,5},{5,4},{6,7},{7,6},{8,9},{9,8},{10,11... | collective-permute-start | bytes 393224 | tf_op jit(solution)/shard_map/ppermute | solution.py:755
  3.1 15.2 %collective-permute-start.1 = (bf16[512,128]{1,0:T(8,128)(2,1)}, bf16[512,128]{1,0:T(8,128)(2,1)S(1)}, u32[]{:S(2)}, u32[]{:S(2)}) collective-permute-start(bf16[512,128]{1,0:T(8,128)(2,1)} %get-tuple-element.84), channel_id=1, source_target_pairs={{0,2},{1,3},{2,0},{3,1},{4,6},{5,7},{6,4},{7,5},{8,10},{9,11},{10,... | collective-permute-start | bytes 393224 | tf_op jit(solution)/shard_map/ppermute | solution.py:755
  6.0 12.3 %collective-permute-start.2 = (bf16[512,128]{1,0:T(8,128)(2,1)}, bf16[512,128]{1,0:T(8,128)(2,1)S(1)}, u32[]{:S(2)}, u32[]{:S(2)}) collective-permute-start(bf16[512,128]{1,0:T(8,128)(2,1)} %get-tuple-element.85), channel_id=1, source_target_pairs={{0,3},{1,2},{2,1},{3,0},{4,7},{5,6},{6,5},{7,4},{8,11},{9,10},{10,... | collective-permute-start | bytes 393224 | tf_op jit(solution)/shard_map/ppermute | solution.py:755
  29.4 11.6 %collective-permute-start.7 = (bf16[784,256]{1,0:T(8,128)(2,1)S(1)}, bf16[784,256]{1,0:T(8,128)(2,1)S(1)}, u32[]{:S(2)}, u32[]{:S(2)}) collective-permute-start(bf16[784,256]{1,0:T(8,128)(2,1)S(1)} %get-tuple-element.89), channel_id=1, source_target_pairs={{0,2},{1,3},{2,0},{3,1},{4,6},{5,7},{6,4},{7,5},{8,10},{9,11},{10,... | collective-permute-start | bytes 1204232 | tf_op jit(solution)/shard_map/ppermute | solution.py:755
  44.0 13.8 %collective-permute-start.9 = (bf16[784,256]{1,0:T(8,128)(2,1)}, bf16[784,256]{1,0:T(8,128)(2,1)S(1)}, u32[]{:S(2)}, u32[]{:S(2)}) collective-permute-start(bf16[784,256]{1,0:T(8,128)(2,1)} %get-tuple-element.91), channel_id=1, source_target_pairs={{0,2},{1,3},{2,0},{3,1},{4,6},{5,7},{6,4},{7,5},{8,10},{9,11},{10,... | collective-permute-start | bytes 1204232 | tf_op jit(solution)/shard_map/ppermute | solution.py:755
  44.7 13.2 %all-to-all-start = ((f32[32,2,256]{2,1,0:T(2,128)}), f32[32,2,256]{2,1,0:T(2,128)S(1)}, u32[]{:S(2)}, u32[]{:S(2)}) async-start(f32[32,2,256]{2,1,0:T(2,128)} %get-tuple-element.92), calls=%async_computation | async-start | bytes 131072 | tf_op jit(solution)/shard_map/all_to_all | solution.py:780
  64.2 14.9 %collective-permute-start.10 = (bf16[784,256]{1,0:T(8,128)(2,1)}, bf16[784,256]{1,0:T(8,128)(2,1)S(1)}, u32[]{:S(2)}, u32[]{:S(2)}) collective-permute-start(bf16[784,256]{1,0:T(8,128)(2,1)} %get-tuple-element.96), channel_id=1, source_target_pairs={{0,2},{1,3},{2,0},{3,1},{4,6},{5,7},{6,4},{7,5},{8,10},{9,11},{10,... | collective-permute-start | bytes 1204232 | tf_op jit(solution)/shard_map/ppermute | solution.py:755
  90.0 26.6 %collective-permute-start.21 = (bf16[9,256,128]{2,1,0:T(8,128)(2,1)}, bf16[9,256,128]{2,1,0:T(8,128)(2,1)}, u32[]{:S(2)}, u32[]{:S(2)}) collective-permute-start(bf16[9,256,128]{2,1,0:T(8,128)(2,1)} %shard_map.299), channel_id=1, source_target_pairs={{0,2},{1,3},{2,0},{3,1},{4,6},{5,7},{6,4},{7,5},{8,10},{9,11},{10,... | collective-permute-start | bytes 1769480 | tf_op jit(solution)/shard_map/ppermute | solution.py:755
  122.9 11.4 %collective-permute-start.23 = (bf16[784,256]{1,0:T(8,128)(2,1)S(1)}, bf16[784,256]{1,0:T(8,128)(2,1)S(1)}, u32[]{:S(2)}, u32[]{:S(2)}) collective-permute-start(bf16[784,256]{1,0:T(8,128)(2,1)S(1)} %shard_map.302), channel_id=1, source_target_pairs={{0,2},{1,3},{2,0},{3,1},{4,6},{5,7},{6,4},{7,5},{8,10},{9,11},{10,... | collective-permute-start | bytes 1204232 | tf_op jit(solution)/shard_map/ppermute | solution.py:755
  124.9 30.2 %collective-permute-start.25 = (bf16[9,256,128]{2,1,0:T(8,128)(2,1)}, bf16[9,256,128]{2,1,0:T(8,128)(2,1)}, u32[]{:S(2)}, u32[]{:S(2)}) collective-permute-start(bf16[9,256,128]{2,1,0:T(8,128)(2,1)} %collective-permute-done.21.refs_8_.refs_12_), channel_id=1, source_target_pairs={{0,1},{1,0},{2,3},{3,2},{4,5},{5,4},{6,7},{7,6},{8,9},{9,8},{10,11... | collective-permute-start | bytes 1769480 | tf_op jit(solution)/shard_map/ppermute | solution.py:755
  140.3 14.8 %collective-permute-start.24 = (bf16[784,256]{1,0:T(8,128)(2,1)}, bf16[784,256]{1,0:T(8,128)(2,1)}, u32[]{:S(2)}, u32[]{:S(2)}) collective-permute-start(bf16[784,256]{1,0:T(8,128)(2,1)} %get-tuple-element.113), channel_id=1, source_target_pairs={{0,2},{1,3},{2,0},{3,1},{4,6},{5,7},{6,4},{7,5},{8,10},{9,11},{10,... | collective-permute-start | bytes 1204232 | tf_op jit(solution)/shard_map/ppermute | solution.py:755
  141.6 11.3 %collective-permute-start.26 = (bf16[384,512]{1,0:T(8,128)(2,1)}, bf16[384,512]{1,0:T(8,128)(2,1)}, u32[]{:S(2)}, u32[]{:S(2)}) collective-permute-start(bf16[384,512]{1,0:T(8,128)(2,1)} %get-tuple-element.110.refs_11_), channel_id=1, source_target_pairs={{0,4},{4,0},{8,12},{12,8},{16,20},{20,16},{24,28},{28,24},{1,5},{5... | collective-permute-start | bytes 1179656 | tf_op jit(solution)/shard_map/ppermute | solution.py:768
  142.2 12.9 %all-to-all-start.2 = ((f32[32,4,256]{2,1,0:T(4,128)}), f32[32,4,256]{2,1,0:T(4,128)S(1)}, u32[]{:S(2)}, u32[]{:S(2)}) async-start(f32[32,4,256]{2,1,0:T(4,128)} %get-tuple-element.111), calls=%async_computation.2 | async-start | bytes 262144 | tf_op jit(solution)/shard_map/all_to_all | solution.py:780
  169.1 20.3 %collective-permute-start.28 = (bf16[4736,128]{1,0:T(8,128)(2,1)}, bf16[4736,128]{1,0:T(8,128)(2,1)}, u32[]{:S(2)}, u32[]{:S(2)}) collective-permute-start(bf16[4736,128]{1,0:T(8,128)(2,1)} %get-tuple-element.123), channel_id=1, source_target_pairs={{0,1},{1,0},{2,3},{3,2},{4,5},{5,4},{6,7},{7,6},{8,9},{9,8},{10,11... | collective-permute-start | bytes 3637256 | tf_op jit(solution)/shard_map/ppermute | solution.py:755
  169.1 23.7 %collective-permute-start.27 = (bf16[784,256]{1,0:T(8,128)(2,1)}, bf16[784,256]{1,0:T(8,128)(2,1)}, u32[]{:S(2)}, u32[]{:S(2)}) collective-permute-start(bf16[784,256]{1,0:T(8,128)(2,1)} %get-tuple-element.117), channel_id=1, source_target_pairs={{0,2},{1,3},{2,0},{3,1},{4,6},{5,7},{6,4},{7,5},{8,10},{9,11},{10,... | collective-permute-start | bytes 1204232 | tf_op jit(solution)/shard_map/ppermute | solution.py:755
  169.9 23.0 %all-to-all-start.3 = ((f32[32,2,256]{2,1,0:T(2,128)}), f32[32,2,256]{2,1,0:T(2,128)S(1)}, u32[]{:S(2)}, u32[]{:S(2)}) async-start(f32[32,2,256]{2,1,0:T(2,128)} %get-tuple-element.118), calls=%async_computation.3 | async-start | bytes 131072 | tf_op jit(solution)/shard_map/all_to_all | solution.py:780
  175.5 11.0 %collective-permute-start.30 = (bf16[96,512]{1,0:T(8,128)(2,1)}, bf16[96,512]{1,0:T(8,128)(2,1)S(1)}, u32[]{:S(2)}, u32[]{:S(2)}) collective-permute-start(bf16[96,512]{1,0:T(8,128)(2,1)} %get-tuple-element.126), channel_id=1, source_target_pairs={{0,16},{4,20},{8,24},{12,28},{16,0},{20,4},{24,8},{28,12},{1,17},{... | collective-permute-start | bytes 294920 | tf_op jit(solution)/shard_map/ppermute | solution.py:768
  197.6 16.1 %collective-permute-start.33 = (bf16[2368,128]{1,0:T(8,128)(2,1)S(1)}, bf16[2368,128]{1,0:T(8,128)(2,1)S(1)}, u32[]{:S(2)}, u32[]{:S(2)}) collective-permute-start(bf16[2368,128]{1,0:T(8,128)(2,1)S(1)} %copy-done.11), channel_id=1, source_target_pairs={{0,4},{4,0},{8,12},{12,8},{16,20},{20,16},{24,28},{28,24},{1,5},{5... | collective-permute-start | bytes 1818632 | tf_op jit(solution)/shard_map/ppermute | solution.py:768
  199.1 10.1 %collective-permute-start.34 = (bf16[96,512]{1,0:T(8,128)(2,1)S(1)}, bf16[96,512]{1,0:T(8,128)(2,1)S(1)}, u32[]{:S(2)}, u32[]{:S(2)}) collective-permute-start(bf16[96,512]{1,0:T(8,128)(2,1)S(1)} %copy-done.9), channel_id=1, source_target_pairs={{0,8},{4,12},{8,0},{12,4},{16,24},{20,28},{24,16},{28,20},{1,9},{5... | collective-permute-start | bytes 294920 | tf_op jit(solution)/shard_map/ppermute | solution.py:768
  200.3 10.7 %collective-permute-start.35 = (bf16[96,512]{1,0:T(8,128)(2,1)S(1)}, bf16[96,512]{1,0:T(8,128)(2,1)S(1)}, u32[]{:S(2)}, u32[]{:S(2)}) collective-permute-start(bf16[96,512]{1,0:T(8,128)(2,1)S(1)} %copy-done.9), channel_id=1, source_target_pairs={{0,16},{4,20},{8,24},{12,28},{16,0},{20,4},{24,8},{28,12},{1,17},{... | collective-permute-start | bytes 294920 | tf_op jit(solution)/shard_map/ppermute | solution.py:768
  217.3 17.1 %collective-permute-start.41 = (bf16[384,512]{1,0:T(8,128)(2,1)}, bf16[384,512]{1,0:T(8,128)(2,1)S(1)}, u32[]{:S(2)}, u32[]{:S(2)}) collective-permute-start(bf16[384,512]{1,0:T(8,128)(2,1)} %get-tuple-element.135.refs_1_), channel_id=1, source_target_pairs={{0,4},{4,0},{8,12},{12,8},{16,20},{20,16},{24,28},{28,24},{1,5},{5... | collective-permute-start | bytes 1179656 | tf_op jit(solution)/shard_map/ppermute | solution.py:768
  218.8 15.6 %collective-permute-start.37 = (bf16[256,512]{1,0:T(8,128)(2,1)}, bf16[256,512]{1,0:T(8,128)(2,1)S(1)}, u32[]{:S(2)}, u32[]{:S(2)}) collective-permute-start(bf16[256,512]{1,0:T(8,128)(2,1)} %get-tuple-element.131), channel_id=1, source_target_pairs={{0,4},{4,0},{8,12},{12,8},{16,20},{20,16},{24,28},{28,24},{1,5},{5... | collective-permute-start | bytes 786440 | tf_op jit(solution)/shard_map/ppermute | solution.py:768
  219.4 9.6 %collective-permute-start.38 = (bf16[592,128]{1,0:T(8,128)(2,1)}, bf16[592,128]{1,0:T(8,128)(2,1)S(1)}, u32[]{:S(2)}, u32[]{:S(2)}) collective-permute-start(bf16[592,128]{1,0:T(8,128)(2,1)} %get-tuple-element.132), channel_id=1, source_target_pairs={{0,8},{4,12},{8,0},{12,4},{16,24},{20,28},{24,16},{28,20},{1,9},{5... | collective-permute-start | bytes 454664 | tf_op jit(solution)/shard_map/ppermute | solution.py:768
  220.6 13.8 %collective-permute-start.39 = (bf16[592,128]{1,0:T(8,128)(2,1)}, bf16[592,128]{1,0:T(8,128)(2,1)S(1)}, u32[]{:S(2)}, u32[]{:S(2)}) collective-permute-start(bf16[592,128]{1,0:T(8,128)(2,1)} %get-tuple-element.133), channel_id=1, source_target_pairs={{0,16},{4,20},{8,24},{12,28},{16,0},{20,4},{24,8},{28,12},{1,17},{... | collective-permute-start | bytes 454664 | tf_op jit(solution)/shard_map/ppermute | solution.py:768
  222.3 12.2 %collective-permute-start.40 = (bf16[592,128]{1,0:T(8,128)(2,1)}, bf16[592,128]{1,0:T(8,128)(2,1)S(1)}, u32[]{:S(2)}, u32[]{:S(2)}) collective-permute-start(bf16[592,128]{1,0:T(8,128)(2,1)} %get-tuple-element.134), channel_id=1, source_target_pairs={{0,24},{4,28},{8,16},{12,20},{16,8},{20,12},{24,0},{28,4},{1,25},{... | collective-permute-start | bytes 454664 | tf_op jit(solution)/shard_map/ppermute | solution.py:768
  239.3 22.4 %collective-permute-start.42 = (bf16[592,128]{1,0:T(8,128)(2,1)}, bf16[592,128]{1,0:T(8,128)(2,1)S(1)}, u32[]{:S(2)}, u32[]{:S(2)}) collective-permute-start(bf16[592,128]{1,0:T(8,128)(2,1)} %get-tuple-element.136.refs_3_.refs_1_), channel_id=1, source_target_pairs={{0,8},{4,12},{8,0},{12,4},{16,24},{20,28},{24,16},{28,20},{1,9},{5... | collective-permute-start | bytes 454664 | tf_op jit(solution)/shard_map/ppermute | solution.py:768
  241.6 20.0 %collective-permute-start.43 = (bf16[592,128]{1,0:T(8,128)(2,1)}, bf16[592,128]{1,0:T(8,128)(2,1)S(1)}, u32[]{:S(2)}, u32[]{:S(2)}) collective-permute-start(bf16[592,128]{1,0:T(8,128)(2,1)} %get-tuple-element.136.refs_3_.refs_1_), channel_id=1, source_target_pairs={{0,16},{4,20},{8,24},{12,28},{16,0},{20,4},{24,8},{28,12},{1,17},{... | collective-permute-start | bytes 454664 | tf_op jit(solution)/shard_map/ppermute | solution.py:768
  242.3 19.4 %collective-permute-start.44 = (bf16[592,128]{1,0:T(8,128)(2,1)}, bf16[592,128]{1,0:T(8,128)(2,1)S(1)}, u32[]{:S(2)}, u32[]{:S(2)}) collective-permute-start(bf16[592,128]{1,0:T(8,128)(2,1)} %get-tuple-element.136.refs_3_.refs_1_), channel_id=1, source_target_pairs={{0,24},{4,28},{8,16},{12,20},{16,8},{20,12},{24,0},{28,4},{1,25},{... | collective-permute-start | bytes 454664 | tf_op jit(solution)/shard_map/ppermute | solution.py:768
  245.1 16.5 %collective-permute-start.46 = (bf16[64,512]{1,0:T(8,128)(2,1)}, bf16[64,512]{1,0:T(8,128)(2,1)S(1)}, u32[]{:S(2)}, u32[]{:S(2)}) collective-permute-start(bf16[64,512]{1,0:T(8,128)(2,1)} %get-tuple-element.139), channel_id=1, source_target_pairs={{0,16},{4,20},{8,24},{12,28},{16,0},{20,4},{24,8},{28,12},{1,17},{... | collective-permute-start | bytes 196616 | tf_op jit(solution)/shard_map/ppermute | solution.py:768
  266.0 29.9 %all-to-all-start.4 = ((bf16[32,64,128]{2,1,0:T(8,128)(2,1)}), bf16[32,64,128]{2,1,0:T(8,128)(2,1)S(1)}, u32[]{:S(2)}, u32[]{:S(2)}) async-start(bf16[32,64,128]{2,1,0:T(8,128)(2,1)} %get-tuple-element.142), calls=%async_computation.4 | async-start | bytes 1048576 | tf_op jit(solution)/shard_map/all_to_all | solution.py:1032
  271.6 20.6 %collective-permute-start.48 = (bf16[2368,128]{1,0:T(8,128)(2,1)}, bf16[2368,128]{1,0:T(8,128)(2,1)S(1)}, u32[]{:S(2)}, u32[]{:S(2)}) collective-permute-start(bf16[2368,128]{1,0:T(8,128)(2,1)} %get-tuple-element.143.refs_1_), channel_id=1, source_target_pairs={{0,4},{4,0},{8,12},{12,8},{16,20},{20,16},{24,28},{28,24},{1,5},{5... | collective-permute-start | bytes 1818632 | tf_op jit(solution)/shard_map/ppermute | solution.py:768
  (78 other events, 421.5 us)

commit v2 on v1

--- a/solution.py
+++ b/solution.py
@@ -41,9 +41,48 @@
         self.array = array
 
 
+class Late:
+    def __init__(self, array):
+        self.array = array
+
+
+class Early:
+    def __init__(self, shape, dtype, parts):
+        self.shape = shape
+        self.dtype = dtype
+        self.parts = parts
+
+
+class Leaving:
+    def __init__(self, target, ref, sems):
+        self.target = target
+        self.ref = ref
+        self.sems = sems
+        self.copies = []
+        self.shape = ref.shape
+        self.dtype = ref.dtype
+
+    def __getitem__(self, index):
+        return self.ref[index]
+
+    def __setitem__(self, index, value):
+        self.ref[index] = value
+
+    def leave(self, source, target):
+        copy = pltpu.make_async_copy(self.ref.at[source], self.target.at[target], self.sems.at[len(self.copies)])
+        copy.start()
+        self.copies.append(copy)
+
+
 class Near:
     def __init__(self, array):
         self.array = array
+
+
+class Loose:
+    def __init__(self, shape, dtype):
+        self.shape = shape
+        self.dtype = dtype
 
 
 class Arriving:
@@ -63,20 +102,25 @@
     return pltpu.VMEM(shape, kind)
 
 
-def call(body, out_shape, scratch=(), deps=(), ints=None, floats=None):
+def call(body, out_shape, scratch=(), deps=(), ints=None, floats=None, work=0, room=VMEM_BYTES):
     single = not isinstance(out_shape, (tuple, list))
     shapes = (out_shape,) if single else tuple(out_shape)
-    away = [isinstance(out, jax.ShapeDtypeStruct) for out in shapes]
-    outs = tuple(pltpu.HBM(out.shape, out.dtype) if far else out for out, far in zip(shapes, away))
+    early = [isinstance(out, Early) for out in shapes]
+    away = [isinstance(out, (jax.ShapeDtypeStruct, Early)) for out in shapes]
+    loose = [isinstance(out, Loose) for out in shapes]
+    outs = tuple(
+        pltpu.HBM(out.shape, out.dtype) if far else jax.ShapeDtypeStruct(out.shape, out.dtype) if free else out
+        for out, far, free in zip(shapes, away, loose)
+    )
     scalars = [array for array in (ints, floats) if array is not None]
 
     def bare(arg):
-        while isinstance(arg, (Pick, Free, Near)):
+        while isinstance(arg, (Pick, Free, Near, Late)):
             arg = arg.array
         return arg
 
     def placed(arg):
-        inner = arg.array if isinstance(arg, Pick) else arg
+        inner = arg.array if isinstance(arg, (Pick, Late)) else arg
         if isinstance(inner, Free):
             return inner.array
         if isinstance(inner, Near):
@@ -84,10 +128,20 @@
         return pltpu.with_memory_space_constraint(inner, pltpu.HBM)
 
     def run(*args):
-        fetched = [isinstance(arg, Pick) and not isinstance(arg.array, Near) for arg in args]
-        buffers = [pltpu.VMEM(arg.array.shape[1:], arg.array.dtype) for arg, own in zip(args, fetched) if own]
-        if buffers:
-            buffers.append(pltpu.SemaphoreType.DMA((len(buffers),)))
+        fetched = [
+            isinstance(arg, Late) or isinstance(arg, Pick) and not isinstance(arg.array, Near) for arg in args
+        ]
+        buffers = [
+            pltpu.VMEM(arg.array.shape[1 if isinstance(arg, Pick) else 0 :], arg.array.dtype)
+            for arg, own in zip(args, fetched)
+            if own
+        ]
+        count = len(buffers)
+        for out, parts in zip(shapes, early):
+            if parts:
+                buffers += [pltpu.VMEM(out.shape, out.dtype), pltpu.SemaphoreType.DMA((out.parts,))]
+        if count:
+            buffers.append(pltpu.SemaphoreType.DMA((count,)))
 
         def kernel(*refs):
             first = refs[: len(scalars)]
@@ -105,7 +159,17 @@
                     copy.start()
                     ref = Arriving(copy, local[place])
                 passed.append(ref)
-            body(*first, *passed, *results, *rest)
+            leaving, done = [], count
+            for result, parts in zip(results, early):
+                if parts:
+                    result = Leaving(result, local[done], local[done + 1])
+                    done += 2
+                leaving.append(result)
+            body(*first, *passed, *leaving, *rest)
+            for result in leaving:
+                if isinstance(result, Leaving):
+                    for copy in result.copies:
+                        copy.wait()
 
         kernel.__name__ = getattr(body, "func", body).__name__
         anywhere = pl.BlockSpec(memory_space=pl.ANY)
@@ -115,11 +179,15 @@
             in_specs=[SMEM] * len(scalars)
             + [anywhere if own else VMEM for own in fetched]
             + [anywhere] * len(deps),
-            out_specs=[VMEM] * len(outs),
+            out_specs=[anywhere if parts else VMEM for parts in early],
             scratch_shapes=buffers + list(scratch),
-            compiler_params=pltpu.CompilerParams(vmem_limit_bytes=VMEM_BYTES),
-        )(*scalars, *[placed(arg) for arg in args], *[bare(dep) for dep in deps])
-        results = tuple(result if far else Near(result) for result, far in zip(results, away))
+            compiler_params=pltpu.CompilerParams(vmem_limit_bytes=room),
+            cost_estimate=pl.CostEstimate(flops=work, bytes_accessed=0, transcendentals=0) if work else None,
+        )(*scalars, *[placed(arg) for arg in args], *[placed(dep) for dep in deps])
+        results = tuple(
+            result if far else Free(result) if free else Near(result)
+            for result, far, free in zip(results, away, loose)
+        )
         return results[0] if single else results
 
     return run
@@ -167,40 +235,43 @@
     return (seg_index(line_rows, seg_count) < count).astype(F32)
 
 
-def split_blocks(ints_ref, w_ref, *refs):
-    size = refs[0].shape[0]
+def split_blocks(
+    ints_ref, w_ref, gain_one_ref, shift_one_ref, gain_two_ref, shift_two_ref, near_ref, far_ref, *refs
+):
+    size = refs[0].shape[0] - 96
+    small = jnp.concatenate(
+        [ref[...] for ref in (gain_one_ref, shift_one_ref, gain_two_ref, shift_two_ref, near_ref, far_ref)]
+        + [jnp.zeros((10, refs[0].shape[1]), F32)],
+        axis=0,
+    )
+    pieces = []
+    for _ in range(3):
+        piece = small.astype(BF16)
+        pieces.append(piece)
+        small = small - piece.astype(F32)
     for bits, ref in enumerate(refs):
         start = (ints_ref[0] ^ bits) * size
-        ref[...] = w_ref[pl.ds(pl.multiple_of(start, size), size), :]
-
-
-def reduce_other(ints_ref, own_ref, near_ref, far_ref, cross_ref, x_ref, part_ref, w_ref):
+        ref[:size, :] = w_ref[pl.ds(pl.multiple_of(start, size), size), :]
+        for index, piece in enumerate(pieces):
+            ref[size + 32 * index : size + 32 * (index + 1), :] = piece
+
+
+def reduce_other(ints_ref, own_ref, near_ref, far_ref, cross_ref, x_ref, part_ref, w_ref, small_ref):
     core = ints_ref[3]
-    size = own_ref.shape[1]
-    for place, (first, second) in enumerate(((own_ref, near_ref), (far_ref, cross_ref))):
-        for index, ref in ((core, first), (1 - core, second)):
-            start = pl.multiple_of((2 * place + index) * size, size)
-            w_ref[:, pl.ds(start, size)] = ref[...]
+    rows, size = w_ref.shape[0], own_ref.shape[1]
+    blocks = (own_ref, near_ref, far_ref, cross_ref)
+    for bits, ref in enumerate(blocks):
+        start = pl.multiple_of((2 * (bits // 2) + (core ^ (bits % 2))) * size, size)
+        w_ref[:, pl.ds(start, size)] = ref[:rows, :]
+    for bits, ref in enumerate(blocks):
+        pieces = [ref[rows + 32 * index : rows + 32 * (index + 1), :].astype(F32) for index in range(3)]
+        small_ref[(2 * ints_ref[1] + core) ^ bits] = (pieces[0] + (pieces[1] + pieces[2]))[:24]
     part_ref[...] = dot32(x_ref[...], w_ref[...]).astype(BF16)
 
 
 def add_low(near_ref, far_ref, out_ref):
     half = out_ref.shape[1]
     out_ref[...] = (far_ref[...] + near_ref[:, half:].astype(F32)).astype(BF16)
-
-
-def pack_small(gain_one_ref, shift_one_ref, gain_two_ref, shift_two_ref, near_ref, far_ref, out_ref):
-    out_ref[...] = jnp.zeros_like(out_ref)
-    for row, ref in enumerate((gain_one_ref, shift_one_ref, gain_two_ref, shift_two_ref)):
-        out_ref[row : row + 1, :] = ref[...]
-    out_ref[4:13, :] = near_ref[...]
-    out_ref[13:22, :] = far_ref[...]
-
-
-def join_small(ints_ref, own_ref, near_ref, far_ref, cross_ref, out_ref):
-    chan = 2 * ints_ref[1] + ints_ref[3]
-    for bits, ref in enumerate((own_ref, near_ref, far_ref, cross_ref)):
-        out_ref[chan ^ bits] = ref[...]
 
 
 def small_row(small_ref, side, row):
@@ -485,7 +556,8 @@
 
 def conv_backward(
     seg_count, ints_ref, floats_ref, grad_ref, more_ref, act_ref, oth_ref, got_ref, back_ref, first_ref, got_one_ref,
-    small_ref, w_ref, from_ref, pair_ref, slope_ref, low_ref, sent_ref, field_ref, cat_ref, acc_ref, w_all_ref,
+    small_ref, w_ref, from_ref, pair_ref, kern_grad_ref, slope_ref, low_ref, sent_ref, keep_ref, send_ref,
+    field_ref, cat_ref, acc_ref, w_all_ref,
 ):
     line_rows = SIDE * seg_count
     half = grad_ref.shape[1]
@@ -510,6 +582,10 @@
     core = ints_ref[3]
     size = half // 2
     depth = 2 * half
+    for index, ref in ((core, keep_ref), (1 - core, send_ref)):
+        lanes = pl.ds(pl.multiple_of(index * size, size), size)
+        ref[:span, :] = field_ref[:, lanes]
+        ref[span:, :] = kern_grad_ref[:, lanes].astype(BF16)
     for tap in range(9):
         w_all_ref[tap, :, :half] = w_ref[tap // 3, (tap % 3) * depth : (tap % 3) * depth + half, :]
         for index, ref in ((core, from_ref), (1 - core, pair_ref)):
@@ -546,28 +622,32 @@
     send_ref[...] = rows_ref[pl.ds(pl.multiple_of((1 - index) * size, 16), size), :]
 
 
-def taps_gradient(seg_count, ints_ref, hid_ref, field_ref, kern_grad_ref, keep_ref, send_ref, taps_ref):
+def taps_gradient(
+    seg_count, ints_ref, hid_ref, field_ref, near_hid_ref, near_field_ref, keep_ref, send_ref, taps_ref, own_ref, near_ref,
+    sum_ref,
+):
     line_rows = SIDE * seg_count
-    taps_ref[...] = jnp.zeros_like(taps_ref)
-    for line in range(SIDE):
-        rows = slice(line * line_rows, (line + 1) * line_rows)
-        store_taps(taps_ref, line, hid_ref[rows, :], line_rows, seg_count)
     step = WIDE * seg_count
     span = SIDE * step
-    depth = taps_ref.shape[1] // 3
-    lanes_of = [pl.ds(pl.multiple_of(index * LANES, LANES), LANES) for index in (ints_ref[3], 1 - ints_ref[3])]
-    fields = jnp.concatenate([field_ref[:, lanes] for lanes in lanes_of], axis=1)
-    for tap in range(9):
-        start = (tap // 3) * step
-        left = taps_ref[start : start + span, (tap % 3) * depth : (tap % 3 + 1) * depth]
-        part = dot32(left, fields, ((0,), (0,))).astype(BF16)
-        for place, ref in enumerate((keep_ref, send_ref)):
-            ref[tap * depth : (tap + 1) * depth, :] = part[:, place * LANES : (place + 1) * LANES]
-    rest = keep_ref.shape[0] - 9 * depth
-    count = kern_grad_ref.shape[0]
-    for lanes, ref in zip(lanes_of, (keep_ref, send_ref)):
-        ref[9 * depth : 9 * depth + count, :] = kern_grad_ref[:, lanes].astype(BF16)
-        ref[9 * depth + count :, :] = jnp.zeros((rest - count, LANES), BF16)
+    taps_ref[...] = jnp.zeros_like(taps_ref)
+    for source, turned in ((hid_ref, own_ref), (near_hid_ref, near_ref)):
+        for line in range(SIDE):
+            rows = slice(line * line_rows, (line + 1) * line_rows)
+            store_taps(taps_ref, line, source[rows, :], line_rows, seg_count)
+        for start in range(0, taps_ref.shape[1], LANES):
+            turned[start : start + LANES, :] = taps_ref[:, start : start + LANES].T
+    depth = taps_ref.shape[1]
+    own, near = field_ref[:span, :], near_field_ref[:span, :]
+    for row_off in range(3):
+        rows = slice(row_off * step, row_off * step + span)
+        part = dot32(own_ref[:, rows], own) + dot32(near_ref[:, rows], near)
+        sum_ref[row_off * depth : (row_off + 1) * depth, :] = part.astype(BF16)
+    rest = sum_ref.shape[0] - 3 * depth
+    count = field_ref.shape[0] - span
+    sum_ref[3 * depth :, :] = jnp.zeros((rest, LANES), BF16)
+    kern_grad = field_ref[span:, :].astype(F32) + near_field_ref[span:, :].astype(F32)
+    sum_ref[3 * depth : 3 * depth + count, :] = kern_grad.astype(BF16)
+    split_rows(sum_ref, ints_ref[4], keep_ref, send_ref)
 
 
 def sum_into(sum_ref, *refs):
@@ -612,34 +692,49 @@
 
 
 def stage_one(places, ints_ref, pack_ref, pack_got_ref, reduce_ref, *refs):
-    wide, refs = refs[:places], refs[places:]
-    blocks, (keep_ref, send_ref, join_ref, sum_ref) = refs[:places], refs[places:]
+    blocks, (keep_ref, send_ref, sum_ref) = refs[:places], refs[places:]
     sum_into(sum_ref, pack_ref, pack_got_ref)
     store_blocks(ints_ref, sum_ref, blocks)
     split_rows(reduce_ref, ints_ref[4], keep_ref, send_ref)
-    join_blocks(ints_ref, wide, join_ref)
 
 
 def stage_two(places, ints_ref, keep_ref, got_ref, *refs):
-    pack, (part_ref, *blocks, sum_ref) = refs[:places], refs[places:]
-    sum_into(part_ref, *pack)
-    sum_into(sum_ref, keep_ref, got_ref)
-    store_blocks(ints_ref, sum_ref, blocks)
-
-
-def stage_three(places, ints_ref, *refs):
-    pack, reduce, (join_ref, columns_ref) = refs[:places], refs[places : 2 * places], refs[2 * places :]
-    join_blocks(ints_ref, pack, join_ref)
-    total = reduce[0][...].astype(F32)
-    for ref in reduce[1:]:
+    pack, refs = refs[:places], refs[places:]
+    outs, sum_ref = refs[:places], refs[places]
+    total = pack[0][...].astype(F32)
+    for ref in pack[1:]:
         total += ref[...].astype(F32)
     total = total.astype(BF16)
-    size = columns_ref.shape[2]
+    sum_into(sum_ref, keep_ref, got_ref)
+    rows, lanes = total.shape
+    size = sum_ref.shape[0] // places
+    for bits, ref in enumerate(outs):
+        ref[:rows, :] = total
+        start = pl.multiple_of((ints_ref[5] ^ bits) * size, 8)
+        block = sum_ref[pl.ds(start, size), :].astype(BF16)
+        for index in range(sum_ref.shape[1] // lanes):
+            ref[rows + index * size : rows + (index + 1) * size, :] = block[:, index * lanes : (index + 1) * lanes]
+
+
+def stage_three(places, rows, ints_ref, *refs):
+    parts, (join_ref, columns_ref) = refs[:places], refs[places:]
+    size = columns_ref.shape[1]
+    for bits, ref in enumerate(parts):
+        start = pl.multiple_of((ints_ref[5] ^ bits) * rows, 8)
+        join_ref[pl.ds(start, rows), :] = ref[:rows, :]
+    total = parts[0][rows:, :].astype(F32)
+    for ref in parts[1:]:
+        total += ref[rows:, :].astype(F32)
+    total = total.astype(BF16)
     for place, side in enumerate((ints_ref[1], 1 - ints_ref[1])):
         for core in range(2):
             start = (2 * place + core) * size
             for clip in range(columns_ref.shape[0] // 4):
-                columns_ref[clip * 4 + 2 * side + core] = total[:, start : start + size]
+                columns_ref[clip * 4 + 2 * side + core] = total[start : start + size, :]
+
+
+def join_places(ints_ref, *refs):
+    join_blocks(ints_ref, refs[:-1], refs[-1])
 
 
 def unpack_spatial(ints_ref, own_ref, got_ref, out_ref, near_ref, far_ref, rows_ref):
@@ -667,7 +762,7 @@
 
 
 def last_norm(
-    seg_count, ints_ref, floats_ref, grad_ref, more_ref, act_ref, oth_ref, got_ref, back_ref, small_ref, low_ref,
+    seg_count, ints_ref, floats_ref, grad_ref, more_ref, act_ref, oth_ref, got_ref, back_ref, small_ref, low_own_ref, low_oth_ref,
 ):
     line_rows = SIDE * seg_count
     side = ints_ref[1]
@@ -682,7 +777,7 @@
             rows = slice(line * line_rows, (line + 1) * line_rows)
             normed = (acts[rows, :].astype(F32) - average) * inv_std
             grad = scale * (grads[rows, :].astype(F32) - mask * (mean + normed * mix))
-            low_ref[rows, place * half : (place + 1) * half] = grad.astype(BF16)
+            (low_own_ref, low_oth_ref)[place][rows, :] = grad.astype(BF16)
 
 
 def pick_rows(ints_ref, w_ref, out_ref):
@@ -705,15 +800,25 @@
     split_rows(out_ref, ints_ref[4], keep_ref, send_ref)
 
 
-def reduce_gradient(ints_ref, x_own_ref, low_ref, x_oth_ref, near_ref, out_ref):
-    part = dot32(x_own_ref[...], low_ref[...], ((0,), (0,)))
-    out_ref[...] = (part + dot32(x_oth_ref[...], near_ref[...], ((0,), (0,)))).astype(BF16)
-
-
-def input_gradient(ints_ref, low_ref, w_ref, resid_ref, near_ref, out_ref):
+def reduce_gradient(
+    ints_ref, x_own_ref, own_ref, oth_ref, x_oth_ref, near_own_ref, near_oth_ref, keep_ref, send_ref, out_ref
+):
+    half = own_ref.shape[1]
+    for place, (low, near) in enumerate(((own_ref, near_own_ref), (oth_ref, near_oth_ref))):
+        part = dot32(x_own_ref[...], low[...], ((0,), (0,))) + dot32(x_oth_ref[...], near[...], ((0,), (0,)))
+        out_ref[:, place * half : (place + 1) * half] = part.astype(BF16)
+    split_rows(out_ref, ints_ref[4], keep_ref, send_ref)
+
+
+def input_gradient(
+    ints_ref, own_ref, oth_ref, w_ref, resid_ref, near_own_ref, near_oth_ref, out_ref
+):
     core = ints_ref[3]
-    out_ref[core] = resid_ref[0] + dot32(low_ref[...], w_ref[...], ((1,), (1,)))
-    out_ref[1 - core] = resid_ref[1] + dot32(near_ref[...], w_ref[...], ((1,), (1,)))
+    half = own_ref.shape[1]
+    w_own, w_oth = w_ref[:, :half], w_ref[:, half:]
+    for clip, (own, oth) in enumerate(((own_ref, oth_ref), (near_own_ref, near_oth_ref))):
+        grad = dot32(own[...], w_own, ((1,), (1,))) + dot32(oth[...], w_oth, ((1,), (1,)))
+        out_ref[core if clip == 0 else 1 - core] = resid_ref[clip] + grad
 
 
 def per_device(
@@ -751,8 +856,8 @@
     sds = jax.ShapeDtypeStruct
 
     def swap(array, bits):
-        array = array.array if isinstance(array, Near) else array
-        return lax.ppermute(array, "chan", [(i, i ^ bits) for i in range(chan_size)])
+        array = array.array if isinstance(array, (Near, Free)) else array
+        return Free(lax.ppermute(array, "chan", [(i, i ^ bits) for i in range(chan_size)]))
 
     def own_first(array, index, size, axis):
         own = lax.dynamic_slice_in_dim(array, index * size, size, axis)
@@ -764,7 +869,7 @@
         return jnp.where(flip, oth, own), jnp.where(flip, own, oth)
 
     def swap_clip(array, bits):
-        array = array.array if isinstance(array, Near) else array
+        array = array.array if isinstance(array, (Near, Free)) else array
         return lax.ppermute(array, "clip", [(i, i ^ bits) for i in range(clip_size)])
 
     parity, place = clip_index % 2, clip_index // 2
@@ -802,22 +907,20 @@
     span = SIDE * WIDE * seg_count
     edge_rows = EDGE * EDGE * seg_count
 
-    block_shape = sds((chan_local, mid_local), BF16)
+    block_shape = sds((chan_local + 96, mid_local), BF16)
     chan = chan_index.astype(jnp.int32)[None]
-    sent_blocks = call(split_blocks, (block_shape,) * chan_size, ints=chan)(w_reduce)
+    sent_blocks = call(split_blocks, (block_shape,) * chan_size, ints=chan)(
+        w_reduce, gain_one[None], shift_one[None], gain_two[None], shift_two[None], near_kern, far_kern
+    )
     got_blocks = {bits: swap(sent_blocks[bits], bits) for bits in (2, 3, 1)}
 
-    small_own = call(pack_small, sds((24, mid_local), F32))(
-        gain_one[None], shift_one[None], gain_two[None], shift_two[None], near_kern, far_kern
-    )
-    small = call(join_small, sds((chan_size, 24, mid_local), F32), ints=ints)(
-        small_own, *[swap(small_own, bits) for bits in (1, 2, 3)]
-    )
-
-    part_oth, w_rows = call(
+    part_oth, w_rows, small = call(
         reduce_other,
-        (near((row_count, mid_width), BF16), sds((chan_local, mid_width), BF16)),
-        deps=(small,),
+        (
+            near((row_count, mid_width), BF16),
+            sds((chan_local, mid_width), BF16),
+            sds((chan_size, 24, mid_local), F32),
+        ),
         ints=ints,
     )(sent_blocks[0], got_blocks[1], got_blocks[2], got_blocks[3], x_oth)
     near_one = swap(part_oth, 1)
@@ -828,7 +931,7 @@
     )(near_one, w_rows, x_own)
     far_one = swap(far_send, 2)
 
-    w_pair = jnp.concatenate(pair(w_spatial, swap(w_spatial, 1)), axis=2)
+    w_pair = jnp.concatenate(pair(w_spatial, swap(w_spatial, 1).array), axis=2)
     w_fwd_own, w_fwd_oth = own_first(w_pair, side_index, half, 1)
     w_fwd = jnp.concatenate([w_fwd_own, w_fwd_oth], axis=1).reshape(3, 3 * mid_width, half)
 
@@ -862,6 +965,8 @@
     gated_oth = gate_call(act_two_oth, True)[0]
     near_oth = swap(gated_oth, 1)
 
+    near_hid = swap(hid_one, 1)
+
     bias_row = jnp.sum(logit_grad.astype(F32), axis=0)
     bias_row = jnp.pad(bias_row, (0, chan_local - class_count))[None]
     act_three, sent_three = call(
@@ -871,7 +976,7 @@
     )(gated_own, gated_oth, near_own, near_oth, w_expand, bias_row)
     got_three = share_clip(sent_three)
 
-    to_side = call(pick_rows, sds((9, half, mid_local), BF16), deps=(sent_three,), ints=ints)(Free(w_spatial))
+    to_side = call(pick_rows, sds((9, half, mid_local), BF16), deps=(sent_two,), ints=ints)(w_spatial)
     from_side = swap(to_side, 2)
     from_pair = swap(from_side, 1)
 
@@ -916,7 +1021,7 @@
     def to_places(blocks):
         if places > 4:
             order = place ^ jnp.arange(places)
-            sent = jnp.stack(blocks)[order]
+            sent = jnp.stack([block.array if isinstance(block, Free) else block for block in blocks])[order]
             return list(lax.all_to_all(sent, "clip", 0, 0, axis_index_groups=groups)[order])
         return [blocks[0]] + [swap_clip(blocks[bits], 2 * bits) for bits in range(1, places)]
 
@@ -924,7 +1029,7 @@
         return (sds((rows // places, width), BF16),) * places
 
     grad_classes = dot32(logit_pair, pooled, ((0,), (0,)))
-    wide_rows = -(-(mid_width + class_count) // unit) * unit
+    wide_rows = (-(-(mid_width + class_count) // unit) + 1) * unit
     wide_keep, wide_send = call(
         expand_gradient, halves(wide_rows, chan_local), [pltpu.VMEM((wide_rows, chan_local), BF16)], ints=ints,
     )(gated_own, gated_oth, near_own, near_oth, low_three_own, low_three_oth, grad_classes)
@@ -954,90 +1059,108 @@
     )(back_own, near_back, far_back, hid_two, gate, act_two, got_two, small, logits_wide)
     slope_two_oth = swap(slope_two_low, 2)
     got_back_two = share_all(sent_back_two)
-    slope_one, slope_one_low, sent_back_one, field_two = call(
+    slope_one, slope_one_low, sent_back_one, field_keep, field_send = call(
         functools.partial(conv_backward, seg_count),
-        (half_f32, half_low, sums_shape, sds((span, half), BF16)),
+        (half_f32, half_low, sums_shape) + (sds((span + 32, mid_local), BF16),) * 2,
         [
+            pltpu.VMEM((span, half), BF16),
             pltpu.VMEM((pad_rows, 3 * mid_width), BF16),
             pltpu.VMEM((span, half), F32),
             pltpu.VMEM((9, half, mid_width), BF16),
         ],
-        deps=(wide_blocks[0],),
+        deps=(wide_blocks[0], near_hid),
         ints=ints,
         floats=floats,
     )(
         slope_two, slope_two_oth, act_two, act_two_oth, got_two, got_back_two, act_one, got_one, small, w_fwd,
-        from_side, from_pair,
+        from_side, from_pair, kern_grad,
     )
     slope_one_oth = swap(slope_one_low, 2)
     got_back_one = share_all(sent_back_one)
 
     pack_rows = -(-(9 * mid_width + 32) // unit) * unit
-    pack_own, pack_send = call(
+    pack_keep, pack_pair = call(
         functools.partial(taps_gradient, seg_count),
-        (sds((pack_rows, mid_local), BF16),) * 2,
-        [pltpu.VMEM((pad_rows, 3 * mid_width), BF16)],
-        ints=ints,
-    )(hid_one, field_two, kern_grad)
-    pack_keep, pack_pair = call(
-        sum_split, halves(pack_rows, mid_local), [pltpu.VMEM((pack_rows, mid_local), BF16)], ints=ints,
-    )(pack_own, swap(pack_send, 1))
-    wide_part = call(sum_parts, sds((wide_rows // clip_size, chan_local), BF16))(*wide_got)
-
-    low_one = call(
+        halves(pack_rows, mid_local),
+        [pltpu.VMEM((pad_rows, 3 * mid_width), BF16)]
+        + [pltpu.VMEM((3 * mid_width, pad_rows), BF16)] * 2
+        + [pltpu.VMEM((pack_rows, mid_local), BF16)],
+        ints=ints,
+        work=20_000_000_000,
+        room=40 * 1024 * 1024,
+    )(hid_one, field_keep, near_hid, swap(field_send, 1))
+
+    wide_part = call(sum_parts, sds((wide_rows // clip_size, chan_local), BF16), deps=(pack_pair,))(*wide_got)
+
+    low_pair = call(
         functools.partial(last_norm, seg_count),
-        sds((row_count, mid_width), BF16),
+        (half_low,) * 2,
         deps=(pack_pair, wide_part),
         ints=ints,
         floats=floats,
+        work=50_000_000_000,
     )(slope_one, slope_one_oth, act_one, act_one_oth, got_one, got_back_one, small)
-    near_low = swap(low_one, 1)
-    reduce_all = call(reduce_gradient, sds((chan_local, mid_width), BF16), ints=ints)(
-        x_own, low_one, x_oth, near_low
-    )
+    near_pair = [swap(low, 1) for low in low_pair]
+    pack_other = swap_clip(pack_pair, 1)
+    reduce_keep, reduce_send = call(
+        reduce_gradient,
+        (Loose((chan_local // 2, mid_width), BF16),) * 2,
+        [pltpu.VMEM((chan_local, mid_width), BF16)],
+        ints=ints,
+    )(x_own, *low_pair, x_oth, *near_pair)
 
     share = chan_local // clip_size
-    stage = call(
-        functools.partial(stage_one, places),
-        blocks_of(pack_rows // 2, mid_local) + halves(chan_local, mid_width) + (sds((wide_rows // 2, chan_local), BF16),),
+    loose_blocks = (Loose((pack_rows // clip_size, mid_local), BF16),) * places
+    pack_blocks = call(
+        sum_blocks,
+        loose_blocks,
         [pltpu.VMEM((pack_rows // 2, mid_local), BF16)],
-        ints=ints,
-    )(pack_keep, swap_clip(pack_pair, 1), reduce_all, *to_places([wide_part] * places))
-    pack_blocks, (reduce_keep, reduce_send, wide_join) = stage[:places], stage[places:]
+        deps=(reduce_send,),
+        ints=ints,
+    )(pack_keep, Free(pack_other))
+    pack_got = to_places(pack_blocks)
+    wide_join = call(
+        join_places, Loose((wide_rows // 2, chan_local), BF16), deps=(pack_blocks[0],), ints=ints,
+    )(*[Free(each) for each in to_places([wide_part] * places)])
+    wide_other = swap_clip(wide_join, 1)
+    reduce_got = swap_clip(reduce_send, 1)
+    part_rows = pack_rows // clip_size
+    parts = call(
+        functools.partial(stage_two, places),
+        (Loose((part_rows + chan_size * share, mid_local), BF16),) * places,
+        [pltpu.VMEM((chan_local // 2, mid_width), F32)],
+        deps=(wide_join,),
+        ints=ints,
+    )(reduce_keep, Free(reduce_got), *[Free(each) if index else each for index, each in enumerate(pack_got)])
+    parts_got = to_places(parts)
     grad_frames = call(
-        input_gradient, sds((2, row_count, chan_local), F32), deps=(pack_blocks[0],), ints=ints,
-    )(low_one, w_rows, grad_resid, near_low)
-    wide_other = swap_clip(wide_join, 1)
-    pack_part, *reduce_blocks = call(
-        functools.partial(stage_two, places),
-        (sds((pack_rows // clip_size, mid_local), BF16),) + blocks_of(chan_local // 2, mid_width),
-        [pltpu.VMEM((chan_local // 2, mid_width), F32)],
-        deps=(grad_frames, wide_other),
-        ints=ints,
-    )(reduce_keep, swap_clip(reduce_send, 1), *to_places(pack_blocks))
+        input_gradient, sds((2, row_count, chan_local), F32), deps=(parts[0],), ints=ints,
+    )(*low_pair, w_rows, grad_resid, *near_pair)
+    pack_join, columns = call(
+        functools.partial(stage_three, places, part_rows),
+        (Loose((pack_rows // 2, mid_local), BF16), sds((everyone, share, mid_local), BF16)),
+        deps=(wide_other, grad_frames),
+        ints=ints,
+    )(*[Free(each) if index else each for index, each in enumerate(parts_got)])
+    pack_other = swap_clip(pack_join, 1)
+    reduce_got = lax.all_to_all(columns, ("clip", "chan"), 0, 0)
+    reduce_got = reduce_got.reshape(places, 2, chan_size, share, mid_local).transpose(2, 1, 0, 3, 4)
+    grad_w_reduce = reduce_got.reshape(chan_size * chan_local, mid_local).astype(F32)
     grad_w_expand, classes_got = call(
         unpack_wide,
         (sds((mid_width, chan_local), F32), sds((wide_rows - mid_width, chan_local), F32)),
         [pltpu.VMEM((wide_rows, chan_local), BF16)],
-        deps=(pack_part,),
-        ints=ints,
-    )(wide_join, wide_other)
+        deps=(pack_join,),
+        ints=ints,
+    )(wide_join, Free(wide_other))
     grad_w_classes = classes_got[:class_count].T
-    pack_join, columns = call(
-        functools.partial(stage_three, places),
-        (sds((pack_rows // 2, mid_local), BF16), sds((everyone, share, mid_local), BF16)),
-        deps=(grad_w_expand,),
-        ints=ints,
-    )(*to_places([pack_part] * places), *to_places(reduce_blocks))
-    reduce_got = lax.all_to_all(columns, ("clip", "chan"), 0, 0)
-    reduce_got = reduce_got.reshape(places, 2, chan_size, share, mid_local).transpose(2, 1, 0, 3, 4)
-    grad_w_reduce = reduce_got.reshape(chan_size * chan_local, mid_local).astype(F32)
     grad_spatial, grad_near, grad_far = call(
         unpack_spatial,
         (sds((9, mid_width, mid_local), F32),) + (sds((9, mid_local), F32),) * 2,
         [pltpu.VMEM((pack_rows, mid_local), BF16)],
         ints=ints,
-    )(pack_join, swap_clip(pack_join, 1))
+        work=20_000_000_000,
+    )(pack_join, Free(pack_other))
 
     mine = lax.dynamic_index_in_dim(got_back_two, clip_index, 0, keepdims=False)
     logits = jnp.sum(mine, axis=0)[2:, :class_count] + class_bias

time: 299 us -> 259 us (0.87)
  waiting for transfers between devices: 86 us -> 68.1 us
  local copies, waits for them, and re-layouts: 27.9 us -> 14.8 us
  Pallas kernels: 90.1 us -> 81.6 us
  other arithmetic: 5.33 us -> 9.7 us
  starting transfers between devices: 72.3 us -> 68.1 us
    ppermute x28 -> x25, waiting for transfers between devices: 59.3 us -> 29.9 us  [swap_clip(): lax.ppermute(array, 'clip', [(i, i ^ bits) for i in range(clip_size)])]
    unnamed x114 -> x54, local copies, waits for them, and re-layouts: 20.3 us -> 6.27 us
    pallas_call x30 -> x28, Pallas kernels: 90.1 us -> 81.6 us  [run(): pl.pallas_call(kernel, out_shape=outs, in_specs=[SMEM] * len(scalars) + [...]
    all_to_all x1, waiting for transfers between devices: 0.01 us -> 8.4 us  [per_device(): reduce_got = lax.all_to_all(columns, ('clip', 'chan'), 0, 0)]
    ppermute x28 -> x25, starting transfers between devices: 40.6 us -> 34.4 us  [swap_clip(): lax.ppermute(array, 'clip', [(i, i ^ bits) for i in range(clip_size)])]
    all_to_all x3, waiting for transfers between devices: 4.67 us -> 10.7 us  [share_all(): got = lax.all_to_all(sent, ('clip', 'chan'), 0, 0)]
    ppermute x21 -> x20, waiting for transfers between devices: 22 us -> 19.1 us  [swap(): lax.ppermute(array, 'chan', [(i, i ^ bits) for i in range(chan_size)])]
    ppermute x21 -> x20, starting transfers between devices: 13.8 us -> 14.1 us  [swap(): lax.ppermute(array, 'chan', [(i, i ^ bits) for i in range(chan_size)])]
  transfers between devices with their start and end apart: 53 -> 49, of which waited for: 23 -> 19; matrix products, arithmetic and copies ran while one was open for 5% -> 7% of each run, Pallas kernels for 18% -> 24%
where the time goes in v2:
time: 259 us; the launch traced here: 258 us
  Pallas kernels  81.6 us (32%)
  starting transfers between devices  68.1 us (26%)
  waiting for transfers between devices  68.1 us (26%)
  local copies, waits for them, and re-layouts  14.8 us (6%)
  blocking collectives  11.9 us (5%)
  other arithmetic  9.7 us (4%)
    pallas_call x28, Pallas kernels, run(): pl.pallas_call(kernel, out_shape=outs, in_specs=[SMEM] * len(scalars) + [...  81.6 us
    ppermute x25, starting transfers between devices, swap_clip(): lax.ppermute(array, 'clip', [(i, i ^ bits) for i in range(clip_size)])  34.4 us
    ppermute x25, waiting for transfers between devices, swap_clip(): lax.ppermute(array, 'clip', [(i, i ^ bits) for i in range(clip_size)])  29.9 us
    ppermute x20, waiting for transfers between devices, swap(): lax.ppermute(array, 'chan', [(i, i ^ bits) for i in range(chan_size)])  19.1 us
    ppermute x20, starting transfers between devices, swap(): lax.ppermute(array, 'chan', [(i, i ^ bits) for i in range(chan_size)])  14.1 us
    all_to_all x3, starting transfers between devices, share_all(): got = lax.all_to_all(sent, ('clip', 'chan'), 0, 0)  13.2 us
    all_to_all x1, blocking collectives, share_all(): got = lax.all_to_all(sent, ('clip', 'chan'), 0, 0)  11.9 us
    all_to_all x3, waiting for transfers between devices, share_all(): got = lax.all_to_all(sent, ('clip', 'chan'), 0, 0)  10.7 us
  transfers between devices with their start and end apart: 49, of which 19 were waited for; matrix products, arithmetic and copies ran while one was open for 7% of the time, Pallas kernels for 24%

profile of v2, /device:TPU:0, one launch (start us, length us, event | category | flops | bytes accessed | tf_op | source)
XLA Modules:
  0.0 257.6 jit_solution(12016021218274849576)
XLA Ops:
  3.2 2.9 %collective-permute-start.1 = (bf16[608,128]{1,0:T(8,128)(2,1)}, bf16[608,128]{1,0:T(8,128)(2,1)S(1)}, u32[]{:S(2)}, u32[]{:S(2)}) collective-permute-start(bf16[608,128]{1,0:T(8,128)(2,1)} %get-tuple-element.84), channel_id=1, source_target_pairs={{0,2},{1,3},{2,0},{3,1},{4,6},{5,7},{6,4},{7,5},{8,10},{9,11},{10,... | collective-permute-start | bytes 466952 | tf_op jit(solution)/shard_map/ppermute | solution.py:860
  13.3 3.0 %shard_map.289 = (bf16[784,512]{1,0:T(8,128)(2,1)S(1)}, bf16[512,512]{1,0:T(8,128)(2,1)}, f32[4,24,128]{2,1,0:T(8,128)}) custom-call(s32[6]{0:T(128)S(1)} %stack.19.refs_0_, bf16[608,128]{1,0:T(8,128)(2,1)} %get-tuple-element.82.refs_1_, bf16[608,128]{1,0:T(8,128)(2,1)S(1)} %collective-permute-done.refs_2_, ...), custom_call_target="tpu_custom_call" | custom-call | tf_op jit(solution)/shard_map/pallas_call | solution.py:176
  18.7 2.8 %shard_map.290 = (f32[784,256]{1,0:T(8,128)S(1)}, bf16[784,256]{1,0:T(8,128)(2,1)S(1)}) custom-call(s32[6]{0:T(128)S(1)} %stack.19.refs_0_, bf16[784,512]{1,0:T(8,128)(2,1)S(1)} %collective-permute-done.3.refs_1_, bf16[512,512]{1,0:T(8,128)(2,1)} %get-tuple-element.87.refs_2_.refs_3_, bf16[2,784,512]{2,1,0:T(8,128)(2,1)} %bitcast.53), custom_call_target="tpu_custom_call" | custom-call | tf_op jit(solution)/shard_map/pallas_call | solution.py:176
  26.7 6.5 %collective-permute-done.4.refs_2_ = bf16[784,256]{1,0:T(8,128)(2,1)S(1)} collective-permute-done((bf16[784,256]{1,0:T(8,128)(2,1)S(1)}, bf16[784,256]{1,0:T(8,128)(2,1)S(1)}, u32[]{:S(2)}, u32[]{:S(2)}) %collective-permute-start.4) | collective-permute-done | bytes 401440 | tf_op jit(solution)/shard_map/ppermute | solution.py:860
  36.6 4.9 %all-to-all-start = ((f32[32,2,256]{2,1,0:T(2,128)}), f32[32,2,256]{2,1,0:T(2,128)S(1)}, u32[]{:S(2)}, u32[]{:S(2)}) async-start(f32[32,2,256]{2,1,0:T(2,128)} %get-tuple-element.92), calls=%async_computation | async-start | bytes 131072 | tf_op jit(solution)/shard_map/all_to_all | solution.py:885
  44.3 4.7 %all-to-all-done = f32[32,2,256]{2,1,0:T(2,128)S(1)} async-done(((f32[32,2,256]{2,1,0:T(2,128)}), f32[32,2,256]{2,1,0:T(2,128)S(1)}, u32[]{:S(2)}, u32[]{:S(2)}) %all-to-all-start) | async-done | bytes 65568 | tf_op jit(solution)/shard_map/all_to_all | solution.py:885
  49.6 5.5 %shard_map.292 = (f32[784,256]{1,0:T(8,128)}, bf16[784,256]{1,0:T(8,128)(2,1)}, f32[32,2,256]{2,1,0:T(2,128)}, bf16[784,512]{1,0:T(8,128)(2,1)}) custom-call(s32[6]{0:T(128)S(1)} %stack.19.refs_0_, f32[3]{0:T(128)S(1)} %pad_maximum_fusion.2.refs_1_, f32[784,256]{1,0:T(8,128)} %get-tuple-element.90.refs_2_.refs_8_.refs_4_, ...), custom_call_target="tpu_custom_call" | custom-call | tf_op jit(solution)/shard_map/pallas_call | solution.py:176
  55.6 11.9 %all_to_all.25 = f32[32,2,256]{2,1,0:T(2,128)} all-to-all(f32[32,2,256]{2,1,0:T(2,128)} %get-tuple-element.95.refs_2_), channel_id=1, replica_groups=mesh['clip'=8,'chan'=4] {'clip','chan'}, dimensions={0} | all-to-all | bytes 131072 | tf_op jit(solution)/shard_map/all_to_all | solution.py:885
  67.4 2.4 shard_map.293
  81.7 2.6 %collective-permute-start.12 = (f32[3,512]{1,0:T(4,128)S(1)}, f32[3,512]{1,0:T(4,128)S(1)}, u32[]{:S(2)}, u32[]{:S(2)}) collective-permute-start(f32[3,512]{1,0:T(4,128)S(1)} %add.91), channel_id=1, source_target_pairs={{0,16},{4,20},{8,24},{12,28},{16,0},{20,4},{24,8},{28,12},{1,17},{... | collective-permute-start | bytes 18440 | tf_op jit(solution)/shard_map/ppermute | solution.py:873
  86.2 3.5 %collective-permute-done.13 = f32[3,512]{1,0:T(4,128)S(1)} collective-permute-done((f32[3,512]{1,0:T(4,128)S(1)}, f32[3,512]{1,0:T(4,128)S(1)}, u32[]{:S(2)}, u32[]{:S(2)}) %collective-permute-start.13) | collective-permute-done | bytes 6176 | tf_op jit(solution)/shard_map/ppermute | solution.py:873
  90.3 5.2 %shard_map.296 = (bf16[2,784,512]{2,1,0:T(8,128)(2,1)}, f32[2,784,512]{2,1,0:T(8,128)S(1)}, f32[2,512]{1,0:T(2,128)S(1)}, f32[2,512]{1,0:T(2,128)S(1)}) custom-call(s32[6]{0:T(128)S(1)} %stack.19.refs_0_, f32[3]{0:T(128)S(1)} %pad_maximum_fusion.2.refs_1_, f32[3,512]{1,0:T(4,128)} %add_add_fusion.refs_2_, f32[1,512]{1,0:T(1,128)} %bitcast.78, ...), custom_call_target="tpu_custom_call" | custom-call | tf_op jit(solution)/shard_map/pallas_call | solution.py:176
  96.2 3.0 %collective-permute-done.14 = f32[2,512]{1,0:T(2,128)S(1)} collective-permute-done((f32[2,512]{1,0:T(2,128)S(1)}, f32[2,512]{1,0:T(2,128)S(1)}, u32[]{:S(2)}, u32[]{:S(2)}) %collective-permute-start.14) | collective-permute-done | bytes 4128 | tf_op jit(solution)/shard_map/ppermute | solution.py:873
  100.2 3.4 %collective-permute-start.17 = (f32[2,512]{1,0:T(2,128)S(1)}, f32[2,512]{1,0:T(2,128)S(1)}, u32[]{:S(2)}, u32[]{:S(2)}) collective-permute-start(f32[2,512]{1,0:T(2,128)S(1)} %add.95), channel_id=1, source_target_pairs={{0,24},{4,28},{8,16},{12,20},{16,8},{20,12},{24,0},{28,4},{1,25},{... | collective-permute-start | bytes 12296 | tf_op jit(solution)/shard_map/ppermute | solution.py:873
  113.1 3.2 %shard_map.301 = (bf16[448,512]{1,0:T(8,128)(2,1)}, bf16[448,512]{1,0:T(8,128)(2,1)}) custom-call(s32[6]{0:T(128)S(1)} %stack.19.refs_0_, bf16[784,256]{1,0:T(8,128)(2,1)S(1)} %get-tuple-element.96.refs_1_, bf16[784,256]{1,0:T(8,128)(2,1)S(1)} %shard_map.294.refs_2_, bf16[784,256]{1,0:T(8,128)(2,1)S(1)} %collective-permute-done.8.refs_3_, ...), custom_call_target="tpu_custom_call" | custom-call | tf_op jit(solution)/shard_map/pallas_call | solution.py:176
  117.7 5.5 %collective-permute-done.20.refs_4_ = bf16[784,256]{1,0:T(8,128)(2,1)S(1)} collective-permute-done((bf16[784,256]{1,0:T(8,128)(2,1)S(1)}, bf16[784,256]{1,0:T(8,128)(2,1)S(1)}, u32[]{:S(2)}, u32[]{:S(2)}) %collective-permute-start.20) | collective-permute-done | bytes 401440 | tf_op jit(solution)/shard_map/ppermute | solution.py:860
  123.1 4.9 %shard_map.302 = (f32[784,256]{1,0:T(8,128)}, bf16[784,256]{1,0:T(8,128)(2,1)}, f32[32,4,256]{2,1,0:T(4,128)}, f32[32,256]{1,0:T(8,128)}) custom-call(s32[6]{0:T(128)S(1)} %stack.19.refs_0_, f32[3]{0:T(128)S(1)} %pad_maximum_fusion.2.refs_1_, f32[784,256]{1,0:T(8,128)S(1)} %get-tuple-element.103.refs_2_, ...), custom_call_target="tpu_custom_call" | custom-call | tf_op jit(solution)/shard_map/pallas_call | solution.py:176
  129.5 3.8 %all-to-all-start.2 = ((f32[32,4,256]{2,1,0:T(4,128)}), f32[32,4,256]{2,1,0:T(4,128)S(1)}, u32[]{:S(2)}, u32[]{:S(2)}) async-start(f32[32,4,256]{2,1,0:T(4,128)} %get-tuple-element.112), calls=%async_computation.2 | async-start | bytes 262144 | tf_op jit(solution)/shard_map/all_to_all | solution.py:885
  135.5 6.0 %all-to-all-done.2 = f32[32,4,256]{2,1,0:T(4,128)S(1)} async-done(((f32[32,4,256]{2,1,0:T(4,128)}), f32[32,4,256]{2,1,0:T(4,128)S(1)}, u32[]{:S(2)}, u32[]{:S(2)}) %all-to-all-start.2) | async-done | bytes 131104 | tf_op jit(solution)/shard_map/all_to_all | solution.py:885
  143.2 7.0 %shard_map.304 = (f32[784,256]{1,0:T(8,128)}, bf16[784,256]{1,0:T(8,128)(2,1)}, f32[32,2,256]{2,1,0:T(2,128)}, bf16[928,128]{1,0:T(8,128)(2,1)}, bf16[928,128]{1,0:T(8,128)(2,1)}) custom-call(s32[6]{0:T(128)S(1)} %stack.19.refs_0_, f32[3]{0:T(128)S(1)} %pad_maximum_fusion.2.refs_1_, f32[784,256]{1,0:T(8,128)} %get-tuple-element.113.refs_2_, ...), custom_call_target="tpu_custom_call" | custom-call | tf_op jit(solution)/shard_map/pallas_call | solution.py:176
  150.9 2.4 collective-permute-start.28
  155.3 4.5 %all-to-all-start.3 = ((f32[32,2,256]{2,1,0:T(2,128)}), f32[32,2,256]{2,1,0:T(2,128)S(1)}, u32[]{:S(2)}, u32[]{:S(2)}) async-start(f32[32,2,256]{2,1,0:T(2,128)} %get-tuple-element.121), calls=%async_computation.3 | async-start | bytes 131072 | tf_op jit(solution)/shard_map/all_to_all | solution.py:885
  159.8 8.0 %shard_map.305 = (bf16[2368,128]{1,0:T(8,128)(2,1)}, bf16[2368,128]{1,0:T(8,128)(2,1)}) custom-call(s32[6]{0:T(128)S(1)} %stack.19.refs_0_, bf16[784,512]{1,0:T(8,128)(2,1)} %get-tuple-element.118.refs_1_, bf16[928,128]{1,0:T(8,128)(2,1)} %get-tuple-element.122.refs_2_, bf16[784,512]{1,0:T(8,128)(2,1)} %collective-permute-done.24.refs_16_.refs_3_, ...), custom_call_target="tpu_custom_call" | custom-call | flops 20000000000 | tf_op jit(solution)/shard_map/pallas_call | solution.py:176
  173.6 2.8 %shard_map.307 = (bf16[784,256]{1,0:T(8,128)(2,1)}, bf16[784,256]{1,0:T(8,128)(2,1)}) custom-call(s32[6]{0:T(128)S(1)} %stack.19.refs_0_, f32[3]{0:T(128)S(1)} %pad_maximum_fusion.2.refs_1_, f32[784,256]{1,0:T(8,128)} %get-tuple-element.119.refs_2_, bf16[784,256]{1,0:T(8,128)(2,1)} %collective-permute-done.25.refs_3_, ...), custom_call_target="tpu_custom_call" | custom-call | flops 49999998976 | tf_op jit(solution)/shard_map/pallas_call | solution.py:176
  178.4 2.4 collective-permute-start.38
  181.8 4.7 %shard_map.308 = (bf16[256,512]{1,0:T(8,128)(2,1)S(1)}, bf16[256,512]{1,0:T(8,128)(2,1)}) custom-call(s32[6]{0:T(128)S(1)} %stack.19.refs_0_, bf16[2,784,512]{2,1,0:T(8,128)(2,1)} %bitcast.56, bf16[784,256]{1,0:T(8,128)(2,1)} %get-tuple-element.128.refs_2_.refs_1_, bf16[784,256]{1,0:T(8,128)(2,1)} %get-tuple-element.129.refs_3_.refs_2_, ...), custom_call_target="tpu_custom_call" | custom-call | tf_op jit(solution)/shard_map/pallas_call | solution.py:176
  200.8 8.1 %collective-permute-done.35.refs_5_ = bf16[592,128]{1,0:T(8,128)(2,1)} collective-permute-done((bf16[592,128]{1,0:T(8,128)(2,1)}, bf16[592,128]{1,0:T(8,128)(2,1)}, u32[]{:S(2)}, u32[]{:S(2)}) %collective-permute-start.35) | collective-permute-done | bytes 151584 | tf_op jit(solution)/shard_map/ppermute | solution.py:873
  216.4 4.0 %shard_map.312.refs_6_ = f32[2,784,512]{2,1,0:T(8,128)} custom-call(s32[6]{0:T(128)S(1)} %stack.19.refs_0_, bf16[784,256]{1,0:T(8,128)(2,1)} %get-tuple-element.128.refs_2_.refs_1_, bf16[784,256]{1,0:T(8,128)(2,1)} %get-tuple-element.129.refs_3_.refs_2_, bf16[512,512]{1,0:T(8,128)(2,1)} %get-tuple-element.87.refs_2_.refs_3_, ...), custom_call_target="tpu_custom_call" | custom-call | tf_op jit(solution)/shard_map/pallas_call | solution.py:176
  220.5 10.5 %collective-permute-done.41.refs_3_ = bf16[848,128]{1,0:T(8,128)(2,1)S(1)} collective-permute-done((bf16[848,128]{1,0:T(8,128)(2,1)S(1)}, bf16[848,128]{1,0:T(8,128)(2,1)S(1)}, u32[]{:S(2)}, u32[]{:S(2)}) %collective-permute-start.41) | collective-permute-done | bytes 217120 | tf_op jit(solution)/shard_map/ppermute | solution.py:873
  234.6 6.3 %all-to-all-start.4 = ((bf16[32,64,128]{2,1,0:T(8,128)(2,1)}), bf16[32,64,128]{2,1,0:T(8,128)(2,1)S(1)}, u32[]{:S(2)}, u32[]{:S(2)}) async-start(bf16[32,64,128]{2,1,0:T(8,128)(2,1)} %get-tuple-element.141), calls=%async_computation.4 | async-start | bytes 1048576 | tf_op jit(solution)/shard_map/all_to_all | solution.py:1146
  240.9 2.5 shard_map.315
  248.0 8.4 %all-to-all-done.4 = bf16[32,64,128]{2,1,0:T(8,128)(2,1)S(1)} async-done(((bf16[32,64,128]{2,1,0:T(8,128)(2,1)}), bf16[32,64,128]{2,1,0:T(8,128)(2,1)S(1)}, u32[]{:S(2)}, u32[]{:S(2)}) %all-to-all-start.4) | async-done | bytes 524320 | tf_op jit(solution)/shard_map/all_to_all | solution.py:1146
  (181 shorter events, 98.7 us)
Async XLA Ops:
  0.7 22.7 %collective-permute-start.5 = (bf16[9,512,128]{2,1,0:T(8,128)(2,1)}, bf16[9,512,128]{2,1,0:T(8,128)(2,1)}, u32[]{:S(2)}, u32[]{:S(2)}) collective-permute-start(bf16[9,512,128]{2,1,0:T(8,128)(2,1)} %refs_1_.3), channel_id=1, source_target_pairs={{0,1},{1,0},{2,3},{3,2},{4,5},{5,4},{6,7},{7,6},{8,9},{9,8},{10,11... | collective-permute-start | bytes 3538952 | tf_op jit(solution)/shard_map/ppermute | solution.py:860
  3.2 8.0 %collective-permute-start.1 = (bf16[608,128]{1,0:T(8,128)(2,1)}, bf16[608,128]{1,0:T(8,128)(2,1)S(1)}, u32[]{:S(2)}, u32[]{:S(2)}) collective-permute-start(bf16[608,128]{1,0:T(8,128)(2,1)} %get-tuple-element.84), channel_id=1, source_target_pairs={{0,2},{1,3},{2,0},{3,1},{4,6},{5,7},{6,4},{7,5},{8,10},{9,11},{10,... | collective-permute-start | bytes 466952 | tf_op jit(solution)/shard_map/ppermute | solution.py:860
  21.5 11.6 %collective-permute-start.4 = (bf16[784,256]{1,0:T(8,128)(2,1)S(1)}, bf16[784,256]{1,0:T(8,128)(2,1)S(1)}, u32[]{:S(2)}, u32[]{:S(2)}) collective-permute-start(bf16[784,256]{1,0:T(8,128)(2,1)S(1)} %get-tuple-element.89), channel_id=1, source_target_pairs={{0,2},{1,3},{2,0},{3,1},{4,6},{5,7},{6,4},{7,5},{8,10},{9,11},{10,... | collective-permute-start | bytes 1204232 | tf_op jit(solution)/shard_map/ppermute | solution.py:860
  34.9 14.1 %collective-permute-start.6 = (bf16[784,256]{1,0:T(8,128)(2,1)}, bf16[784,256]{1,0:T(8,128)(2,1)S(1)}, u32[]{:S(2)}, u32[]{:S(2)}) collective-permute-start(bf16[784,256]{1,0:T(8,128)(2,1)} %get-tuple-element.91), channel_id=1, source_target_pairs={{0,2},{1,3},{2,0},{3,1},{4,6},{5,7},{6,4},{7,5},{8,10},{9,11},{10,... | collective-permute-start | bytes 1204232 | tf_op jit(solution)/shard_map/ppermute | solution.py:860
  36.6 12.3 %all-to-all-start = ((f32[32,2,256]{2,1,0:T(2,128)}), f32[32,2,256]{2,1,0:T(2,128)S(1)}, u32[]{:S(2)}, u32[]{:S(2)}) async-start(f32[32,2,256]{2,1,0:T(2,128)} %get-tuple-element.92), calls=%async_computation | async-start | bytes 131072 | tf_op jit(solution)/shard_map/all_to_all | solution.py:885
  55.1 15.0 %collective-permute-start.7 = (bf16[784,256]{1,0:T(8,128)(2,1)}, bf16[784,256]{1,0:T(8,128)(2,1)S(1)}, u32[]{:S(2)}, u32[]{:S(2)}) collective-permute-start(bf16[784,256]{1,0:T(8,128)(2,1)} %get-tuple-element.97), channel_id=1, source_target_pairs={{0,2},{1,3},{2,0},{3,1},{4,6},{5,7},{6,4},{7,5},{8,10},{9,11},{10,... | collective-permute-start | bytes 1204232 | tf_op jit(solution)/shard_map/ppermute | solution.py:860
  79.7 26.5 %collective-permute-start.18 = (bf16[9,256,128]{2,1,0:T(8,128)(2,1)}, bf16[9,256,128]{2,1,0:T(8,128)(2,1)}, u32[]{:S(2)}, u32[]{:S(2)}) collective-permute-start(bf16[9,256,128]{2,1,0:T(8,128)(2,1)} %shard_map.297), channel_id=1, source_target_pairs={{0,2},{1,3},{2,0},{3,1},{4,6},{5,7},{6,4},{7,5},{8,10},{9,11},{10,... | collective-permute-start | bytes 1769480 | tf_op jit(solution)/shard_map/ppermute | solution.py:860
  108.0 27.5 %collective-permute-start.24 = (bf16[784,512]{1,0:T(8,128)(2,1)}, bf16[784,512]{1,0:T(8,128)(2,1)}, u32[]{:S(2)}, u32[]{:S(2)}) collective-permute-start(bf16[784,512]{1,0:T(8,128)(2,1)} %get-tuple-element.118.refs_1_), channel_id=1, source_target_pairs={{0,1},{1,0},{2,3},{3,2},{4,5},{5,4},{6,7},{7,6},{8,9},{9,8},{10,11... | collective-permute-start | bytes 2408456 | tf_op jit(solution)/shard_map/ppermute | solution.py:860
  108.5 27.0 %collective-permute-start.22 = (bf16[9,256,128]{2,1,0:T(8,128)(2,1)}, bf16[9,256,128]{2,1,0:T(8,128)(2,1)}, u32[]{:S(2)}, u32[]{:S(2)}) collective-permute-start(bf16[9,256,128]{2,1,0:T(8,128)(2,1)} %collective-permute-done.18.refs_8_.refs_12_), channel_id=1, source_target_pairs={{0,1},{1,0},{2,3},{3,2},{4,5},{5,4},{6,7},{7,6},{8,9},{9,8},{10,11... | collective-permute-start | bytes 1769480 | tf_op jit(solution)/shard_map/ppermute | solution.py:860
  111.4 11.7 %collective-permute-start.20 = (bf16[784,256]{1,0:T(8,128)(2,1)S(1)}, bf16[784,256]{1,0:T(8,128)(2,1)S(1)}, u32[]{:S(2)}, u32[]{:S(2)}) collective-permute-start(bf16[784,256]{1,0:T(8,128)(2,1)S(1)} %shard_map.300), channel_id=1, source_target_pairs={{0,2},{1,3},{2,0},{3,1},{4,6},{5,7},{6,4},{7,5},{8,10},{9,11},{10,... | collective-permute-start | bytes 1204232 | tf_op jit(solution)/shard_map/ppermute | solution.py:860
  116.4 16.9 %collective-permute-start.23 = (bf16[448,512]{1,0:T(8,128)(2,1)}, bf16[448,512]{1,0:T(8,128)(2,1)}, u32[]{:S(2)}, u32[]{:S(2)}) collective-permute-start(bf16[448,512]{1,0:T(8,128)(2,1)} %get-tuple-element.111.refs_11_), channel_id=1, source_target_pairs={{0,4},{4,0},{8,12},{12,8},{16,20},{20,16},{24,28},{28,24},{1,5},{5... | collective-permute-start | bytes 1376264 | tf_op jit(solution)/shard_map/ppermute | solution.py:873
  128.0 13.5 %collective-permute-start.21 = (bf16[784,256]{1,0:T(8,128)(2,1)}, bf16[784,256]{1,0:T(8,128)(2,1)}, u32[]{:S(2)}, u32[]{:S(2)}) collective-permute-start(bf16[784,256]{1,0:T(8,128)(2,1)} %get-tuple-element.114), channel_id=1, source_target_pairs={{0,2},{1,3},{2,0},{3,1},{4,6},{5,7},{6,4},{7,5},{8,10},{9,11},{10,... | collective-permute-start | bytes 1204232 | tf_op jit(solution)/shard_map/ppermute | solution.py:860
  129.5 12.0 %all-to-all-start.2 = ((f32[32,4,256]{2,1,0:T(4,128)}), f32[32,4,256]{2,1,0:T(4,128)S(1)}, u32[]{:S(2)}, u32[]{:S(2)}) async-start(f32[32,4,256]{2,1,0:T(4,128)} %get-tuple-element.112), calls=%async_computation.2 | async-start | bytes 262144 | tf_op jit(solution)/shard_map/all_to_all | solution.py:885
  150.2 9.6 %collective-permute-start.26 = (bf16[928,128]{1,0:T(8,128)(2,1)}, bf16[928,128]{1,0:T(8,128)(2,1)}, u32[]{:S(2)}, u32[]{:S(2)}) collective-permute-start(bf16[928,128]{1,0:T(8,128)(2,1)} %get-tuple-element.123), channel_id=1, source_target_pairs={{0,1},{1,0},{2,3},{3,2},{4,5},{5,4},{6,7},{7,6},{8,9},{9,8},{10,11... | collective-permute-start | bytes 712712 | tf_op jit(solution)/shard_map/ppermute | solution.py:860
  150.4 19.1 %collective-permute-start.27 = (bf16[112,512]{1,0:T(8,128)(2,1)}, bf16[112,512]{1,0:T(8,128)(2,1)S(1)}, u32[]{:S(2)}, u32[]{:S(2)}) collective-permute-start(bf16[112,512]{1,0:T(8,128)(2,1)} %get-tuple-element.125), channel_id=1, source_target_pairs={{0,8},{4,12},{8,0},{12,4},{16,24},{20,28},{24,16},{28,20},{1,9},{5... | collective-permute-start | bytes 344072 | tf_op jit(solution)/shard_map/ppermute | solution.py:873
  150.9 18.6 %collective-permute-start.28 = (bf16[112,512]{1,0:T(8,128)(2,1)}, bf16[112,512]{1,0:T(8,128)(2,1)S(1)}, u32[]{:S(2)}, u32[]{:S(2)}) collective-permute-start(bf16[112,512]{1,0:T(8,128)(2,1)} %get-tuple-element.126), channel_id=1, source_target_pairs={{0,16},{4,20},{8,24},{12,28},{16,0},{20,4},{24,8},{28,12},{1,17},{... | collective-permute-start | bytes 344072 | tf_op jit(solution)/shard_map/ppermute | solution.py:873
  153.4 16.2 %collective-permute-start.29 = (bf16[112,512]{1,0:T(8,128)(2,1)}, bf16[112,512]{1,0:T(8,128)(2,1)}, u32[]{:S(2)}, u32[]{:S(2)}) collective-permute-start(bf16[112,512]{1,0:T(8,128)(2,1)} %get-tuple-element.127), channel_id=1, source_target_pairs={{0,24},{4,28},{8,16},{12,20},{16,8},{20,12},{24,0},{28,4},{1,25},{... | collective-permute-start | bytes 344072 | tf_op jit(solution)/shard_map/ppermute | solution.py:873
  154.8 17.2 %collective-permute-start.25 = (bf16[784,256]{1,0:T(8,128)(2,1)}, bf16[784,256]{1,0:T(8,128)(2,1)}, u32[]{:S(2)}, u32[]{:S(2)}) collective-permute-start(bf16[784,256]{1,0:T(8,128)(2,1)} %get-tuple-element.120), channel_id=1, source_target_pairs={{0,2},{1,3},{2,0},{3,1},{4,6},{5,7},{6,4},{7,5},{8,10},{9,11},{10,... | collective-permute-start | bytes 1204232 | tf_op jit(solution)/shard_map/ppermute | solution.py:860
  155.3 16.8 %all-to-all-start.3 = ((f32[32,2,256]{2,1,0:T(2,128)}), f32[32,2,256]{2,1,0:T(2,128)S(1)}, u32[]{:S(2)}, u32[]{:S(2)}) async-start(f32[32,2,256]{2,1,0:T(2,128)} %get-tuple-element.121), calls=%async_computation.3 | async-start | bytes 131072 | tf_op jit(solution)/shard_map/all_to_all | solution.py:885
  167.8 20.0 %collective-permute-start.33 = (bf16[2368,128]{1,0:T(8,128)(2,1)}, bf16[2368,128]{1,0:T(8,128)(2,1)}, u32[]{:S(2)}, u32[]{:S(2)}) collective-permute-start(bf16[2368,128]{1,0:T(8,128)(2,1)} %get-tuple-element.124.refs_4_.refs_9_), channel_id=1, source_target_pairs={{0,4},{4,0},{8,12},{12,8},{16,20},{20,16},{24,28},{28,24},{1,5},{5... | collective-permute-start | bytes 1818632 | tf_op jit(solution)/shard_map/ppermute | solution.py:873
  177.0 12.4 %collective-permute-start.37 = (bf16[112,512]{1,0:T(8,128)(2,1)S(1)}, bf16[112,512]{1,0:T(8,128)(2,1)S(1)}, u32[]{:S(2)}, u32[]{:S(2)}) collective-permute-start(bf16[112,512]{1,0:T(8,128)(2,1)S(1)} %copy-done.8), channel_id=1, source_target_pairs={{0,8},{4,12},{8,0},{12,4},{16,24},{20,28},{24,16},{28,20},{1,9},{5... | collective-permute-start | bytes 344072 | tf_op jit(solution)/shard_map/ppermute | solution.py:873
  178.4 11.9 %collective-permute-start.38 = (bf16[112,512]{1,0:T(8,128)(2,1)S(1)}, bf16[112,512]{1,0:T(8,128)(2,1)S(1)}, u32[]{:S(2)}, u32[]{:S(2)}) collective-permute-start(bf16[112,512]{1,0:T(8,128)(2,1)S(1)} %copy-done.8), channel_id=1, source_target_pairs={{0,16},{4,20},{8,24},{12,28},{16,0},{20,4},{24,8},{28,12},{1,17},{... | collective-permute-start | bytes 344072 | tf_op jit(solution)/shard_map/ppermute | solution.py:873
  180.9 9.4 %collective-permute-start.39 = (bf16[112,512]{1,0:T(8,128)(2,1)S(1)}, bf16[112,512]{1,0:T(8,128)(2,1)S(1)}, u32[]{:S(2)}, u32[]{:S(2)}) collective-permute-start(bf16[112,512]{1,0:T(8,128)(2,1)S(1)} %copy-done.8), channel_id=1, source_target_pairs={{0,24},{4,28},{8,16},{12,20},{16,8},{20,12},{24,0},{28,4},{1,25},{... | collective-permute-start | bytes 344072 | tf_op jit(solution)/shard_map/ppermute | solution.py:873
  187.2 21.6 %collective-permute-start.32 = (bf16[256,512]{1,0:T(8,128)(2,1)}, bf16[256,512]{1,0:T(8,128)(2,1)}, u32[]{:S(2)}, u32[]{:S(2)}) collective-permute-start(bf16[256,512]{1,0:T(8,128)(2,1)} %get-tuple-element.131.refs_3_), channel_id=1, source_target_pairs={{0,4},{4,0},{8,12},{12,8},{16,20},{20,16},{24,28},{28,24},{1,5},{5... | collective-permute-start | bytes 786440 | tf_op jit(solution)/shard_map/ppermute | solution.py:873
  191.7 39.3 %collective-permute-start.43 = (bf16[448,512]{1,0:T(8,128)(2,1)}, bf16[448,512]{1,0:T(8,128)(2,1)}, u32[]{:S(2)}, u32[]{:S(2)}) collective-permute-start(bf16[448,512]{1,0:T(8,128)(2,1)} %shard_map.310.refs_7_.refs_1_), channel_id=1, source_target_pairs={{0,4},{4,0},{8,12},{12,8},{16,20},{20,16},{24,28},{28,24},{1,5},{5... | collective-permute-start | bytes 1376264 | tf_op jit(solution)/shard_map/ppermute | solution.py:873
  195.3 13.5 %collective-permute-start.35 = (bf16[592,128]{1,0:T(8,128)(2,1)}, bf16[592,128]{1,0:T(8,128)(2,1)}, u32[]{:S(2)}, u32[]{:S(2)}) collective-permute-start(bf16[592,128]{1,0:T(8,128)(2,1)} %copy-done.14), channel_id=1, source_target_pairs={{0,16},{4,20},{8,24},{12,28},{16,0},{20,4},{24,8},{28,12},{1,17},{... | collective-permute-start | bytes 454664 | tf_op jit(solution)/shard_map/ppermute | solution.py:873
  197.1 11.7 %collective-permute-start.36 = (bf16[592,128]{1,0:T(8,128)(2,1)}, bf16[592,128]{1,0:T(8,128)(2,1)}, u32[]{:S(2)}, u32[]{:S(2)}) collective-permute-start(bf16[592,128]{1,0:T(8,128)(2,1)} %copy-done.13), channel_id=1, source_target_pairs={{0,24},{4,28},{8,16},{12,20},{16,8},{20,12},{24,0},{28,4},{1,25},{... | collective-permute-start | bytes 454664 | tf_op jit(solution)/shard_map/ppermute | solution.py:873
  211.1 9.3 %collective-permute-start.40 = (bf16[848,128]{1,0:T(8,128)(2,1)S(1)}, bf16[848,128]{1,0:T(8,128)(2,1)S(1)}, u32[]{:S(2)}, u32[]{:S(2)}) collective-permute-start(bf16[848,128]{1,0:T(8,128)(2,1)S(1)} %get-tuple-element.138), channel_id=1, source_target_pairs={{0,8},{4,12},{8,0},{12,4},{16,24},{20,28},{24,16},{28,20},{1,9},{5... | collective-permute-start | bytes 651272 | tf_op jit(solution)/shard_map/ppermute | solution.py:873
  213.4 17.6 %collective-permute-start.41 = (bf16[848,128]{1,0:T(8,128)(2,1)S(1)}, bf16[848,128]{1,0:T(8,128)(2,1)S(1)}, u32[]{:S(2)}, u32[]{:S(2)}) collective-permute-start(bf16[848,128]{1,0:T(8,128)(2,1)S(1)} %get-tuple-element.139), channel_id=1, source_target_pairs={{0,16},{4,20},{8,24},{12,28},{16,0},{20,4},{24,8},{28,12},{1,17},{... | collective-permute-start | bytes 651272 | tf_op jit(solution)/shard_map/ppermute | solution.py:873
  214.4 16.6 %collective-permute-start.42 = (bf16[848,128]{1,0:T(8,128)(2,1)S(1)}, bf16[848,128]{1,0:T(8,128)(2,1)S(1)}, u32[]{:S(2)}, u32[]{:S(2)}) collective-permute-start(bf16[848,128]{1,0:T(8,128)(2,1)S(1)} %get-tuple-element.140), channel_id=1, source_target_pairs={{0,24},{4,28},{8,16},{12,20},{16,8},{20,12},{24,0},{28,4},{1,25},{... | collective-permute-start | bytes 651272 | tf_op jit(solution)/shard_map/ppermute | solution.py:873
  232.5 13.4 %collective-permute-start.44 = (bf16[2368,128]{1,0:T(8,128)(2,1)S(1)}, bf16[2368,128]{1,0:T(8,128)(2,1)S(1)}, u32[]{:S(2)}, u32[]{:S(2)}) collective-permute-start(bf16[2368,128]{1,0:T(8,128)(2,1)S(1)} %get-tuple-element.142.refs_1_.refs_3_), channel_id=1, source_target_pairs={{0,4},{4,0},{8,12},{12,8},{16,20},{20,16},{24,28},{28,24},{1,5},{5... | collective-permute-start | bytes 1818632 | tf_op jit(solution)/shard_map/ppermute | solution.py:873
  234.6 21.8 %all-to-all-start.4 = ((bf16[32,64,128]{2,1,0:T(8,128)(2,1)}), bf16[32,64,128]{2,1,0:T(8,128)(2,1)S(1)}, u32[]{:S(2)}, u32[]{:S(2)}) async-start(bf16[32,64,128]{2,1,0:T(8,128)(2,1)} %get-tuple-element.141), calls=%async_computation.4 | async-start | bytes 1048576 | tf_op jit(solution)/shard_map/all_to_all | solution.py:1146
  (44 other events, 325.6 us)

commit v3 on v2

--- a/solution.py
+++ b/solution.py
@@ -13,6 +13,7 @@
 EPSILON = 1e-05
 LANES = 128
 F32 = jnp.float32
+WORK = {"taps_gradient": 20, "unpack_spatial": 20, "last_norm": 1, "stage_two": 50}
 BF16 = jnp.bfloat16
 VMEM_BYTES = 20 * 1024 * 1024
 
@@ -102,7 +103,7 @@
     return pltpu.VMEM(shape, kind)
 
 
-def call(body, out_shape, scratch=(), deps=(), ints=None, floats=None, work=0, room=VMEM_BYTES):
+def call(body, out_shape, scratch=(), deps=(), ints=None, floats=None, room=VMEM_BYTES):
     single = not isinstance(out_shape, (tuple, list))
     shapes = (out_shape,) if single else tuple(out_shape)
     early = [isinstance(out, Early) for out in shapes]
@@ -113,6 +114,8 @@
         for out, far, free in zip(shapes, away, loose)
     )
     scalars = [array for array in (ints, floats) if array is not None]
+    name = getattr(body, "func", body).__name__
+    work = WORK.get(name, 0)
 
     def bare(arg):
         while isinstance(arg, (Pick, Free, Near, Late)):
@@ -171,7 +174,7 @@
                     for copy in result.copies:
                         copy.wait()
 
-        kernel.__name__ = getattr(body, "func", body).__name__
+        kernel.__name__ = name
         anywhere = pl.BlockSpec(memory_space=pl.ANY)
         results = pl.pallas_call(
             kernel,
@@ -182,7 +185,7 @@
             out_specs=[anywhere if parts else VMEM for parts in early],
             scratch_shapes=buffers + list(scratch),
             compiler_params=pltpu.CompilerParams(vmem_limit_bytes=room),
-            cost_estimate=pl.CostEstimate(flops=work, bytes_accessed=0, transcendentals=0) if work else None,
+            cost_estimate=pl.CostEstimate(flops=work * 1_000_000_000, bytes_accessed=0, transcendentals=0) if work else None,
         )(*scalars, *[placed(arg) for arg in args], *[placed(dep) for dep in deps])
         results = tuple(
             result if far else Free(result) if free else Near(result)
@@ -206,6 +209,17 @@
 
 def line_sums(values, row_of):
     return jnp.sum(values.reshape(-1, 8, values.shape[1]), axis=0) + row_of
+
+
+def clear_taps(cat_ref, seg_count):
+    depth = cat_ref.shape[1] // 3
+    for tap in range(3):
+        lanes = slice(tap * depth, (tap + 1) * depth)
+        spans = [(0, WIDE + 1 - tap), (SIDE * WIDE + WIDE - tap, cat_ref.shape[0] // seg_count)]
+        spans += [((line + 1) * WIDE + WIDE - tap, (line + 1) * WIDE + WIDE + 1 - tap) for line in range(SIDE - 1)]
+        for first, last in spans:
+            rows = (last - first) * seg_count
+            cat_ref[first * seg_count : last * seg_count, lanes] = jnp.zeros((rows, depth), cat_ref.dtype)
 
 
 def send_sums(sent_ref, total, cross):
@@ -256,17 +270,20 @@
             ref[size + 32 * index : size + 32 * (index + 1), :] = piece
 
 
-def reduce_other(ints_ref, own_ref, near_ref, far_ref, cross_ref, x_ref, part_ref, w_ref, small_ref):
+def reduce_side(ints_ref, first_ref, second_ref, x_oth_ref, x_own_ref, oth_ref, own_ref, w_ref, *small_refs):
     core = ints_ref[3]
-    rows, size = w_ref.shape[0], own_ref.shape[1]
-    blocks = (own_ref, near_ref, far_ref, cross_ref)
-    for bits, ref in enumerate(blocks):
-        start = pl.multiple_of((2 * (bits // 2) + (core ^ (bits % 2))) * size, size)
-        w_ref[:, pl.ds(start, size)] = ref[:rows, :]
-    for bits, ref in enumerate(blocks):
-        pieces = [ref[rows + 32 * index : rows + 32 * (index + 1), :].astype(F32) for index in range(3)]
-        small_ref[(2 * ints_ref[1] + core) ^ bits] = (pieces[0] + (pieces[1] + pieces[2]))[:24]
-    part_ref[...] = dot32(x_ref[...], w_ref[...]).astype(BF16)
+    rows, size = w_ref.shape[0], first_ref.shape[1]
+    for index, ref in ((core, first_ref), (1 - core, second_ref)):
+        w_ref[:, pl.ds(pl.multiple_of(index * size, size), size)] = ref[:rows, :]
+        for small_ref in small_refs:
+            pieces = [ref[rows + 32 * piece : rows + 32 * (piece + 1), :].astype(F32) for piece in range(3)]
+            small_ref[index] = (pieces[0] + (pieces[1] + pieces[2]))[:24]
+    oth_ref[...] = dot32(x_oth_ref[...], w_ref[...]).astype(BF16)
+    own_ref[...] = dot32(x_own_ref[...], w_ref[...])
+
+
+def add_near(own_ref, near_ref, out_ref):
+    out_ref[...] = (own_ref[...] + near_ref[...].astype(F32)).astype(BF16)
 
 
 def add_low(near_ref, far_ref, out_ref):
@@ -274,25 +291,17 @@
     out_ref[...] = (far_ref[...] + near_ref[:, half:].astype(F32)).astype(BF16)
 
 
-def small_row(small_ref, side, row):
-    return jnp.concatenate([small_ref[2 * side + core, row : row + 1, :] for core in range(2)], axis=1)
-
-
-def reduce_own(ints_ref, near_ref, w_ref, x_ref, part_ref, send_ref):
-    half = w_ref.shape[1] // 2
-    send = dot32(x_ref[...], w_ref[:, half:]) + near_ref[:, half:].astype(F32)
-    send_ref[...] = send.astype(BF16)
-    part_ref[...] = dot32(x_ref[...], w_ref[:, :half]) + near_ref[:, :half].astype(F32)
-
-
-def first_sums(seg_count, ints_ref, part_ref, far_ref, act_ref, low_ref, sent_ref):
+def small_row(small_ref, row):
+    return jnp.concatenate([small_ref[core, row : row + 1, :] for core in range(2)], axis=1)
+
+
+def first_sums(seg_count, ints_ref, part_ref, near_ref, far_ref, low_ref, sent_ref):
     line_rows = SIDE * seg_count
     mask = line_mask(line_rows, seg_count, ints_ref[0])
-    total = cross = jnp.zeros((8, act_ref.shape[1]), F32)
+    total = cross = jnp.zeros((8, low_ref.shape[1]), F32)
     for line in range(SIDE):
         rows = slice(line * line_rows, (line + 1) * line_rows)
-        act = part_ref[rows, :] + far_ref[rows, :].astype(F32)
-        act_ref[rows, :] = act
+        act = part_ref[rows, :] + near_ref[rows, :].astype(F32) + far_ref[rows, :].astype(F32)
         low_ref[rows, :] = act.astype(BF16)
         kept = act * mask
         total = line_sums(kept, total)
@@ -301,21 +310,21 @@
 
 
 def conv_forward(
-    seg_count, ints_ref, floats_ref, own_ref, oth_ref, got_ref, small_ref, w_ref,
-    act_ref, low_ref, sent_ref, hid_ref, cat_ref, acc_ref,
+    seg_count, ints_ref, floats_ref, own_ref, oth_ref, got_ref, small_own_ref, small_oth_ref, w_ref,
+    low_ref, sent_ref, hid_ref, cat_ref, acc_ref,
 ):
     line_rows = SIDE * seg_count
     half = own_ref.shape[1]
     side = ints_ref[1]
-    cat_ref[...] = jnp.zeros_like(cat_ref)
+    clear_taps(cat_ref, seg_count)
     own, oth = [
-        norm_rows(side_sums(got_ref, index), small_row(small_ref, index, 0), small_row(small_ref, index, 1), floats_ref[0])
-        for index in (side, 1 - side)
+        norm_rows(side_sums(got_ref, index), small_row(small_ref, 0), small_row(small_ref, 1), floats_ref[0])
+        for index, small_ref in ((side, small_own_ref), (1 - side, small_oth_ref))
     ]
     average, scale, shift, _ = [jnp.concatenate(pieces, axis=1) for pieces in zip(own, oth)]
     for line in range(SIDE):
         rows = slice(line * line_rows, (line + 1) * line_rows)
-        act = jnp.concatenate([own_ref[rows, :], oth_ref[rows, :].astype(F32)], axis=1)
+        act = jnp.concatenate([own_ref[rows, :], oth_ref[rows, :]], axis=1).astype(F32)
         pre = (act - average) * scale + shift
         hid = (pre * jax.nn.sigmoid(pre)).astype(BF16)
         hid_ref[rows, :] = hid
@@ -333,7 +342,6 @@
     for line in range(SIDE):
         rows = slice(line * line_rows, (line + 1) * line_rows)
         act = acc_ref[line * step : line * step + line_rows, :]
-        act_ref[rows, :] = act
         low_ref[rows, :] = act.astype(BF16)
         kept = act * mask
         total = line_sums(kept, total)
@@ -376,7 +384,7 @@
     follows = next_mask(line_rows, seg_count, ints_ref[0])
     for core in range(act_ref.shape[1] // LANES):
         lanes = slice(core * LANES, (core + 1) * LANES)
-        rows_for = small_ref.at[2 * side + core]
+        rows_for = small_ref.at[core]
         average, scale, shift, _ = norm_rows(sums[:, lanes], rows_for[2:3, :], rows_for[3:4, :], floats_ref[0])
         for line in range(SIDE):
             rows = slice(line * line_rows, (line + 1) * line_rows)
@@ -445,13 +453,14 @@
             resid = x_ref[rows, :].astype(F32) + gain * normed + shift
             logistic = jax.nn.sigmoid(resid)
             output = mask * resid * logistic
-            out_ref[place, rows, :] = output.astype(BF16)
+            out_ref[clip, rows, :] = output.astype(BF16)
             pool = line_sums(output, pool)
             grad = (grad_ref[rows, :].astype(F32) + flat) * mask
             grad = grad * (logistic * (1.0 + resid * (1.0 - logistic)))
             resid_ref[clip, rows, :] = grad
             total = line_sums(grad, total)
             cross = line_sums(grad * normed, cross)
+        out_ref.leave(clip, place)
         pooled_ref[clip : clip + 1, :] = jnp.sum(pool, axis=0, keepdims=True) * floats_ref[1 + clip]
     send_sums(sent_ref, total, cross)
 
@@ -482,7 +491,7 @@
 
 def gate_backward(
     seg_count, ints_ref, floats_ref, grad_ref, near_ref, far_ref, hid_ref, gate_ref, act_ref, got_ref, small_ref,
-    logit_ref, slope_ref, low_ref, sent_ref, kern_grad_ref, field_ref, pad_ref, back_ref,
+    logit_ref, low_ref, sent_ref, kern_grad_ref, field_ref, pad_ref, back_ref,
 ):
     line_rows = SIDE * seg_count
     pad_ref[...] = jnp.zeros_like(pad_ref)
@@ -495,7 +504,7 @@
     totals_all, cross_all = [], []
     for core in range(act_ref.shape[1] // LANES):
         lanes = slice(core * LANES, (core + 1) * LANES)
-        rows_for = small_ref.at[2 * side + core]
+        rows_for = small_ref.at[core]
         average, scale, shift, inv_std = norm_rows(sums[:, lanes], rows_for[2:3, :], rows_for[3:4, :], floats_ref[0])
 
         def whole_grad(rows):
@@ -533,9 +542,8 @@
             before = back_ref[first + 7 : first + 7 + line_rows, :]
             here = back_ref[first + 8 : first + 8 + line_rows, :]
             grad = whole_grad(rows) * (1.0 + gate_ref[rows, lanes]) + before - here
-            centred = act_ref[rows, lanes] - average
+            centred = act_ref[rows, lanes].astype(F32) - average
             grad = grad * silu_slope(centred * scale + shift)
-            slope_ref[rows, lanes] = grad
             low_ref[rows, lanes] = grad.astype(BF16)
             total = line_sums(grad, total)
             cross = line_sums(grad * (centred * inv_std), cross)
@@ -548,7 +556,7 @@
 
 def back_rows(got_ref, back_ref, small_ref, row, side, count):
     average, scale, shift, inv_std = norm_rows(
-        side_sums(got_ref, side), small_row(small_ref, side, row), small_row(small_ref, side, row + 1), count
+        side_sums(got_ref, side), small_row(small_ref, row), small_row(small_ref, row + 1), count
     )
     back = side_sums(back_ref, side) / count
     return average, inv_std, scale, back[0:1, :], back[1:2, :], shift
@@ -556,9 +564,9 @@
 
 def conv_backward(
     seg_count, ints_ref, floats_ref, grad_ref, more_ref, act_ref, oth_ref, got_ref, back_ref, first_ref, got_one_ref,
-    small_ref, w_ref, from_ref, pair_ref, kern_grad_ref, slope_ref, low_ref, sent_ref, keep_ref, send_ref,
-    field_ref, cat_ref, acc_ref, w_all_ref,
-):
+    small_own_ref, small_oth_ref, w_ref, kern_grad_ref, low_ref, sent_ref, keep_ref, *rest,
+):
+    send_refs, (field_ref, cat_ref, acc_ref) = rest[:-3], rest[-3:]
     line_rows = SIDE * seg_count
     half = grad_ref.shape[1]
     step = WIDE * seg_count
@@ -566,50 +574,48 @@
     side = ints_ref[1]
     count = floats_ref[0]
     mask = line_mask(line_rows, seg_count, ints_ref[0])
-    cat_ref[...] = jnp.zeros_like(cat_ref)
+    clear_taps(cat_ref, seg_count)
     field_ref[...] = jnp.zeros_like(field_ref)
-    own = back_rows(got_ref, back_ref, small_ref, 2, side, count)
-    oth = back_rows(got_ref, back_ref, small_ref, 2, 1 - side, count)
+    own = back_rows(got_ref, back_ref, small_own_ref, 2, side, count)
+    oth = back_rows(got_ref, back_ref, small_oth_ref, 2, 1 - side, count)
     average, inv_std, scale, mean, mix, _ = [jnp.concatenate(pieces, axis=1) for pieces in zip(own, oth)]
     for line in range(SIDE):
         rows = slice(line * line_rows, (line + 1) * line_rows)
-        act = jnp.concatenate([act_ref[rows, :], oth_ref[rows, :].astype(F32)], axis=1)
-        grad = jnp.concatenate([grad_ref[rows, :], more_ref[rows, :].astype(F32)], axis=1)
+        act = jnp.concatenate([act_ref[rows, :], oth_ref[rows, :]], axis=1).astype(F32)
+        grad = jnp.concatenate([grad_ref[rows, :], more_ref[rows, :]], axis=1).astype(F32)
         normed = (act - average) * inv_std
         low = (scale * (grad - mask * (mean + normed * mix))).astype(BF16)
         store_taps(cat_ref, line, low, line_rows, seg_count)
         field_ref[line * step : line * step + line_rows, :] = low[:, :half]
+    size = half // 2
     core = ints_ref[3]
-    size = half // 2
-    depth = 2 * half
-    for index, ref in ((core, keep_ref), (1 - core, send_ref)):
-        lanes = pl.ds(pl.multiple_of(index * size, size), size)
-        ref[:span, :] = field_ref[:, lanes]
-        ref[span:, :] = kern_grad_ref[:, lanes].astype(BF16)
-    for tap in range(9):
-        w_all_ref[tap, :, :half] = w_ref[tap // 3, (tap % 3) * depth : (tap % 3) * depth + half, :]
-        for index, ref in ((core, from_ref), (1 - core, pair_ref)):
-            w_all_ref[tap, :, pl.ds(pl.multiple_of(half + index * size, size), size)] = ref[tap]
+    keep_lanes, send_lanes = [pl.ds(pl.multiple_of(index * size, size), size) for index in (core, 1 - core)]
+    keep_ref[:span, :] = field_ref[:, keep_lanes]
+    keep_ref[span:, :] = kern_grad_ref[:, keep_lanes].astype(BF16)
+    start = 0
+    for ref in send_refs:
+        rows = ref.shape[0]
+        if start + rows <= span:
+            ref[...] = field_ref[start : start + rows, send_lanes]
+        else:
+            ref[: span - start, :] = field_ref[start:, send_lanes]
+            ref[span - start :, :] = kern_grad_ref[:, send_lanes].astype(BF16)
+        start += rows
     for row_off in range(3):
-        rows = slice(row_off * step, row_off * step + span)
-        part = sum(
-            dot32(cat_ref[rows, tap * depth : (tap + 1) * depth], w_all_ref[8 - 3 * row_off - tap], ((1,), (1,)))
-            for tap in range(3)
-        )
+        part = dot32(cat_ref[row_off * step : row_off * step + span, :], w_ref[row_off])
         if row_off == 0:
             acc_ref[...] = part
         else:
             acc_ref[...] += part
     average, scale, shift, inv_std = norm_rows(
-        side_sums(got_one_ref, side), small_row(small_ref, side, 0), small_row(small_ref, side, 1), count
+        side_sums(got_one_ref, side), small_row(small_own_ref, 0), small_row(small_own_ref, 1), count
     )
     total = cross = jnp.zeros((8, half), F32)
     for line in range(SIDE):
         rows = slice(line * line_rows, (line + 1) * line_rows)
-        centred = first_ref[rows, :] - average
+        centred = first_ref[rows, :].astype(F32) - average
         grad = acc_ref[line * step : line * step + line_rows, :]
         grad = grad * silu_slope(centred * scale + shift)
-        slope_ref[rows, :] = grad
         low_ref[rows, :] = grad.astype(BF16)
         total = line_sums(grad, total)
         cross = line_sums(grad * (centred * inv_std), cross)
@@ -623,13 +629,13 @@
 
 
 def taps_gradient(
-    seg_count, ints_ref, hid_ref, field_ref, near_hid_ref, near_field_ref, keep_ref, send_ref, taps_ref, own_ref, near_ref,
-    sum_ref,
-):
+    seg_count, ints_ref, hid_ref, field_ref, near_hid_ref, *rest,
+):
+    near_field_refs, (keep_ref, send_ref, taps_ref, own_ref, near_ref, sum_ref) = rest[:-6], rest[-6:]
     line_rows = SIDE * seg_count
     step = WIDE * seg_count
     span = SIDE * step
-    taps_ref[...] = jnp.zeros_like(taps_ref)
+    clear_taps(taps_ref, seg_count)
     for source, turned in ((hid_ref, own_ref), (near_hid_ref, near_ref)):
         for line in range(SIDE):
             rows = slice(line * line_rows, (line + 1) * line_rows)
@@ -637,7 +643,8 @@
         for start in range(0, taps_ref.shape[1], LANES):
             turned[start : start + LANES, :] = taps_ref[:, start : start + LANES].T
     depth = taps_ref.shape[1]
-    own, near = field_ref[:span, :], near_field_ref[:span, :]
+    near_field = jnp.concatenate([ref[...] for ref in near_field_refs], axis=0)
+    own, near = field_ref[:span, :], near_field[:span, :]
     for row_off in range(3):
         rows = slice(row_off * step, row_off * step + span)
         part = dot32(own_ref[:, rows], own) + dot32(near_ref[:, rows], near)
@@ -645,7 +652,7 @@
     rest = sum_ref.shape[0] - 3 * depth
     count = field_ref.shape[0] - span
     sum_ref[3 * depth :, :] = jnp.zeros((rest, LANES), BF16)
-    kern_grad = field_ref[span:, :].astype(F32) + near_field_ref[span:, :].astype(F32)
+    kern_grad = field_ref[span:, :].astype(F32) + near_field[span:, :].astype(F32)
     sum_ref[3 * depth : 3 * depth + count, :] = kern_grad.astype(BF16)
     split_rows(sum_ref, ints_ref[4], keep_ref, send_ref)
 
@@ -762,7 +769,8 @@
 
 
 def last_norm(
-    seg_count, ints_ref, floats_ref, grad_ref, more_ref, act_ref, oth_ref, got_ref, back_ref, small_ref, low_own_ref, low_oth_ref,
+    seg_count, ints_ref, floats_ref, grad_ref, more_ref, act_ref, oth_ref, got_ref, back_ref, small_own_ref, small_oth_ref,
+    low_own_ref, low_oth_ref,
 ):
     line_rows = SIDE * seg_count
     side = ints_ref[1]
@@ -771,7 +779,7 @@
     for place, (grads, acts) in enumerate(((grad_ref, act_ref), (more_ref, oth_ref))):
         index = side if place == 0 else 1 - side
         average, inv_std, scale, mean, mix, _ = back_rows(
-            got_ref, back_ref, small_ref, 0, index, floats_ref[0]
+            got_ref, back_ref, (small_own_ref, small_oth_ref)[place], 0, index, floats_ref[0]
         )
         for line in range(SIDE):
             rows = slice(line * line_rows, (line + 1) * line_rows)
@@ -783,6 +791,19 @@
 def pick_rows(ints_ref, w_ref, out_ref):
     size = out_ref.shape[1]
     out_ref[...] = w_ref[:, pl.ds(pl.multiple_of((1 - ints_ref[1]) * size, size), size), :]
+
+
+def join_back(ints_ref, w_ref, from_ref, pair_ref, out_ref):
+    half = out_ref.shape[2]
+    size = half // 2
+    depth = 2 * half
+    for tap in range(9):
+        row_off, col = (8 - tap) // 3, (8 - tap) % 3
+        own = w_ref[tap // 3, (tap % 3) * depth : (tap % 3) * depth + half, :]
+        out_ref[row_off, col * depth : col * depth + half, :] = own.T
+        for index, ref in ((ints_ref[3], from_ref), (1 - ints_ref[3], pair_ref)):
+            start = pl.multiple_of(col * depth + half + index * size, size)
+            out_ref[row_off, pl.ds(start, size), :] = ref[tap].T
 
 
 def expand_gradient(
@@ -811,11 +832,10 @@
 
 
 def input_gradient(
-    ints_ref, own_ref, oth_ref, w_ref, resid_ref, near_own_ref, near_oth_ref, out_ref
+    ints_ref, own_ref, oth_ref, w_own_ref, w_oth_ref, resid_ref, near_own_ref, near_oth_ref, out_ref
 ):
     core = ints_ref[3]
-    half = own_ref.shape[1]
-    w_own, w_oth = w_ref[:, :half], w_ref[:, half:]
+    w_own, w_oth = w_own_ref[...], w_oth_ref[...]
     for clip, (own, oth) in enumerate(((own_ref, oth_ref), (near_own_ref, near_oth_ref))):
         grad = dot32(own[...], w_own, ((1,), (1,))) + dot32(oth[...], w_oth, ((1,), (1,)))
         out_ref[core if clip == 0 else 1 - core] = resid_ref[clip] + grad
@@ -883,7 +903,7 @@
 
     def share_all(sent):
         got = lax.all_to_all(sent, ("clip", "chan"), 0, 0)
-        return got.reshape((clip_size, chan_size) + sent.shape[1:])
+        return Free(got.reshape((clip_size, chan_size) + sent.shape[1:]))
 
     def share_clip(sent):
         sent = sent.array
@@ -914,41 +934,45 @@
     )
     got_blocks = {bits: swap(sent_blocks[bits], bits) for bits in (2, 3, 1)}
 
-    part_oth, w_rows, small = call(
-        reduce_other,
-        (
-            near((row_count, mid_width), BF16),
-            sds((chan_local, mid_width), BF16),
-            sds((chan_size, 24, mid_local), F32),
-        ),
-        ints=ints,
-    )(sent_blocks[0], got_blocks[1], got_blocks[2], got_blocks[3], x_oth)
-    near_one = swap(part_oth, 1)
-    part_own, far_send = call(
-        reduce_own,
-        (near((row_count, half), F32), near((row_count, half), BF16)),
-        ints=ints,
-    )(near_one, w_rows, x_own)
-    far_one = swap(far_send, 2)
+    def side_call(first, second, deps=()):
+        return call(
+            reduce_side,
+            (
+                near((row_count, half), BF16),
+                near((row_count, half), F32),
+                sds((chan_local, half), BF16),
+                sds((2, 24, mid_local), F32),
+            ),
+            deps=deps,
+            ints=ints,
+        )(first, second, x_oth, x_own)
+
+    oth_one, own_one, w_own_side, small_own = side_call(sent_blocks[0], got_blocks[1])
+    near_one = swap(oth_one, 1)
+    oth_far, own_far, w_oth_side, small_oth = side_call(got_blocks[2], got_blocks[3], (small_own,))
+    far_one = swap(call(add_near, near((row_count, half), BF16))(own_far, swap(oth_far, 1)), 2)
 
     w_pair = jnp.concatenate(pair(w_spatial, swap(w_spatial, 1).array), axis=2)
     w_fwd_own, w_fwd_oth = own_first(w_pair, side_index, half, 1)
     w_fwd = jnp.concatenate([w_fwd_own, w_fwd_oth], axis=1).reshape(3, 3 * mid_width, half)
 
-    act_one, act_one_low, sent_one = call(
-        functools.partial(first_sums, seg_count), (half_f32, half_low, sums_shape), deps=(w_fwd,), ints=ints,
-    )(part_own, far_one)
-    act_one_oth = swap(act_one_low, 2)
+    act_one, sent_one = call(
+        functools.partial(first_sums, seg_count), (half_low, sums_shape), deps=(w_fwd,), ints=ints,
+    )(own_one, near_one, far_one)
+    act_one_oth = swap(act_one, 2)
     got_one = share_all(sent_one)
 
-    act_two, act_two_low, sent_two, hid_one = call(
+    to_side = call(pick_rows, sds((9, half, mid_local), BF16), ints=ints)(w_spatial)
+
+    act_two, sent_two, hid_one = call(
         functools.partial(conv_forward, seg_count),
-        (half_f32, half_low, sums_shape, sds((row_count, mid_width), BF16)),
+        (half_low, sums_shape, sds((row_count, mid_width), BF16)),
         [pltpu.VMEM((pad_rows, 3 * mid_width), BF16), pltpu.VMEM((span, half), F32)],
+        deps=(to_side,),
         ints=ints,
         floats=floats,
-    )(act_one, act_one_oth, got_one, small, w_fwd)
-    act_two_oth = swap(act_two_low, 2)
+    )(act_one, act_one_oth, got_one, small_own, small_oth, w_fwd)
+    act_two_oth = swap(act_two, 2)
     got_two = share_all(sent_two)
 
     def gate_call(act, other):
@@ -958,7 +982,7 @@
             [pltpu.VMEM((row_count + 8, LANES), F32), pltpu.VMEM((edge_rows, LANES), F32)],
             ints=ints,
             floats=floats,
-        )(act, got_two, small)
+        )(act, got_two, small_oth if other else small_own)
 
     gated_own, hid_two, gate = gate_call(act_two, False)
     near_own = swap(gated_own, 1)
@@ -976,7 +1000,6 @@
     )(gated_own, gated_oth, near_own, near_oth, w_expand, bias_row)
     got_three = share_clip(sent_three)
 
-    to_side = call(pick_rows, sds((9, half, mid_local), BF16), deps=(sent_two,), ints=ints)(w_spatial)
     from_side = swap(to_side, 2)
     from_pair = swap(from_side, 1)
 
@@ -986,11 +1009,12 @@
     output, grad_resid, pooled, sent_back = call(
         functools.partial(finish, seg_count),
         (
-            sds((2, row_count, chan_local), BF16),
+            Early((2, row_count, chan_local), BF16, 2),
             near((2, row_count, chan_local), F32),
             near((2, chan_local), F32),
             near((2, chan_local), F32),
         ),
+        deps=(from_side,),
         ints=ints,
         floats=floats,
     )(
@@ -1007,7 +1031,7 @@
         else:
             outs += [near((row_count, mid_width), BF16)]
         return call(
-            functools.partial(expand_backward, seg_count, clip), tuple(outs), deps=(from_side,), ints=ints, floats=floats,
+            functools.partial(expand_backward, seg_count, clip), tuple(outs), ints=ints, floats=floats,
         )(got_three, got_back, gain_three[None], Pick(grad_resid, clip), Pick(act_three, clip), w_expand)
 
     low_three_oth, back_oth = back_call(1)
@@ -1021,7 +1045,7 @@
     def to_places(blocks):
         if places > 4:
             order = place ^ jnp.arange(places)
-            sent = jnp.stack([block.array if isinstance(block, Free) else block for block in blocks])[order]
+            sent = jnp.stack([block.array if isinstance(block, (Free, Near)) else block for block in blocks])[order]
             return list(lax.all_to_all(sent, "clip", 0, 0, axis_index_groups=groups)[order])
         return [blocks[0]] + [swap_clip(blocks[bits], 2 * bits) for bits in range(1, places)]
 
@@ -1035,45 +1059,52 @@
     )(gated_own, gated_oth, near_own, near_oth, low_three_own, low_three_oth, grad_classes)
 
     far_back = swap(call(add_low, near_low_half, deps=())(near_back, back_far), 2)
+    grad_bias = got_three[2, :class_count]
     wide_blocks = call(
         sum_blocks,
         blocks_of(wide_rows // 2, chan_local),
         [pltpu.VMEM((wide_rows // 2, chan_local), BF16)],
+        deps=(grad_bias,),
         ints=ints,
     )(wide_keep, swap_clip(wide_send, 1))
     wide_got = to_places(wide_blocks)
 
+    w_back = call(
+        join_back, sds((3, 3 * mid_width, half), BF16), deps=(wide_send,), ints=ints,
+    )(w_fwd, from_side, from_pair)
+
     logits_part = jnp.concatenate(own_first(dot32(pooled, w_classes), core_index, 1, 0))
     logits_wide = jnp.pad(logits_part, ((0, 0), (0, half - class_count)))
-    slope_two, slope_two_low, sent_back_two, kern_grad = call(
+    slope_two, sent_back_two, kern_grad = call(
         functools.partial(gate_backward, seg_count),
-        (half_f32, half_low, sds((everyone, 4, half), F32), sds((32, half), F32)),
+        (half_low, sds((everyone, 4, half), F32), sds((32, half), F32)),
         [
             pltpu.VMEM((edge_rows, LANES), F32),
             pltpu.VMEM((edge_rows, LANES), F32),
             pltpu.VMEM((row_count + 8, LANES), F32),
         ],
-        deps=(wide_send,),
+        deps=(w_back,),
         ints=ints,
         floats=floats,
-    )(back_own, near_back, far_back, hid_two, gate, act_two, got_two, small, logits_wide)
-    slope_two_oth = swap(slope_two_low, 2)
+    )(back_own, near_back, far_back, hid_two, gate, act_two, got_two, small_own, logits_wide)
+    slope_two_oth = swap(slope_two, 2)
     got_back_two = share_all(sent_back_two)
-    slope_one, slope_one_low, sent_back_one, field_keep, field_send = call(
+    field_rows = (span + 32,)
+    slope_one_low, sent_back_one, field_keep, *field_send = call(
         functools.partial(conv_backward, seg_count),
-        (half_f32, half_low, sums_shape) + (sds((span + 32, mid_local), BF16),) * 2,
+        (half_low, sums_shape, sds((span + 32, mid_local), BF16))
+        + tuple(sds((rows, mid_local), BF16) for rows in field_rows),
         [
             pltpu.VMEM((span, half), BF16),
             pltpu.VMEM((pad_rows, 3 * mid_width), BF16),
             pltpu.VMEM((span, half), F32),
-            pltpu.VMEM((9, half, mid_width), BF16),
         ],
         deps=(wide_blocks[0], near_hid),
         ints=ints,
         floats=floats,
     )(
-        slope_two, slope_two_oth, act_two, act_two_oth, got_two, got_back_two, act_one, got_one, small, w_fwd,
-        from_side, from_pair, kern_grad,
+        slope_two, slope_two_oth, act_two, act_two_oth.array, got_two, got_back_two, act_one, got_one,
+        small_own, small_oth, w_back, kern_grad,
     )
     slope_one_oth = swap(slope_one_low, 2)
     got_back_one = share_all(sent_back_one)
@@ -1086,9 +1117,8 @@
         + [pltpu.VMEM((3 * mid_width, pad_rows), BF16)] * 2
         + [pltpu.VMEM((pack_rows, mid_local), BF16)],
         ints=ints,
-        work=20_000_000_000,
         room=40 * 1024 * 1024,
-    )(hid_one, field_keep, near_hid, swap(field_send, 1))
+    )(hid_one, field_keep, near_hid, *[swap(each, 1) for each in field_send])
 
     wide_part = call(sum_parts, sds((wide_rows // clip_size, chan_local), BF16), deps=(pack_pair,))(*wide_got)
 
@@ -1098,13 +1128,12 @@
         deps=(pack_pair, wide_part),
         ints=ints,
         floats=floats,
-        work=50_000_000_000,
-    )(slope_one, slope_one_oth, act_one, act_one_oth, got_one, got_back_one, small)
+    )(slope_one_low, slope_one_oth, act_one, act_one_oth.array, got_one, got_back_one, small_own, small_oth)
     near_pair = [swap(low, 1) for low in low_pair]
     pack_other = swap_clip(pack_pair, 1)
     reduce_keep, reduce_send = call(
         reduce_gradient,
-        (Loose((chan_local // 2, mid_width), BF16),) * 2,
+        (Loose((chan_local // 2, mid_width), BF16), Loose((chan_local // 2, mid_width), BF16)),
         [pltpu.VMEM((chan_local, mid_width), BF16)],
         ints=ints,
     )(x_own, *low_pair, x_oth, *near_pair)
@@ -1120,7 +1149,7 @@
     )(pack_keep, Free(pack_other))
     pack_got = to_places(pack_blocks)
     wide_join = call(
-        join_places, Loose((wide_rows // 2, chan_local), BF16), deps=(pack_blocks[0],), ints=ints,
+        join_places, sds((wide_rows // 2, chan_local), BF16), deps=(pack_blocks[0],), ints=ints,
     )(*[Free(each) for each in to_places([wide_part] * places)])
     wide_other = swap_clip(wide_join, 1)
     reduce_got = swap_clip(reduce_send, 1)
@@ -1135,7 +1164,7 @@
     parts_got = to_places(parts)
     grad_frames = call(
         input_gradient, sds((2, row_count, chan_local), F32), deps=(parts[0],), ints=ints,
-    )(*low_pair, w_rows, grad_resid, *near_pair)
+    )(*low_pair, w_own_side, w_oth_side, grad_resid, *near_pair)
     pack_join, columns = call(
         functools.partial(stage_three, places, part_rows),
         (Loose((pack_rows // 2, mid_local), BF16), sds((everyone, share, mid_local), BF16)),
@@ -1159,13 +1188,13 @@
         (sds((9, mid_width, mid_local), F32),) + (sds((9, mid_local), F32),) * 2,
         [pltpu.VMEM((pack_rows, mid_local), BF16)],
         ints=ints,
-        work=20_000_000_000,
     )(pack_join, Free(pack_other))
 
-    mine = lax.dynamic_index_in_dim(got_back_two, clip_index, 0, keepdims=False)
+    mine = lax.dynamic_index_in_dim(got_back_two.array, clip_index, 0, keepdims=False)
     logits = jnp.sum(mine, axis=0)[2:, :class_count] + class_bias
 
     def own_sums(got):
+        got = got.array
         sums = jnp.sum(got.reshape((clip_size, 2, 2) + got.shape[2:]), axis=(0, 2))
         sums = lax.dynamic_index_in_dim(sums, side_index, 0, keepdims=False)
         return lax.dynamic_slice_in_dim(sums[:2], core_index * mid_local, mid_local, 1)
@@ -1173,7 +1202,6 @@
     grads_one = own_sums(got_back_one)
     grads_two = own_sums(got_back_two)
     grads_three = got_back
-    grad_bias = got_three[2, :class_count]
 
     def whole(array):
         return array.reshape(2, pixel_count, seg_count, chan_local).transpose(0, 2, 1, 3)

time: 259 us -> 245 us (0.946)
  waiting for transfers between devices: 68.1 us -> 51.3 us
  Pallas kernels: 81.6 us -> 85.2 us
    ppermute x20 -> x21, waiting for transfers between devices: 19.1 us -> 9.18 us  [swap(): lax.ppermute(array, 'chan', [(i, i ^ bits) for i in range(chan_size)])]
    pallas_call x28 -> x30, Pallas kernels: 81.6 us -> 85.2 us  [run(): pl.pallas_call(kernel, out_shape=outs, in_specs=[SMEM] * len(scalars) + [...]
    all_to_all x3, waiting for transfers between devices: 10.7 us -> 7.33 us  [share_all(): got = lax.all_to_all(sent, ('clip', 'chan'), 0, 0)]
    ppermute x25, waiting for transfers between devices: 29.9 us -> 26.6 us  [swap_clip(): lax.ppermute(array, 'clip', [(i, i ^ bits) for i in range(clip_size)])]
    ppermute x25, starting transfers between devices: 34.4 us -> 37.4 us  [swap_clip(): lax.ppermute(array, 'clip', [(i, i ^ bits) for i in range(clip_size)])]
    ppermute x20 -> x21, starting transfers between devices: 14.1 us -> 14.5 us  [swap(): lax.ppermute(array, 'chan', [(i, i ^ bits) for i in range(chan_size)])]
    unnamed x54 -> x42, local copies, waits for them, and re-layouts: 6.27 us -> 5.99 us
  transfers between devices with their start and end apart: 49 -> 50, of which waited for: 19 -> 17; matrix products, arithmetic and copies ran while one was open for 7% -> 7% of each run, Pallas kernels for 24% -> 26%
where the time goes in v3:
time: 245 us; the launch traced here: 244 us
  Pallas kernels  85.2 us (35%)
  starting transfers between devices  69.3 us (28%)
  waiting for transfers between devices  51.3 us (21%)
  local copies, waits for them, and re-layouts  14.6 us (6%)
  blocking collectives  11.7 us (5%)
  other arithmetic  7.99 us (3%)
    pallas_call x30, Pallas kernels, run(): pl.pallas_call(kernel, out_shape=outs, in_specs=[SMEM] * len(scalars) + [...  85.2 us
    ppermute x25, starting transfers between devices, swap_clip(): lax.ppermute(array, 'clip', [(i, i ^ bits) for i in range(clip_size)])  37.4 us
    ppermute x25, waiting for transfers between devices, swap_clip(): lax.ppermute(array, 'clip', [(i, i ^ bits) for i in range(clip_size)])  26.6 us
    ppermute x21, starting transfers between devices, swap(): lax.ppermute(array, 'chan', [(i, i ^ bits) for i in range(chan_size)])  14.5 us
    all_to_all x3, starting transfers between devices, share_all(): got = lax.all_to_all(sent, ('clip', 'chan'), 0, 0)  12.6 us
    all_to_all x1, blocking collectives, share_all(): got = lax.all_to_all(sent, ('clip', 'chan'), 0, 0)  11.7 us
    ppermute x21, waiting for transfers between devices, swap(): lax.ppermute(array, 'chan', [(i, i ^ bits) for i in range(chan_size)])  9.18 us
    all_to_all x1, waiting for transfers between devices, per_device(): reduce_got = lax.all_to_all(columns, ('clip', 'chan'), 0, 0)  8.2 us
  transfers between devices with their start and end apart: 50, of which 17 were waited for; matrix products, arithmetic and copies ran while one was open for 7% of the time, Pallas kernels for 26%

profile of v3, /device:TPU:0, one launch (start us, length us, event | category | flops | bytes accessed | tf_op | source)
XLA Modules:
  0.0 243.6 jit_solution(16039600959790472434)
XLA Ops:
  3.2 2.9 %collective-permute-start.2 = (bf16[608,128]{1,0:T(8,128)(2,1)}, bf16[608,128]{1,0:T(8,128)(2,1)S(1)}, u32[]{:S(2)}, u32[]{:S(2)}) collective-permute-start(bf16[608,128]{1,0:T(8,128)(2,1)} %get-tuple-element.85), channel_id=1, source_target_pairs={{0,2},{1,3},{2,0},{3,1},{4,6},{5,7},{6,4},{7,5},{8,10},{9,11},{10,... | collective-permute-start | bytes 466952 | tf_op jit(solution)/shard_map/ppermute | solution.py:880
  8.8 3.4 %shard_map.289 = (bf16[784,256]{1,0:T(8,128)(2,1)S(1)}, f32[784,256]{1,0:T(8,128)S(1)}, bf16[512,256]{1,0:T(8,128)(2,1)}, f32[2,24,128]{2,1,0:T(8,128)}) custom-call(s32[6]{0:T(128)S(1)} %stack.19.refs_0_, bf16[608,128]{1,0:T(8,128)(2,1)} %get-tuple-element.81.refs_1_, bf16[608,128]{1,0:T(8,128)(2,1)S(1)} %collective-permute-done.refs_2_, ...), custom_call_target="tpu_custom_call" | custom-call | tf_op jit(solution)/shard_map/pallas_call | solution.py:179
  13.3 3.0 %shard_map.290 = (bf16[784,256]{1,0:T(8,128)(2,1)S(1)}, f32[784,256]{1,0:T(8,128)S(1)}, bf16[512,256]{1,0:T(8,128)(2,1)}, f32[2,24,128]{2,1,0:T(8,128)}) custom-call(s32[6]{0:T(128)S(1)} %stack.19.refs_0_, bf16[608,128]{1,0:T(8,128)(2,1)S(1)} %collective-permute-done.2.refs_1_, bf16[608,128]{1,0:T(8,128)(2,1)S(1)} %collective-permute-done.3.refs_2_, ...), custom_call_target="tpu_custom_call" | custom-call | tf_op jit(solution)/shard_map/pallas_call | solution.py:179
  23.4 6.5 %collective-permute-done.5.refs_3_ = bf16[784,256]{1,0:T(8,128)(2,1)S(1)} collective-permute-done((bf16[784,256]{1,0:T(8,128)(2,1)S(1)}, bf16[784,256]{1,0:T(8,128)(2,1)S(1)}, u32[]{:S(2)}, u32[]{:S(2)}) %collective-permute-start.5) | collective-permute-done | bytes 401440 | tf_op jit(solution)/shard_map/ppermute | solution.py:880
  33.1 4.9 %all-to-all-start = ((f32[32,2,256]{2,1,0:T(2,128)}), f32[32,2,256]{2,1,0:T(2,128)S(1)}, u32[]{:S(2)}, u32[]{:S(2)}) async-start(f32[32,2,256]{2,1,0:T(2,128)} %get-tuple-element.91), calls=%async_computation | async-start | bytes 131072 | tf_op jit(solution)/shard_map/all_to_all | solution.py:905
  42.9 2.5 %all-to-all-done = f32[32,2,256]{2,1,0:T(2,128)S(1)} async-done(((f32[32,2,256]{2,1,0:T(2,128)}), f32[32,2,256]{2,1,0:T(2,128)S(1)}, u32[]{:S(2)}, u32[]{:S(2)}) %all-to-all-start) | async-done | bytes 65568 | tf_op jit(solution)/shard_map/all_to_all | solution.py:905
  45.5 5.5 %shard_map.294 = (bf16[784,256]{1,0:T(8,128)(2,1)}, f32[32,2,256]{2,1,0:T(2,128)}, bf16[784,512]{1,0:T(8,128)(2,1)}) custom-call(s32[6]{0:T(128)S(1)} %stack.19.refs_0_, f32[3]{0:T(128)S(1)} %pad_maximum_fusion.2.refs_1_, bf16[784,256]{1,0:T(8,128)(2,1)} %get-tuple-element.90.refs_2_.refs_8_.refs_4_, ...), custom_call_target="tpu_custom_call" | custom-call | tf_op jit(solution)/shard_map/pallas_call | solution.py:179
  51.4 11.7 %all_to_all.25 = f32[32,2,256]{2,1,0:T(2,128)S(1)} all-to-all(f32[32,2,256]{2,1,0:T(2,128)} %get-tuple-element.94), channel_id=1, replica_groups=mesh['clip'=8,'chan'=4] {'clip','chan'}, dimensions={0} | all-to-all | bytes 131072 | tf_op jit(solution)/shard_map/all_to_all | solution.py:905
  76.3 2.6 %collective-permute-start.13 = (f32[3,512]{1,0:T(4,128)S(1)}, f32[3,512]{1,0:T(4,128)S(1)}, u32[]{:S(2)}, u32[]{:S(2)}) collective-permute-start(f32[3,512]{1,0:T(4,128)S(1)} %add.91), channel_id=1, source_target_pairs={{0,16},{4,20},{8,24},{12,28},{16,0},{20,4},{24,8},{28,12},{1,17},{... | collective-permute-start | bytes 18440 | tf_op jit(solution)/shard_map/ppermute | solution.py:893
  80.8 3.5 %collective-permute-done.14 = f32[3,512]{1,0:T(4,128)S(1)} collective-permute-done((f32[3,512]{1,0:T(4,128)S(1)}, f32[3,512]{1,0:T(4,128)S(1)}, u32[]{:S(2)}, u32[]{:S(2)}) %collective-permute-start.14) | collective-permute-done | bytes 6176 | tf_op jit(solution)/shard_map/ppermute | solution.py:893
  84.9 4.9 %shard_map.298 = (bf16[2,784,512]{2,1,0:T(8,128)(2,1)}, f32[2,784,512]{2,1,0:T(8,128)S(1)}, f32[2,512]{1,0:T(2,128)S(1)}, f32[2,512]{1,0:T(2,128)S(1)}) custom-call(s32[6]{0:T(128)S(1)} %stack.19.refs_0_, f32[3]{0:T(128)S(1)} %pad_maximum_fusion.2.refs_1_, f32[3,512]{1,0:T(4,128)} %add_add_fusion.refs_2_, f32[1,512]{1,0:T(1,128)} %bitcast.80, ...), custom_call_target="tpu_custom_call" | custom-call | tf_op jit(solution)/shard_map/pallas_call | solution.py:179
  94.9 3.0 %collective-permute-start.19 = (f32[2,512]{1,0:T(2,128)S(1)}, f32[2,512]{1,0:T(2,128)S(1)}, u32[]{:S(2)}, u32[]{:S(2)}) collective-permute-start(f32[2,512]{1,0:T(2,128)S(1)} %add.95), channel_id=1, source_target_pairs={{0,24},{4,28},{8,16},{12,20},{16,8},{20,12},{24,0},{28,4},{1,25},{... | collective-permute-start | bytes 12296 | tf_op jit(solution)/shard_map/ppermute | solution.py:893
  107.9 3.2 %shard_map.302 = (bf16[448,512]{1,0:T(8,128)(2,1)}, bf16[448,512]{1,0:T(8,128)(2,1)}) custom-call(s32[6]{0:T(128)S(1)} %stack.19.refs_0_, bf16[784,256]{1,0:T(8,128)(2,1)S(1)} %get-tuple-element.95.refs_1_, bf16[784,256]{1,0:T(8,128)(2,1)S(1)} %shard_map.296.refs_2_, bf16[784,256]{1,0:T(8,128)(2,1)S(1)} %collective-permute-done.9.refs_3_, ...), custom_call_target="tpu_custom_call" | custom-call | tf_op jit(solution)/shard_map/pallas_call | solution.py:179
  113.1 3.7 %shard_map.303.refs_11_.refs_12_ = bf16[3,1536,256]{2,1,0:T(8,128)(2,1)} custom-call(s32[6]{0:T(128)S(1)} %stack.19.refs_0_, bf16[3,1536,256]{2,1,0:T(8,128)(2,1)} %bitcast.74, bf16[9,256,128]{2,1,0:T(8,128)(2,1)S(1)} %collective-permute-done.15.refs_12_.refs_2_, bf16[9,256,128]{2,1,0:T(8,128)(2,1)S(1)} %collective-permute-done.22.refs_3_, ...), custom_call_target="tpu_custom_call" | custom-call | tf_op jit(solution)/shard_map/pallas_call | solution.py:179
  117.1 4.8 %shard_map.304 = (bf16[784,256]{1,0:T(8,128)(2,1)}, f32[32,4,256]{2,1,0:T(4,128)}, f32[32,256]{1,0:T(8,128)}) custom-call(s32[6]{0:T(128)S(1)} %stack.19.refs_0_, f32[3]{0:T(128)S(1)} %pad_maximum_fusion.2.refs_1_, f32[784,256]{1,0:T(8,128)S(1)} %get-tuple-element.101.refs_2_, bf16[784,512]{1,0:T(8,128)(2,1)S(1)} %collective-permute-done.20.refs_0_.refs_3_, ...), custom_call_target="tpu_custom_call" | custom-call | tf_op jit(solution)/shard_map/pallas_call | solution.py:179
  123.4 4.2 %all-to-all-start.2 = ((f32[32,4,256]{2,1,0:T(4,128)}), f32[32,4,256]{2,1,0:T(4,128)S(1)}, u32[]{:S(2)}, u32[]{:S(2)}) async-start(f32[32,4,256]{2,1,0:T(4,128)} %get-tuple-element.110), calls=%async_computation.2 | async-start | bytes 262144 | tf_op jit(solution)/shard_map/all_to_all | solution.py:905
  131.0 4.8 %all-to-all-done.2 = f32[32,4,256]{2,1,0:T(4,128)S(1)} async-done(((f32[32,4,256]{2,1,0:T(4,128)}), f32[32,4,256]{2,1,0:T(4,128)S(1)}, u32[]{:S(2)}, u32[]{:S(2)}) %all-to-all-start.2) | async-done | bytes 131104 | tf_op jit(solution)/shard_map/all_to_all | solution.py:905
  135.8 5.9 %shard_map.306 = (bf16[784,256]{1,0:T(8,128)(2,1)}, f32[32,2,256]{2,1,0:T(2,128)}, bf16[928,128]{1,0:T(8,128)(2,1)}, bf16[928,128]{1,0:T(8,128)(2,1)}) custom-call(s32[6]{0:T(128)S(1)} %stack.19.refs_0_, f32[3]{0:T(128)S(1)} %pad_maximum_fusion.2.refs_1_, bf16[784,256]{1,0:T(8,128)(2,1)} %get-tuple-element.111.refs_2_, ...), custom_call_target="tpu_custom_call" | custom-call | tf_op jit(solution)/shard_map/pallas_call | solution.py:179
  142.4 2.4 collective-permute-start.29
  147.0 3.5 %all-to-all-start.3 = ((f32[32,2,256]{2,1,0:T(2,128)}), f32[32,2,256]{2,1,0:T(2,128)S(1)}, u32[]{:S(2)}, u32[]{:S(2)}) async-start(f32[32,2,256]{2,1,0:T(2,128)} %get-tuple-element.117), calls=%async_computation.3 | async-start | bytes 131072 | tf_op jit(solution)/shard_map/all_to_all | solution.py:905
  150.5 7.9 %shard_map.307 = (bf16[2368,128]{1,0:T(8,128)(2,1)}, bf16[2368,128]{1,0:T(8,128)(2,1)}) custom-call(s32[6]{0:T(128)S(1)} %stack.19.refs_0_, bf16[784,512]{1,0:T(8,128)(2,1)} %get-tuple-element.115.refs_1_, bf16[928,128]{1,0:T(8,128)(2,1)} %get-tuple-element.118.refs_2_, bf16[784,512]{1,0:T(8,128)(2,1)} %collective-permute-done.25.refs_15_.refs_3_, ...), custom_call_target="tpu_custom_call" | custom-call | flops 20000000000 | tf_op jit(solution)/shard_map/pallas_call | solution.py:179
  162.0 2.7 %shard_map.309 = (bf16[784,256]{1,0:T(8,128)(2,1)}, bf16[784,256]{1,0:T(8,128)(2,1)}) custom-call(s32[6]{0:T(128)S(1)} %stack.19.refs_0_, f32[3]{0:T(128)S(1)} %pad_maximum_fusion.2.refs_1_, bf16[784,256]{1,0:T(8,128)(2,1)} %get-tuple-element.116.refs_2_, bf16[784,256]{1,0:T(8,128)(2,1)} %collective-permute-done.26.refs_3_, ...), custom_call_target="tpu_custom_call" | custom-call | flops 1000000000 | tf_op jit(solution)/shard_map/pallas_call | solution.py:179
  166.7 2.4 %collective-permute-start.39 = (bf16[112,512]{1,0:T(8,128)(2,1)}, bf16[112,512]{1,0:T(8,128)(2,1)}, u32[]{:S(2)}, u32[]{:S(2)}) collective-permute-start(bf16[112,512]{1,0:T(8,128)(2,1)} %shard_map.308.refs_11_.refs_1_), channel_id=1, source_target_pairs={{0,16},{4,20},{8,24},{12,28},{16,0},{20,4},{24,8},{28,12},{1,17},{... | collective-permute-start | bytes 344072 | tf_op jit(solution)/shard_map/ppermute | solution.py:893
  169.2 4.9 %shard_map.310 = (bf16[256,512]{1,0:T(8,128)(2,1)S(1)}, bf16[256,512]{1,0:T(8,128)(2,1)}) custom-call(s32[6]{0:T(128)S(1)} %stack.19.refs_0_, bf16[2,784,512]{2,1,0:T(8,128)(2,1)} %bitcast.70, bf16[784,256]{1,0:T(8,128)(2,1)} %get-tuple-element.124.refs_2_.refs_1_, bf16[784,256]{1,0:T(8,128)(2,1)} %get-tuple-element.125.refs_3_.refs_2_, ...), custom_call_target="tpu_custom_call" | custom-call | tf_op jit(solution)/shard_map/pallas_call | solution.py:179
  179.7 3.1 %collective-permute-start.36 = (bf16[592,128]{1,0:T(8,128)(2,1)}, bf16[592,128]{1,0:T(8,128)(2,1)}, u32[]{:S(2)}, u32[]{:S(2)}) collective-permute-start(bf16[592,128]{1,0:T(8,128)(2,1)} %get-tuple-element.133), channel_id=1, source_target_pairs={{0,16},{4,20},{8,24},{12,28},{16,0},{20,4},{24,8},{28,12},{1,17},{... | collective-permute-start | bytes 454664 | tf_op jit(solution)/shard_map/ppermute | solution.py:893
  189.0 5.2 %collective-permute-done.36.refs_5_ = bf16[592,128]{1,0:T(8,128)(2,1)} collective-permute-done((bf16[592,128]{1,0:T(8,128)(2,1)}, bf16[592,128]{1,0:T(8,128)(2,1)}, u32[]{:S(2)}, u32[]{:S(2)}) %collective-permute-start.36) | collective-permute-done | bytes 151584 | tf_op jit(solution)/shard_map/ppermute | solution.py:893
  197.6 2.5 %collective-permute-start.41 = (bf16[848,128]{1,0:T(8,128)(2,1)S(1)}, bf16[848,128]{1,0:T(8,128)(2,1)S(1)}, u32[]{:S(2)}, u32[]{:S(2)}) collective-permute-start(bf16[848,128]{1,0:T(8,128)(2,1)S(1)} %get-tuple-element.136), channel_id=1, source_target_pairs={{0,8},{4,12},{8,0},{12,4},{16,24},{20,28},{24,16},{28,20},{1,9},{5... | collective-permute-start | bytes 651272 | tf_op jit(solution)/shard_map/ppermute | solution.py:893
  203.1 4.0 %shard_map.314.refs_6_ = f32[2,784,512]{2,1,0:T(8,128)} custom-call(s32[6]{0:T(128)S(1)} %stack.19.refs_0_, bf16[784,256]{1,0:T(8,128)(2,1)} %get-tuple-element.124.refs_2_.refs_1_, bf16[784,256]{1,0:T(8,128)(2,1)} %get-tuple-element.125.refs_3_.refs_2_, bf16[512,256]{1,0:T(8,128)(2,1)} %get-tuple-element.126.refs_3_, ...), custom_call_target="tpu_custom_call" | custom-call | tf_op jit(solution)/shard_map/pallas_call | solution.py:179
  207.2 10.4 %collective-permute-done.42.refs_3_ = bf16[848,128]{1,0:T(8,128)(2,1)S(1)} collective-permute-done((bf16[848,128]{1,0:T(8,128)(2,1)S(1)}, bf16[848,128]{1,0:T(8,128)(2,1)S(1)}, u32[]{:S(2)}, u32[]{:S(2)}) %collective-permute-start.42) | collective-permute-done | bytes 217120 | tf_op jit(solution)/shard_map/ppermute | solution.py:893
  222.0 4.9 %all-to-all-start.4 = ((bf16[32,64,128]{2,1,0:T(8,128)(2,1)}), bf16[32,64,128]{2,1,0:T(8,128)(2,1)S(1)}, u32[]{:S(2)}, u32[]{:S(2)}) async-start(bf16[32,64,128]{2,1,0:T(8,128)(2,1)} %get-tuple-element.139), calls=%async_computation.4 | async-start | bytes 1048576 | tf_op jit(solution)/shard_map/all_to_all | solution.py:1175
  227.9 2.4 shard_map.317
  234.2 8.2 %all-to-all-done.4 = bf16[32,64,128]{2,1,0:T(8,128)(2,1)S(1)} async-done(((bf16[32,64,128]{2,1,0:T(8,128)(2,1)}), bf16[32,64,128]{2,1,0:T(8,128)(2,1)S(1)}, u32[]{:S(2)}, u32[]{:S(2)}) %all-to-all-start.4) | async-done | bytes 524320 | tf_op jit(solution)/shard_map/all_to_all | solution.py:1175
  (173 shorter events, 96.3 us)
Async XLA Ops:
  0.7 19.4 %collective-permute-start.6 = (bf16[9,512,128]{2,1,0:T(8,128)(2,1)}, bf16[9,512,128]{2,1,0:T(8,128)(2,1)}, u32[]{:S(2)}, u32[]{:S(2)}) collective-permute-start(bf16[9,512,128]{2,1,0:T(8,128)(2,1)} %refs_1_.3), channel_id=1, source_target_pairs={{0,1},{1,0},{2,3},{3,2},{4,5},{5,4},{6,7},{7,6},{8,9},{9,8},{10,11... | collective-permute-start | bytes 3538952 | tf_op jit(solution)/shard_map/ppermute | solution.py:880
  3.2 9.0 %collective-permute-start.2 = (bf16[608,128]{1,0:T(8,128)(2,1)}, bf16[608,128]{1,0:T(8,128)(2,1)S(1)}, u32[]{:S(2)}, u32[]{:S(2)}) collective-permute-start(bf16[608,128]{1,0:T(8,128)(2,1)} %get-tuple-element.85), channel_id=1, source_target_pairs={{0,2},{1,3},{2,0},{3,1},{4,6},{5,7},{6,4},{7,5},{8,10},{9,11},{10,... | collective-permute-start | bytes 466952 | tf_op jit(solution)/shard_map/ppermute | solution.py:880
  18.2 11.6 %collective-permute-start.5 = (bf16[784,256]{1,0:T(8,128)(2,1)S(1)}, bf16[784,256]{1,0:T(8,128)(2,1)S(1)}, u32[]{:S(2)}, u32[]{:S(2)}) collective-permute-start(bf16[784,256]{1,0:T(8,128)(2,1)S(1)} %shard_map.291), channel_id=1, source_target_pairs={{0,2},{1,3},{2,0},{3,1},{4,6},{5,7},{6,4},{7,5},{8,10},{9,11},{10,... | collective-permute-start | bytes 1204232 | tf_op jit(solution)/shard_map/ppermute | solution.py:880
  31.4 14.1 %collective-permute-start.7 = (bf16[784,256]{1,0:T(8,128)(2,1)}, bf16[784,256]{1,0:T(8,128)(2,1)S(1)}, u32[]{:S(2)}, u32[]{:S(2)}) collective-permute-start(bf16[784,256]{1,0:T(8,128)(2,1)} %get-tuple-element.90.refs_2_.refs_8_.refs_4_), channel_id=1, source_target_pairs={{0,2},{1,3},{2,0},{3,1},{4,6},{5,7},{6,4},{7,5},{8,10},{9,11},{10,... | collective-permute-start | bytes 1204232 | tf_op jit(solution)/shard_map/ppermute | solution.py:880
  33.1 12.3 %all-to-all-start = ((f32[32,2,256]{2,1,0:T(2,128)}), f32[32,2,256]{2,1,0:T(2,128)S(1)}, u32[]{:S(2)}, u32[]{:S(2)}) async-start(f32[32,2,256]{2,1,0:T(2,128)} %get-tuple-element.91), calls=%async_computation | async-start | bytes 131072 | tf_op jit(solution)/shard_map/all_to_all | solution.py:905
  51.0 14.6 %collective-permute-start.8 = (bf16[784,256]{1,0:T(8,128)(2,1)}, bf16[784,256]{1,0:T(8,128)(2,1)S(1)}, u32[]{:S(2)}, u32[]{:S(2)}) collective-permute-start(bf16[784,256]{1,0:T(8,128)(2,1)} %get-tuple-element.93.refs_2_.refs_7_.refs_4_), channel_id=1, source_target_pairs={{0,2},{1,3},{2,0},{3,1},{4,6},{5,7},{6,4},{7,5},{8,10},{9,11},{10,... | collective-permute-start | bytes 1204232 | tf_op jit(solution)/shard_map/ppermute | solution.py:880
  68.0 16.9 %collective-permute-start.15 = (bf16[9,256,128]{2,1,0:T(8,128)(2,1)S(1)}, bf16[9,256,128]{2,1,0:T(8,128)(2,1)S(1)}, u32[]{:S(2)}, u32[]{:S(2)}) collective-permute-start(bf16[9,256,128]{2,1,0:T(8,128)(2,1)S(1)} %copy-done.16), channel_id=1, source_target_pairs={{0,2},{1,3},{2,0},{3,1},{4,6},{5,7},{6,4},{7,5},{8,10},{9,11},{10,... | collective-permute-start | bytes 1769480 | tf_op jit(solution)/shard_map/ppermute | solution.py:880
  102.8 10.4 %collective-permute-start.22 = (bf16[9,256,128]{2,1,0:T(8,128)(2,1)S(1)}, bf16[9,256,128]{2,1,0:T(8,128)(2,1)S(1)}, u32[]{:S(2)}, u32[]{:S(2)}) collective-permute-start(bf16[9,256,128]{2,1,0:T(8,128)(2,1)S(1)} %collective-permute-done.15.refs_12_.refs_2_), channel_id=1, source_target_pairs={{0,1},{1,0},{2,3},{3,2},{4,5},{5,4},{6,7},{7,6},{8,9},{9,8},{10,11... | collective-permute-start | bytes 1769480 | tf_op jit(solution)/shard_map/ppermute | solution.py:880
  103.3 27.8 %collective-permute-start.25 = (bf16[784,512]{1,0:T(8,128)(2,1)}, bf16[784,512]{1,0:T(8,128)(2,1)}, u32[]{:S(2)}, u32[]{:S(2)}) collective-permute-start(bf16[784,512]{1,0:T(8,128)(2,1)} %get-tuple-element.115.refs_1_), channel_id=1, source_target_pairs={{0,1},{1,0},{2,3},{3,2},{4,5},{5,4},{6,7},{7,6},{8,9},{9,8},{10,11... | collective-permute-start | bytes 2408456 | tf_op jit(solution)/shard_map/ppermute | solution.py:880
  105.4 11.7 %collective-permute-start.21 = (bf16[784,256]{1,0:T(8,128)(2,1)S(1)}, bf16[784,256]{1,0:T(8,128)(2,1)S(1)}, u32[]{:S(2)}, u32[]{:S(2)}) collective-permute-start(bf16[784,256]{1,0:T(8,128)(2,1)S(1)} %shard_map.301), channel_id=1, source_target_pairs={{0,2},{1,3},{2,0},{3,1},{4,6},{5,7},{6,4},{7,5},{8,10},{9,11},{10,... | collective-permute-start | bytes 1204232 | tf_op jit(solution)/shard_map/ppermute | solution.py:880
  111.1 17.7 %collective-permute-start.24 = (bf16[448,512]{1,0:T(8,128)(2,1)}, bf16[448,512]{1,0:T(8,128)(2,1)}, u32[]{:S(2)}, u32[]{:S(2)}) collective-permute-start(bf16[448,512]{1,0:T(8,128)(2,1)} %get-tuple-element.109.refs_4_), channel_id=1, source_target_pairs={{0,4},{4,0},{8,12},{12,8},{16,20},{20,16},{24,28},{28,24},{1,5},{5... | collective-permute-start | bytes 1376264 | tf_op jit(solution)/shard_map/ppermute | solution.py:893
  121.9 13.9 %collective-permute-start.23 = (bf16[784,256]{1,0:T(8,128)(2,1)}, bf16[784,256]{1,0:T(8,128)(2,1)}, u32[]{:S(2)}, u32[]{:S(2)}) collective-permute-start(bf16[784,256]{1,0:T(8,128)(2,1)} %get-tuple-element.111.refs_2_), channel_id=1, source_target_pairs={{0,2},{1,3},{2,0},{3,1},{4,6},{5,7},{6,4},{7,5},{8,10},{9,11},{10,... | collective-permute-start | bytes 1204232 | tf_op jit(solution)/shard_map/ppermute | solution.py:880
  123.4 12.5 %all-to-all-start.2 = ((f32[32,4,256]{2,1,0:T(4,128)}), f32[32,4,256]{2,1,0:T(4,128)S(1)}, u32[]{:S(2)}, u32[]{:S(2)}) async-start(f32[32,4,256]{2,1,0:T(4,128)} %get-tuple-element.110), calls=%async_computation.2 | async-start | bytes 262144 | tf_op jit(solution)/shard_map/all_to_all | solution.py:905
  141.9 18.4 %collective-permute-start.28 = (bf16[112,512]{1,0:T(8,128)(2,1)}, bf16[112,512]{1,0:T(8,128)(2,1)}, u32[]{:S(2)}, u32[]{:S(2)}) collective-permute-start(bf16[112,512]{1,0:T(8,128)(2,1)} %get-tuple-element.121), channel_id=1, source_target_pairs={{0,8},{4,12},{8,0},{12,4},{16,24},{20,28},{24,16},{28,20},{1,9},{5... | collective-permute-start | bytes 344072 | tf_op jit(solution)/shard_map/ppermute | solution.py:893
  142.4 17.9 %collective-permute-start.29 = (bf16[112,512]{1,0:T(8,128)(2,1)}, bf16[112,512]{1,0:T(8,128)(2,1)}, u32[]{:S(2)}, u32[]{:S(2)}) collective-permute-start(bf16[112,512]{1,0:T(8,128)(2,1)} %get-tuple-element.122), channel_id=1, source_target_pairs={{0,16},{4,20},{8,24},{12,28},{16,0},{20,4},{24,8},{28,12},{1,17},{... | collective-permute-start | bytes 344072 | tf_op jit(solution)/shard_map/ppermute | solution.py:893
  144.8 15.4 %collective-permute-start.30 = (bf16[112,512]{1,0:T(8,128)(2,1)}, bf16[112,512]{1,0:T(8,128)(2,1)}, u32[]{:S(2)}, u32[]{:S(2)}) collective-permute-start(bf16[112,512]{1,0:T(8,128)(2,1)} %get-tuple-element.123), channel_id=1, source_target_pairs={{0,24},{4,28},{8,16},{12,20},{16,8},{20,12},{24,0},{28,4},{1,25},{... | collective-permute-start | bytes 344072 | tf_op jit(solution)/shard_map/ppermute | solution.py:893
  146.3 15.7 %collective-permute-start.26 = (bf16[784,256]{1,0:T(8,128)(2,1)}, bf16[784,256]{1,0:T(8,128)(2,1)}, u32[]{:S(2)}, u32[]{:S(2)}) collective-permute-start(bf16[784,256]{1,0:T(8,128)(2,1)} %get-tuple-element.116.refs_2_), channel_id=1, source_target_pairs={{0,2},{1,3},{2,0},{3,1},{4,6},{5,7},{6,4},{7,5},{8,10},{9,11},{10,... | collective-permute-start | bytes 1204232 | tf_op jit(solution)/shard_map/ppermute | solution.py:880
  147.0 15.0 %all-to-all-start.3 = ((f32[32,2,256]{2,1,0:T(2,128)}), f32[32,2,256]{2,1,0:T(2,128)S(1)}, u32[]{:S(2)}, u32[]{:S(2)}) async-start(f32[32,2,256]{2,1,0:T(2,128)} %get-tuple-element.117), calls=%async_computation.3 | async-start | bytes 131072 | tf_op jit(solution)/shard_map/all_to_all | solution.py:905
  158.5 18.1 %collective-permute-start.34 = (bf16[2368,128]{1,0:T(8,128)(2,1)}, bf16[2368,128]{1,0:T(8,128)(2,1)}, u32[]{:S(2)}, u32[]{:S(2)}) collective-permute-start(bf16[2368,128]{1,0:T(8,128)(2,1)} %get-tuple-element.120.refs_4_.refs_10_), channel_id=1, source_target_pairs={{0,4},{4,0},{8,12},{12,8},{16,20},{20,16},{24,28},{28,24},{1,5},{5... | collective-permute-start | bytes 1818632 | tf_op jit(solution)/shard_map/ppermute | solution.py:893
  165.3 14.4 %collective-permute-start.38 = (bf16[112,512]{1,0:T(8,128)(2,1)}, bf16[112,512]{1,0:T(8,128)(2,1)}, u32[]{:S(2)}, u32[]{:S(2)}) collective-permute-start(bf16[112,512]{1,0:T(8,128)(2,1)} %shard_map.308.refs_11_.refs_1_), channel_id=1, source_target_pairs={{0,8},{4,12},{8,0},{12,4},{16,24},{20,28},{24,16},{28,20},{1,9},{5... | collective-permute-start | bytes 344072 | tf_op jit(solution)/shard_map/ppermute | solution.py:893
  166.7 16.0 %collective-permute-start.39 = (bf16[112,512]{1,0:T(8,128)(2,1)}, bf16[112,512]{1,0:T(8,128)(2,1)}, u32[]{:S(2)}, u32[]{:S(2)}) collective-permute-start(bf16[112,512]{1,0:T(8,128)(2,1)} %shard_map.308.refs_11_.refs_1_), channel_id=1, source_target_pairs={{0,16},{4,20},{8,24},{12,28},{16,0},{20,4},{24,8},{28,12},{1,17},{... | collective-permute-start | bytes 344072 | tf_op jit(solution)/shard_map/ppermute | solution.py:893
  174.8 19.4 %collective-permute-start.33 = (bf16[256,512]{1,0:T(8,128)(2,1)}, bf16[256,512]{1,0:T(8,128)(2,1)}, u32[]{:S(2)}, u32[]{:S(2)}) collective-permute-start(bf16[256,512]{1,0:T(8,128)(2,1)} %get-tuple-element.129.refs_3_), channel_id=1, source_target_pairs={{0,4},{4,0},{8,12},{12,8},{16,20},{20,16},{24,28},{28,24},{1,5},{5... | collective-permute-start | bytes 786440 | tf_op jit(solution)/shard_map/ppermute | solution.py:893
  175.3 9.4 %collective-permute-start.40 = (bf16[112,512]{1,0:T(8,128)(2,1)}, bf16[112,512]{1,0:T(8,128)(2,1)}, u32[]{:S(2)}, u32[]{:S(2)}) collective-permute-start(bf16[112,512]{1,0:T(8,128)(2,1)} %shard_map.308.refs_11_.refs_1_), channel_id=1, source_target_pairs={{0,24},{4,28},{8,16},{12,20},{16,8},{20,12},{24,0},{28,4},{1,25},{... | collective-permute-start | bytes 344072 | tf_op jit(solution)/shard_map/ppermute | solution.py:893
  179.7 9.3 %collective-permute-start.35 = (bf16[592,128]{1,0:T(8,128)(2,1)}, bf16[592,128]{1,0:T(8,128)(2,1)}, u32[]{:S(2)}, u32[]{:S(2)}) collective-permute-start(bf16[592,128]{1,0:T(8,128)(2,1)} %get-tuple-element.132), channel_id=1, source_target_pairs={{0,8},{4,12},{8,0},{12,4},{16,24},{20,28},{24,16},{28,20},{1,9},{5... | collective-permute-start | bytes 454664 | tf_op jit(solution)/shard_map/ppermute | solution.py:893
  179.7 14.6 %collective-permute-start.36 = (bf16[592,128]{1,0:T(8,128)(2,1)}, bf16[592,128]{1,0:T(8,128)(2,1)}, u32[]{:S(2)}, u32[]{:S(2)}) collective-permute-start(bf16[592,128]{1,0:T(8,128)(2,1)} %get-tuple-element.133), channel_id=1, source_target_pairs={{0,16},{4,20},{8,24},{12,28},{16,0},{20,4},{24,8},{28,12},{1,17},{... | collective-permute-start | bytes 454664 | tf_op jit(solution)/shard_map/ppermute | solution.py:893
  182.8 11.5 %collective-permute-start.37 = (bf16[592,128]{1,0:T(8,128)(2,1)}, bf16[592,128]{1,0:T(8,128)(2,1)}, u32[]{:S(2)}, u32[]{:S(2)}) collective-permute-start(bf16[592,128]{1,0:T(8,128)(2,1)} %get-tuple-element.134), channel_id=1, source_target_pairs={{0,24},{4,28},{8,16},{12,20},{16,8},{20,12},{24,0},{28,4},{1,25},{... | collective-permute-start | bytes 454664 | tf_op jit(solution)/shard_map/ppermute | solution.py:893
  187.5 30.2 %collective-permute-start.44 = (bf16[448,512]{1,0:T(8,128)(2,1)}, bf16[448,512]{1,0:T(8,128)(2,1)S(1)}, u32[]{:S(2)}, u32[]{:S(2)}) collective-permute-start(bf16[448,512]{1,0:T(8,128)(2,1)} %shard_map.312.refs_7_.refs_1_), channel_id=1, source_target_pairs={{0,4},{4,0},{8,12},{12,8},{16,20},{20,16},{24,28},{28,24},{1,5},{5... | collective-permute-start | bytes 1376264 | tf_op jit(solution)/shard_map/ppermute | solution.py:893
  197.6 9.7 %collective-permute-start.41 = (bf16[848,128]{1,0:T(8,128)(2,1)S(1)}, bf16[848,128]{1,0:T(8,128)(2,1)S(1)}, u32[]{:S(2)}, u32[]{:S(2)}) collective-permute-start(bf16[848,128]{1,0:T(8,128)(2,1)S(1)} %get-tuple-element.136), channel_id=1, source_target_pairs={{0,8},{4,12},{8,0},{12,4},{16,24},{20,28},{24,16},{28,20},{1,9},{5... | collective-permute-start | bytes 651272 | tf_op jit(solution)/shard_map/ppermute | solution.py:893
  200.0 17.6 %collective-permute-start.42 = (bf16[848,128]{1,0:T(8,128)(2,1)S(1)}, bf16[848,128]{1,0:T(8,128)(2,1)S(1)}, u32[]{:S(2)}, u32[]{:S(2)}) collective-permute-start(bf16[848,128]{1,0:T(8,128)(2,1)S(1)} %get-tuple-element.137), channel_id=1, source_target_pairs={{0,16},{4,20},{8,24},{12,28},{16,0},{20,4},{24,8},{28,12},{1,17},{... | collective-permute-start | bytes 651272 | tf_op jit(solution)/shard_map/ppermute | solution.py:893
  200.6 17.1 %collective-permute-start.43 = (bf16[848,128]{1,0:T(8,128)(2,1)S(1)}, bf16[848,128]{1,0:T(8,128)(2,1)S(1)}, u32[]{:S(2)}, u32[]{:S(2)}) collective-permute-start(bf16[848,128]{1,0:T(8,128)(2,1)S(1)} %get-tuple-element.138), channel_id=1, source_target_pairs={{0,24},{4,28},{8,16},{12,20},{16,8},{20,12},{24,0},{28,4},{1,25},{... | collective-permute-start | bytes 651272 | tf_op jit(solution)/shard_map/ppermute | solution.py:893
  219.9 12.2 %collective-permute-start.45 = (bf16[2368,128]{1,0:T(8,128)(2,1)S(1)}, bf16[2368,128]{1,0:T(8,128)(2,1)S(1)}, u32[]{:S(2)}, u32[]{:S(2)}) collective-permute-start(bf16[2368,128]{1,0:T(8,128)(2,1)S(1)} %get-tuple-element.140.refs_1_.refs_3_), channel_id=1, source_target_pairs={{0,4},{4,0},{8,12},{12,8},{16,20},{20,16},{24,28},{28,24},{1,5},{5... | collective-permute-start | bytes 1818632 | tf_op jit(solution)/shard_map/ppermute | solution.py:893
  222.0 20.4 %all-to-all-start.4 = ((bf16[32,64,128]{2,1,0:T(8,128)(2,1)}), bf16[32,64,128]{2,1,0:T(8,128)(2,1)S(1)}, u32[]{:S(2)}, u32[]{:S(2)}) async-start(bf16[32,64,128]{2,1,0:T(8,128)(2,1)} %get-tuple-element.139), calls=%async_computation.4 | async-start | bytes 1048576 | tf_op jit(solution)/shard_map/all_to_all | solution.py:1175
  (39 other events, 299.1 us)

commit v4 on v3

--- a/solution.py
+++ b/solution.py
@@ -927,7 +927,7 @@
     span = SIDE * WIDE * seg_count
     edge_rows = EDGE * EDGE * seg_count
 
-    block_shape = sds((chan_local + 96, mid_local), BF16)
+    block_shape = Loose((chan_local + 96, mid_local), BF16)
     chan = chan_index.astype(jnp.int32)[None]
     sent_blocks = call(split_blocks, (block_shape,) * chan_size, ints=chan)(
         w_reduce, gain_one[None], shift_one[None], gain_two[None], shift_two[None], near_kern, far_kern
@@ -1053,7 +1053,7 @@
         return (sds((rows // places, width), BF16),) * places
 
     grad_classes = dot32(logit_pair, pooled, ((0,), (0,)))
-    wide_rows = (-(-(mid_width + class_count) // unit) + 1) * unit
+    wide_rows = -(-(mid_width + class_count) // unit) * unit
     wide_keep, wide_send = call(
         expand_gradient, halves(wide_rows, chan_local), [pltpu.VMEM((wide_rows, chan_local), BF16)], ints=ints,
     )(gated_own, gated_oth, near_own, near_oth, low_three_own, low_three_oth, grad_classes)
@@ -1089,7 +1089,8 @@
     )(back_own, near_back, far_back, hid_two, gate, act_two, got_two, small_own, logits_wide)
     slope_two_oth = swap(slope_two, 2)
     got_back_two = share_all(sent_back_two)
-    field_rows = (span + 32,)
+    field_rows = ((span + 32) // 48 * 16,) * 2
+    field_rows += (span + 32 - sum(field_rows),)
     slope_one_low, sent_back_one, field_keep, *field_send = call(
         functools.partial(conv_backward, seg_count),
         (half_low, sums_shape, sds((span + 32, mid_local), BF16))
@@ -1110,22 +1111,23 @@
     got_back_one = share_all(sent_back_one)
 
     pack_rows = -(-(9 * mid_width + 32) // unit) * unit
+    wide_part = call(sum_parts, sds((wide_rows // clip_size, chan_local), BF16), deps=(sent_back_one,))(*wide_got)
     pack_keep, pack_pair = call(
         functools.partial(taps_gradient, seg_count),
         halves(pack_rows, mid_local),
         [pltpu.VMEM((pad_rows, 3 * mid_width), BF16)]
         + [pltpu.VMEM((3 * mid_width, pad_rows), BF16)] * 2
         + [pltpu.VMEM((pack_rows, mid_local), BF16)],
+        deps=(wide_part,),
         ints=ints,
         room=40 * 1024 * 1024,
     )(hid_one, field_keep, near_hid, *[swap(each, 1) for each in field_send])
 
-    wide_part = call(sum_parts, sds((wide_rows // clip_size, chan_local), BF16), deps=(pack_pair,))(*wide_got)
 
     low_pair = call(
         functools.partial(last_norm, seg_count),
         (half_low,) * 2,
-        deps=(pack_pair, wide_part),
+        deps=(pack_pair,),
         ints=ints,
         floats=floats,
     )(slope_one_low, slope_one_oth, act_one, act_one_oth.array, got_one, got_back_one, small_own, small_oth)
@@ -1133,13 +1135,13 @@
     pack_other = swap_clip(pack_pair, 1)
     reduce_keep, reduce_send = call(
         reduce_gradient,
-        (Loose((chan_local // 2, mid_width), BF16), Loose((chan_local // 2, mid_width), BF16)),
+        (sds((chan_local // 2, mid_width), BF16), Loose((chan_local // 2, mid_width), BF16)),
         [pltpu.VMEM((chan_local, mid_width), BF16)],
         ints=ints,
     )(x_own, *low_pair, x_oth, *near_pair)
 
     share = chan_local // clip_size
-    loose_blocks = (Loose((pack_rows // clip_size, mid_local), BF16),) * places
+    loose_blocks = (sds((pack_rows // clip_size, mid_local), BF16),) * places
     pack_blocks = call(
         sum_blocks,
         loose_blocks,

time: 245 us -> 239 us (0.976)
  local copies, waits for them, and re-layouts: 14.6 us -> 9.62 us
  starting transfers between devices: 69.3 us -> 72.9 us
  waiting for transfers between devices: 51.3 us -> 48.3 us
    unnamed x42 -> x32, local copies, waits for them, and re-layouts: 5.99 us -> 1.06 us
    all_to_all x3, waiting for transfers between devices: 7.33 us -> 3.07 us  [share_all(): got = lax.all_to_all(sent, ('clip', 'chan'), 0, 0)]
    ppermute x21 -> x23, starting transfers between devices: 14.5 us -> 16.1 us  [swap(): lax.ppermute(array, 'chan', [(i, i ^ bits) for i in range(chan_size)])]
    ppermute x21 -> x23, waiting for transfers between devices: 9.18 us -> 9.46 us  [swap(): lax.ppermute(array, 'chan', [(i, i ^ bits) for i in range(chan_size)])]
  transfers between devices with their start and end apart: 50 -> 52, of which waited for: 17 -> 18; matrix products, arithmetic and copies ran while one was open for 7% -> 7% of each run, Pallas kernels for 26% -> 29%
where the time goes in v4:
time: 239 us; the launch traced here: 238 us
  Pallas kernels  83.8 us (35%)
  starting transfers between devices  72.9 us (31%)
  waiting for transfers between devices  48.3 us (20%)
  blocking collectives  11.7 us (5%)
  local copies, waits for them, and re-layouts  9.62 us (4%)
  other arithmetic  7.99 us (3%)
    pallas_call x30, Pallas kernels, run(): pl.pallas_call(kernel, out_shape=outs, in_specs=[SMEM] * len(scalars) + [...  83.8 us
    ppermute x25, starting transfers between devices, swap_clip(): lax.ppermute(array, 'clip', [(i, i ^ bits) for i in range(clip_size)])  38.3 us
    ppermute x25, waiting for transfers between devices, swap_clip(): lax.ppermute(array, 'clip', [(i, i ^ bits) for i in range(clip_size)])  27.6 us
    ppermute x23, starting transfers between devices, swap(): lax.ppermute(array, 'chan', [(i, i ^ bits) for i in range(chan_size)])  16.1 us
    all_to_all x3, starting transfers between devices, share_all(): got = lax.all_to_all(sent, ('clip', 'chan'), 0, 0)  14.4 us
    all_to_all x1, blocking collectives, share_all(): got = lax.all_to_all(sent, ('clip', 'chan'), 0, 0)  11.7 us
    ppermute x23, waiting for transfers between devices, swap(): lax.ppermute(array, 'chan', [(i, i ^ bits) for i in range(chan_size)])  9.46 us
    all_to_all x1, waiting for transfers between devices, per_device(): reduce_got = lax.all_to_all(columns, ('clip', 'chan'), 0, 0)  8.21 us
  transfers between devices with their start and end apart: 52, of which 18 were waited for; matrix products, arithmetic and copies ran while one was open for 7% of the time, Pallas kernels for 29%

profile of v4, /device:TPU:0, one launch (start us, length us, event | category | flops | bytes accessed | tf_op | source)
XLA Modules:
  0.0 237.9 jit_solution(5089260148620476858)
XLA Ops:
  2.5 2.9 %collective-permute-start.2 = (bf16[608,128]{1,0:T(8,128)(2,1)S(1)}, bf16[608,128]{1,0:T(8,128)(2,1)S(1)}, u32[]{:S(2)}, u32[]{:S(2)}) collective-permute-start(bf16[608,128]{1,0:T(8,128)(2,1)S(1)} %get-tuple-element.87), channel_id=1, source_target_pairs={{0,2},{1,3},{2,0},{3,1},{4,6},{5,7},{6,4},{7,5},{8,10},{9,11},{10,... | collective-permute-start | bytes 466952 | tf_op jit(solution)/shard_map/ppermute | solution.py:880
  8.1 3.0 %shard_map.289 = (bf16[784,256]{1,0:T(8,128)(2,1)S(1)}, f32[784,256]{1,0:T(8,128)S(1)}, bf16[512,256]{1,0:T(8,128)(2,1)}, f32[2,24,128]{2,1,0:T(8,128)}) custom-call(s32[6]{0:T(128)S(1)} %stack.19.refs_0_, bf16[608,128]{1,0:T(8,128)(2,1)S(1)} %get-tuple-element.83.refs_1_, bf16[608,128]{1,0:T(8,128)(2,1)S(1)} %collective-permute-done.refs_2_, ...), custom_call_target="tpu_custom_call" | custom-call | tf_op jit(solution)/shard_map/pallas_call | solution.py:179
  12.4 3.0 %shard_map.290 = (bf16[784,256]{1,0:T(8,128)(2,1)S(1)}, f32[784,256]{1,0:T(8,128)S(1)}, bf16[512,256]{1,0:T(8,128)(2,1)}, f32[2,24,128]{2,1,0:T(8,128)}) custom-call(s32[6]{0:T(128)S(1)} %stack.19.refs_0_, bf16[608,128]{1,0:T(8,128)(2,1)S(1)} %collective-permute-done.2.refs_1_, bf16[608,128]{1,0:T(8,128)(2,1)S(1)} %collective-permute-done.3.refs_2_, ...), custom_call_target="tpu_custom_call" | custom-call | tf_op jit(solution)/shard_map/pallas_call | solution.py:179
  22.5 6.5 %collective-permute-done.5.refs_3_ = bf16[784,256]{1,0:T(8,128)(2,1)S(1)} collective-permute-done((bf16[784,256]{1,0:T(8,128)(2,1)S(1)}, bf16[784,256]{1,0:T(8,128)(2,1)S(1)}, u32[]{:S(2)}, u32[]{:S(2)}) %collective-permute-start.5) | collective-permute-done | bytes 401440 | tf_op jit(solution)/shard_map/ppermute | solution.py:880
  32.2 4.9 %all-to-all-start = ((f32[32,2,256]{2,1,0:T(2,128)}), f32[32,2,256]{2,1,0:T(2,128)S(1)}, u32[]{:S(2)}, u32[]{:S(2)}) async-start(f32[32,2,256]{2,1,0:T(2,128)} %get-tuple-element.93), calls=%async_computation | async-start | bytes 131072 | tf_op jit(solution)/shard_map/all_to_all | solution.py:905
  42.1 2.5 %all-to-all-done = f32[32,2,256]{2,1,0:T(2,128)S(1)} async-done(((f32[32,2,256]{2,1,0:T(2,128)}), f32[32,2,256]{2,1,0:T(2,128)S(1)}, u32[]{:S(2)}, u32[]{:S(2)}) %all-to-all-start) | async-done | bytes 65568 | tf_op jit(solution)/shard_map/all_to_all | solution.py:905
  44.6 5.5 %shard_map.294 = (bf16[784,256]{1,0:T(8,128)(2,1)}, f32[32,2,256]{2,1,0:T(2,128)}, bf16[784,512]{1,0:T(8,128)(2,1)}) custom-call(s32[6]{0:T(128)S(1)} %stack.19.refs_0_, f32[3]{0:T(128)S(1)} %pad_maximum_fusion.2.refs_1_, bf16[784,256]{1,0:T(8,128)(2,1)} %get-tuple-element.92.refs_2_.refs_8_.refs_4_, ...), custom_call_target="tpu_custom_call" | custom-call | tf_op jit(solution)/shard_map/pallas_call | solution.py:179
  50.5 11.7 %all_to_all.25 = f32[32,2,256]{2,1,0:T(2,128)S(1)} all-to-all(f32[32,2,256]{2,1,0:T(2,128)} %get-tuple-element.96), channel_id=1, replica_groups=mesh['clip'=8,'chan'=4] {'clip','chan'}, dimensions={0} | all-to-all | bytes 131072 | tf_op jit(solution)/shard_map/all_to_all | solution.py:905
  75.4 2.6 %collective-permute-start.13 = (f32[3,512]{1,0:T(4,128)S(1)}, f32[3,512]{1,0:T(4,128)S(1)}, u32[]{:S(2)}, u32[]{:S(2)}) collective-permute-start(f32[3,512]{1,0:T(4,128)S(1)} %add.91), channel_id=1, source_target_pairs={{0,16},{4,20},{8,24},{12,28},{16,0},{20,4},{24,8},{28,12},{1,17},{... | collective-permute-start | bytes 18440 | tf_op jit(solution)/shard_map/ppermute | solution.py:893
  80.0 3.5 %collective-permute-done.14 = f32[3,512]{1,0:T(4,128)S(1)} collective-permute-done((f32[3,512]{1,0:T(4,128)S(1)}, f32[3,512]{1,0:T(4,128)S(1)}, u32[]{:S(2)}, u32[]{:S(2)}) %collective-permute-start.14) | collective-permute-done | bytes 6176 | tf_op jit(solution)/shard_map/ppermute | solution.py:893
  84.0 4.9 %shard_map.298 = (bf16[2,784,512]{2,1,0:T(8,128)(2,1)}, f32[2,784,512]{2,1,0:T(8,128)S(1)}, f32[2,512]{1,0:T(2,128)S(1)}, f32[2,512]{1,0:T(2,128)S(1)}) custom-call(s32[6]{0:T(128)S(1)} %stack.19.refs_0_, f32[3]{0:T(128)S(1)} %pad_maximum_fusion.2.refs_1_, f32[3,512]{1,0:T(4,128)} %add_add_fusion.refs_2_, f32[1,512]{1,0:T(1,128)} %bitcast.80, ...), custom_call_target="tpu_custom_call" | custom-call | tf_op jit(solution)/shard_map/pallas_call | solution.py:179
  94.0 3.0 %collective-permute-start.19 = (f32[2,512]{1,0:T(2,128)S(1)}, f32[2,512]{1,0:T(2,128)S(1)}, u32[]{:S(2)}, u32[]{:S(2)}) collective-permute-start(f32[2,512]{1,0:T(2,128)S(1)} %add.95), channel_id=1, source_target_pairs={{0,24},{4,28},{8,16},{12,20},{16,8},{20,12},{24,0},{28,4},{1,25},{... | collective-permute-start | bytes 12296 | tf_op jit(solution)/shard_map/ppermute | solution.py:893
  107.0 3.2 %shard_map.302 = (bf16[384,512]{1,0:T(8,128)(2,1)}, bf16[384,512]{1,0:T(8,128)(2,1)}) custom-call(s32[6]{0:T(128)S(1)} %stack.19.refs_0_, bf16[784,256]{1,0:T(8,128)(2,1)S(1)} %get-tuple-element.97.refs_1_, bf16[784,256]{1,0:T(8,128)(2,1)S(1)} %shard_map.296.refs_2_, bf16[784,256]{1,0:T(8,128)(2,1)S(1)} %collective-permute-done.9.refs_3_, ...), custom_call_target="tpu_custom_call" | custom-call | tf_op jit(solution)/shard_map/pallas_call | solution.py:179
  112.2 3.7 %shard_map.303.refs_11_.refs_12_ = bf16[3,1536,256]{2,1,0:T(8,128)(2,1)} custom-call(s32[6]{0:T(128)S(1)} %stack.19.refs_0_, bf16[3,1536,256]{2,1,0:T(8,128)(2,1)} %bitcast.74, bf16[9,256,128]{2,1,0:T(8,128)(2,1)S(1)} %collective-permute-done.15.refs_12_.refs_2_, bf16[9,256,128]{2,1,0:T(8,128)(2,1)S(1)} %collective-permute-done.22.refs_3_, ...), custom_call_target="tpu_custom_call" | custom-call | tf_op jit(solution)/shard_map/pallas_call | solution.py:179
  116.2 4.8 %shard_map.304 = (bf16[784,256]{1,0:T(8,128)(2,1)}, f32[32,4,256]{2,1,0:T(4,128)}, f32[32,256]{1,0:T(8,128)}) custom-call(s32[6]{0:T(128)S(1)} %stack.19.refs_0_, f32[3]{0:T(128)S(1)} %pad_maximum_fusion.2.refs_1_, f32[784,256]{1,0:T(8,128)S(1)} %get-tuple-element.103.refs_2_, bf16[784,512]{1,0:T(8,128)(2,1)S(1)} %collective-permute-done.20.refs_0_.refs_3_, ...), custom_call_target="tpu_custom_call" | custom-call | tf_op jit(solution)/shard_map/pallas_call | solution.py:179
  122.5 4.2 %all-to-all-start.2 = ((f32[32,4,256]{2,1,0:T(4,128)}), f32[32,4,256]{2,1,0:T(4,128)S(1)}, u32[]{:S(2)}, u32[]{:S(2)}) async-start(f32[32,4,256]{2,1,0:T(4,128)} %get-tuple-element.112), calls=%async_computation.2 | async-start | bytes 262144 | tf_op jit(solution)/shard_map/all_to_all | solution.py:905
  131.8 2.4 %collective-permute-start.31 = (bf16[96,512]{1,0:T(8,128)(2,1)}, bf16[96,512]{1,0:T(8,128)(2,1)}, u32[]{:S(2)}, u32[]{:S(2)}) collective-permute-start(bf16[96,512]{1,0:T(8,128)(2,1)} %get-tuple-element.125), channel_id=1, source_target_pairs={{0,16},{4,20},{8,24},{12,28},{16,0},{20,4},{24,8},{28,12},{1,17},{... | collective-permute-start | bytes 294920 | tf_op jit(solution)/shard_map/ppermute | solution.py:893
  134.9 5.8 %shard_map.306 = (bf16[784,256]{1,0:T(8,128)(2,1)}, f32[32,2,256]{2,1,0:T(2,128)}, bf16[928,128]{1,0:T(8,128)(2,1)}, bf16[304,128]{1,0:T(8,128)(2,1)}, bf16[304,...) custom-call(s32[6]{0:T(128)S(1)} %stack.19.refs_0_, f32[3]{0:T(128)S(1)} %pad_maximum_fusion.2.refs_1_, ...), custom_call_target="tpu_custom_call" | custom-call | tf_op jit(solution)/shard_map/pallas_call | solution.py:179
  141.5 5.2 %all-to-all-start.3 = ((f32[32,2,256]{2,1,0:T(2,128)}), f32[32,2,256]{2,1,0:T(2,128)S(1)}, u32[]{:S(2)}, u32[]{:S(2)}) async-start(f32[32,2,256]{2,1,0:T(2,128)} %get-tuple-element.119.refs_4_), calls=%async_computation.3 | async-start | bytes 131072 | tf_op jit(solution)/shard_map/all_to_all | solution.py:905
  150.4 8.0 %shard_map.308 = (bf16[2368,128]{1,0:T(8,128)(2,1)}, bf16[2368,128]{1,0:T(8,128)(2,1)}) custom-call(s32[6]{0:T(128)S(1)} %stack.19.refs_0_, bf16[784,512]{1,0:T(8,128)(2,1)} %get-tuple-element.117.refs_1_, bf16[928,128]{1,0:T(8,128)(2,1)} %get-tuple-element.120.refs_2_, bf16[784,512]{1,0:T(8,128)(2,1)} %collective-permute-done.25.refs_15_.refs_3_, ...), custom_call_target="tpu_custom_call" | custom-call | flops 20000000000 | tf_op jit(solution)/shard_map/pallas_call | solution.py:179
  159.8 2.7 %shard_map.309 = (bf16[784,256]{1,0:T(8,128)(2,1)}, bf16[784,256]{1,0:T(8,128)(2,1)}) custom-call(s32[6]{0:T(128)S(1)} %stack.19.refs_0_, f32[3]{0:T(128)S(1)} %pad_maximum_fusion.2.refs_1_, bf16[784,256]{1,0:T(8,128)(2,1)} %get-tuple-element.118.refs_2_, bf16[784,256]{1,0:T(8,128)(2,1)} %collective-permute-done.26.refs_3_, ...), custom_call_target="tpu_custom_call" | custom-call | flops 1000000000 | tf_op jit(solution)/shard_map/pallas_call | solution.py:179
  164.5 2.5 %collective-permute-start.41 = (bf16[96,512]{1,0:T(8,128)(2,1)}, bf16[96,512]{1,0:T(8,128)(2,1)}, u32[]{:S(2)}, u32[]{:S(2)}) collective-permute-start(bf16[96,512]{1,0:T(8,128)(2,1)} %shard_map.307.refs_7_.refs_1_), channel_id=1, source_target_pairs={{0,16},{4,20},{8,24},{12,28},{16,0},{20,4},{24,8},{28,12},{1,17},{... | collective-permute-start | bytes 294920 | tf_op jit(solution)/shard_map/ppermute | solution.py:893
  166.9 4.9 %shard_map.310 = (bf16[256,512]{1,0:T(8,128)(2,1)}, bf16[256,512]{1,0:T(8,128)(2,1)}) custom-call(s32[6]{0:T(128)S(1)} %stack.19.refs_0_, bf16[2,784,512]{2,1,0:T(8,128)(2,1)} %bitcast.70, bf16[784,256]{1,0:T(8,128)(2,1)} %get-tuple-element.128.refs_2_.refs_1_, bf16[784,256]{1,0:T(8,128)(2,1)} %get-tuple-element.129.refs_3_.refs_2_, ...), custom_call_target="tpu_custom_call" | custom-call | tf_op jit(solution)/shard_map/pallas_call | solution.py:179
  174.1 2.4 %shard_map.311 = (bf16[592,128]{1,0:T(8,128)(2,1)}, bf16[592,128]{1,0:T(8,128)(2,1)}, bf16[592,128]{1,0:T(8,128)(2,1)}, bf16[592,128]{1,0:T(8,128)(2,1)}) custom-call(s32[6]{0:T(128)S(1)} %stack.19.refs_0_, bf16[2368,128]{1,0:T(8,128)(2,1)} %get-tuple-element.134.refs_1_, bf16[2368,128]{1,0:T(8,128)(2,1)} %collective-permute-done.36.refs_2_, ...), custom_call_target="tpu_custom_call" | custom-call | tf_op jit(solution)/shard_map/pallas_call | solution.py:179
  178.6 2.9 %collective-permute-start.38 = (bf16[592,128]{1,0:T(8,128)(2,1)}, bf16[592,128]{1,0:T(8,128)(2,1)}, u32[]{:S(2)}, u32[]{:S(2)}) collective-permute-start(bf16[592,128]{1,0:T(8,128)(2,1)} %get-tuple-element.137), channel_id=1, source_target_pairs={{0,16},{4,20},{8,24},{12,28},{16,0},{20,4},{24,8},{28,12},{1,17},{... | collective-permute-start | bytes 454664 | tf_op jit(solution)/shard_map/ppermute | solution.py:893
  186.9 4.8 %collective-permute-done.38.refs_5_ = bf16[592,128]{1,0:T(8,128)(2,1)} collective-permute-done((bf16[592,128]{1,0:T(8,128)(2,1)}, bf16[592,128]{1,0:T(8,128)(2,1)}, u32[]{:S(2)}, u32[]{:S(2)}) %collective-permute-start.38) | collective-permute-done | bytes 151584 | tf_op jit(solution)/shard_map/ppermute | solution.py:893
  193.3 2.4 %collective-permute-start.43 = (bf16[848,128]{1,0:T(8,128)(2,1)S(1)}, bf16[848,128]{1,0:T(8,128)(2,1)S(1)}, u32[]{:S(2)}, u32[]{:S(2)}) collective-permute-start(bf16[848,128]{1,0:T(8,128)(2,1)S(1)} %get-tuple-element.140), channel_id=1, source_target_pairs={{0,8},{4,12},{8,0},{12,4},{16,24},{20,28},{24,16},{28,20},{1,9},{5... | collective-permute-start | bytes 651272 | tf_op jit(solution)/shard_map/ppermute | solution.py:893
  198.7 4.0 %shard_map.314.refs_6_ = f32[2,784,512]{2,1,0:T(8,128)} custom-call(s32[6]{0:T(128)S(1)} %stack.19.refs_0_, bf16[784,256]{1,0:T(8,128)(2,1)} %get-tuple-element.128.refs_2_.refs_1_, bf16[784,256]{1,0:T(8,128)(2,1)} %get-tuple-element.129.refs_3_.refs_2_, bf16[512,256]{1,0:T(8,128)(2,1)} %get-tuple-element.130.refs_3_, ...), custom_call_target="tpu_custom_call" | custom-call | tf_op jit(solution)/shard_map/pallas_call | solution.py:179
  202.7 10.4 %collective-permute-done.44.refs_3_ = bf16[848,128]{1,0:T(8,128)(2,1)S(1)} collective-permute-done((bf16[848,128]{1,0:T(8,128)(2,1)S(1)}, bf16[848,128]{1,0:T(8,128)(2,1)S(1)}, u32[]{:S(2)}, u32[]{:S(2)}) %collective-permute-start.44) | collective-permute-done | bytes 217120 | tf_op jit(solution)/shard_map/ppermute | solution.py:893
  217.0 4.1 %all-to-all-start.4 = ((bf16[32,64,128]{2,1,0:T(8,128)(2,1)}), bf16[32,64,128]{2,1,0:T(8,128)(2,1)S(1)}, u32[]{:S(2)}, u32[]{:S(2)}) async-start(bf16[32,64,128]{2,1,0:T(8,128)(2,1)} %get-tuple-element.143), calls=%async_computation.4 | async-start | bytes 1048576 | tf_op jit(solution)/shard_map/all_to_all | solution.py:1177
  222.1 2.3 shard_map.317
  228.5 8.2 %all-to-all-done.4 = bf16[32,64,128]{2,1,0:T(8,128)(2,1)S(1)} async-done(((bf16[32,64,128]{2,1,0:T(8,128)(2,1)}), bf16[32,64,128]{2,1,0:T(8,128)(2,1)S(1)}, u32[]{:S(2)}, u32[]{:S(2)}) %all-to-all-start.4) | async-done | bytes 524320 | tf_op jit(solution)/shard_map/all_to_all | solution.py:1177
  (167 shorter events, 93.1 us)
Async XLA Ops:
  0.7 18.5 %collective-permute-start.6 = (bf16[9,512,128]{2,1,0:T(8,128)(2,1)}, bf16[9,512,128]{2,1,0:T(8,128)(2,1)}, u32[]{:S(2)}, u32[]{:S(2)}) collective-permute-start(bf16[9,512,128]{2,1,0:T(8,128)(2,1)} %refs_1_.3), channel_id=1, source_target_pairs={{0,1},{1,0},{2,3},{3,2},{4,5},{5,4},{6,7},{7,6},{8,9},{9,8},{10,11... | collective-permute-start | bytes 3538952 | tf_op jit(solution)/shard_map/ppermute | solution.py:880
  17.3 11.6 %collective-permute-start.5 = (bf16[784,256]{1,0:T(8,128)(2,1)S(1)}, bf16[784,256]{1,0:T(8,128)(2,1)S(1)}, u32[]{:S(2)}, u32[]{:S(2)}) collective-permute-start(bf16[784,256]{1,0:T(8,128)(2,1)S(1)} %shard_map.291), channel_id=1, source_target_pairs={{0,2},{1,3},{2,0},{3,1},{4,6},{5,7},{6,4},{7,5},{8,10},{9,11},{10,... | collective-permute-start | bytes 1204232 | tf_op jit(solution)/shard_map/ppermute | solution.py:880
  30.5 14.1 %collective-permute-start.7 = (bf16[784,256]{1,0:T(8,128)(2,1)}, bf16[784,256]{1,0:T(8,128)(2,1)S(1)}, u32[]{:S(2)}, u32[]{:S(2)}) collective-permute-start(bf16[784,256]{1,0:T(8,128)(2,1)} %get-tuple-element.92.refs_2_.refs_8_.refs_4_), channel_id=1, source_target_pairs={{0,2},{1,3},{2,0},{3,1},{4,6},{5,7},{6,4},{7,5},{8,10},{9,11},{10,... | collective-permute-start | bytes 1204232 | tf_op jit(solution)/shard_map/ppermute | solution.py:880
  32.2 12.3 %all-to-all-start = ((f32[32,2,256]{2,1,0:T(2,128)}), f32[32,2,256]{2,1,0:T(2,128)S(1)}, u32[]{:S(2)}, u32[]{:S(2)}) async-start(f32[32,2,256]{2,1,0:T(2,128)} %get-tuple-element.93), calls=%async_computation | async-start | bytes 131072 | tf_op jit(solution)/shard_map/all_to_all | solution.py:905
  50.1 14.6 %collective-permute-start.8 = (bf16[784,256]{1,0:T(8,128)(2,1)}, bf16[784,256]{1,0:T(8,128)(2,1)S(1)}, u32[]{:S(2)}, u32[]{:S(2)}) collective-permute-start(bf16[784,256]{1,0:T(8,128)(2,1)} %get-tuple-element.95.refs_2_.refs_7_.refs_4_), channel_id=1, source_target_pairs={{0,2},{1,3},{2,0},{3,1},{4,6},{5,7},{6,4},{7,5},{8,10},{9,11},{10,... | collective-permute-start | bytes 1204232 | tf_op jit(solution)/shard_map/ppermute | solution.py:880
  67.2 16.9 %collective-permute-start.15 = (bf16[9,256,128]{2,1,0:T(8,128)(2,1)S(1)}, bf16[9,256,128]{2,1,0:T(8,128)(2,1)S(1)}, u32[]{:S(2)}, u32[]{:S(2)}) collective-permute-start(bf16[9,256,128]{2,1,0:T(8,128)(2,1)S(1)} %copy-done.11), channel_id=1, source_target_pairs={{0,2},{1,3},{2,0},{3,1},{4,6},{5,7},{6,4},{7,5},{8,10},{9,11},{10,... | collective-permute-start | bytes 1769480 | tf_op jit(solution)/shard_map/ppermute | solution.py:880
  101.9 10.4 %collective-permute-start.22 = (bf16[9,256,128]{2,1,0:T(8,128)(2,1)S(1)}, bf16[9,256,128]{2,1,0:T(8,128)(2,1)S(1)}, u32[]{:S(2)}, u32[]{:S(2)}) collective-permute-start(bf16[9,256,128]{2,1,0:T(8,128)(2,1)S(1)} %collective-permute-done.15.refs_12_.refs_2_), channel_id=1, source_target_pairs={{0,1},{1,0},{2,3},{3,2},{4,5},{5,4},{6,7},{7,6},{8,9},{9,8},{10,11... | collective-permute-start | bytes 1769480 | tf_op jit(solution)/shard_map/ppermute | solution.py:880
  102.4 32.0 %collective-permute-start.25 = (bf16[784,512]{1,0:T(8,128)(2,1)}, bf16[784,512]{1,0:T(8,128)(2,1)}, u32[]{:S(2)}, u32[]{:S(2)}) collective-permute-start(bf16[784,512]{1,0:T(8,128)(2,1)} %get-tuple-element.117.refs_1_), channel_id=1, source_target_pairs={{0,1},{1,0},{2,3},{3,2},{4,5},{5,4},{6,7},{7,6},{8,9},{9,8},{10,11... | collective-permute-start | bytes 2408456 | tf_op jit(solution)/shard_map/ppermute | solution.py:880
  104.5 11.7 %collective-permute-start.21 = (bf16[784,256]{1,0:T(8,128)(2,1)S(1)}, bf16[784,256]{1,0:T(8,128)(2,1)S(1)}, u32[]{:S(2)}, u32[]{:S(2)}) collective-permute-start(bf16[784,256]{1,0:T(8,128)(2,1)S(1)} %shard_map.301), channel_id=1, source_target_pairs={{0,2},{1,3},{2,0},{3,1},{4,6},{5,7},{6,4},{7,5},{8,10},{9,11},{10,... | collective-permute-start | bytes 1204232 | tf_op jit(solution)/shard_map/ppermute | solution.py:880
  110.2 17.7 %collective-permute-start.24 = (bf16[384,512]{1,0:T(8,128)(2,1)}, bf16[384,512]{1,0:T(8,128)(2,1)}, u32[]{:S(2)}, u32[]{:S(2)}) collective-permute-start(bf16[384,512]{1,0:T(8,128)(2,1)} %get-tuple-element.111.refs_4_), channel_id=1, source_target_pairs={{0,4},{4,0},{8,12},{12,8},{16,20},{20,16},{24,28},{28,24},{1,5},{5... | collective-permute-start | bytes 1179656 | tf_op jit(solution)/shard_map/ppermute | solution.py:893
  121.0 13.9 %collective-permute-start.23 = (bf16[784,256]{1,0:T(8,128)(2,1)}, bf16[784,256]{1,0:T(8,128)(2,1)}, u32[]{:S(2)}, u32[]{:S(2)}) collective-permute-start(bf16[784,256]{1,0:T(8,128)(2,1)} %get-tuple-element.113.refs_2_), channel_id=1, source_target_pairs={{0,2},{1,3},{2,0},{3,1},{4,6},{5,7},{6,4},{7,5},{8,10},{9,11},{10,... | collective-permute-start | bytes 1204232 | tf_op jit(solution)/shard_map/ppermute | solution.py:880
  122.5 12.5 %all-to-all-start.2 = ((f32[32,4,256]{2,1,0:T(4,128)}), f32[32,4,256]{2,1,0:T(4,128)S(1)}, u32[]{:S(2)}, u32[]{:S(2)}) async-start(f32[32,4,256]{2,1,0:T(4,128)} %get-tuple-element.112), calls=%async_computation.2 | async-start | bytes 262144 | tf_op jit(solution)/shard_map/all_to_all | solution.py:905
  130.0 11.3 %collective-permute-start.30 = (bf16[96,512]{1,0:T(8,128)(2,1)}, bf16[96,512]{1,0:T(8,128)(2,1)}, u32[]{:S(2)}, u32[]{:S(2)}) collective-permute-start(bf16[96,512]{1,0:T(8,128)(2,1)} %get-tuple-element.124), channel_id=1, source_target_pairs={{0,8},{4,12},{8,0},{12,4},{16,24},{20,28},{24,16},{28,20},{1,9},{5... | collective-permute-start | bytes 294920 | tf_op jit(solution)/shard_map/ppermute | solution.py:893
  131.8 15.0 %collective-permute-start.31 = (bf16[96,512]{1,0:T(8,128)(2,1)}, bf16[96,512]{1,0:T(8,128)(2,1)}, u32[]{:S(2)}, u32[]{:S(2)}) collective-permute-start(bf16[96,512]{1,0:T(8,128)(2,1)} %get-tuple-element.125), channel_id=1, source_target_pairs={{0,16},{4,20},{8,24},{12,28},{16,0},{20,4},{24,8},{28,12},{1,17},{... | collective-permute-start | bytes 294920 | tf_op jit(solution)/shard_map/ppermute | solution.py:893
  134.2 14.4 %collective-permute-start.32 = (bf16[96,512]{1,0:T(8,128)(2,1)}, bf16[96,512]{1,0:T(8,128)(2,1)}, u32[]{:S(2)}, u32[]{:S(2)}) collective-permute-start(bf16[96,512]{1,0:T(8,128)(2,1)} %get-tuple-element.126), channel_id=1, source_target_pairs={{0,24},{4,28},{8,16},{12,20},{16,8},{20,12},{24,0},{28,4},{1,25},{... | collective-permute-start | bytes 294920 | tf_op jit(solution)/shard_map/ppermute | solution.py:893
  140.8 9.6 %collective-permute-start.29 = (bf16[320,128]{1,0:T(8,128)(2,1)}, bf16[320,128]{1,0:T(8,128)(2,1)}, u32[]{:S(2)}, u32[]{:S(2)}) collective-permute-start(bf16[320,128]{1,0:T(8,128)(2,1)} %get-tuple-element.123), channel_id=1, source_target_pairs={{0,1},{1,0},{2,3},{3,2},{4,5},{5,4},{6,7},{7,6},{8,9},{9,8},{10,11... | collective-permute-start | bytes 245768 | tf_op jit(solution)/shard_map/ppermute | solution.py:880
  141.0 9.3 %collective-permute-start.27 = (bf16[304,128]{1,0:T(8,128)(2,1)}, bf16[304,128]{1,0:T(8,128)(2,1)}, u32[]{:S(2)}, u32[]{:S(2)}) collective-permute-start(bf16[304,128]{1,0:T(8,128)(2,1)} %get-tuple-element.121), channel_id=1, source_target_pairs={{0,1},{1,0},{2,3},{3,2},{4,5},{5,4},{6,7},{7,6},{8,9},{9,8},{10,11... | collective-permute-start | bytes 233480 | tf_op jit(solution)/shard_map/ppermute | solution.py:880
  141.5 18.2 %all-to-all-start.3 = ((f32[32,2,256]{2,1,0:T(2,128)}), f32[32,2,256]{2,1,0:T(2,128)S(1)}, u32[]{:S(2)}, u32[]{:S(2)}) async-start(f32[32,2,256]{2,1,0:T(2,128)} %get-tuple-element.119.refs_4_), calls=%async_computation.3 | async-start | bytes 131072 | tf_op jit(solution)/shard_map/all_to_all | solution.py:905
  146.8 13.0 %collective-permute-start.26 = (bf16[784,256]{1,0:T(8,128)(2,1)}, bf16[784,256]{1,0:T(8,128)(2,1)}, u32[]{:S(2)}, u32[]{:S(2)}) collective-permute-start(bf16[784,256]{1,0:T(8,128)(2,1)} %get-tuple-element.118.refs_2_), channel_id=1, source_target_pairs={{0,2},{1,3},{2,0},{3,1},{4,6},{5,7},{6,4},{7,5},{8,10},{9,11},{10,... | collective-permute-start | bytes 1204232 | tf_op jit(solution)/shard_map/ppermute | solution.py:880
  158.3 15.8 %collective-permute-start.36 = (bf16[2368,128]{1,0:T(8,128)(2,1)}, bf16[2368,128]{1,0:T(8,128)(2,1)}, u32[]{:S(2)}, u32[]{:S(2)}) collective-permute-start(bf16[2368,128]{1,0:T(8,128)(2,1)} %get-tuple-element.127.refs_10_), channel_id=1, source_target_pairs={{0,4},{4,0},{8,12},{12,8},{16,20},{20,16},{24,28},{28,24},{1,5},{5... | collective-permute-start | bytes 1818632 | tf_op jit(solution)/shard_map/ppermute | solution.py:893
  163.0 15.6 %collective-permute-start.40 = (bf16[96,512]{1,0:T(8,128)(2,1)}, bf16[96,512]{1,0:T(8,128)(2,1)}, u32[]{:S(2)}, u32[]{:S(2)}) collective-permute-start(bf16[96,512]{1,0:T(8,128)(2,1)} %shard_map.307.refs_7_.refs_1_), channel_id=1, source_target_pairs={{0,8},{4,12},{8,0},{12,4},{16,24},{20,28},{24,16},{28,20},{1,9},{5... | collective-permute-start | bytes 294920 | tf_op jit(solution)/shard_map/ppermute | solution.py:893
  164.5 17.0 %collective-permute-start.41 = (bf16[96,512]{1,0:T(8,128)(2,1)}, bf16[96,512]{1,0:T(8,128)(2,1)}, u32[]{:S(2)}, u32[]{:S(2)}) collective-permute-start(bf16[96,512]{1,0:T(8,128)(2,1)} %shard_map.307.refs_7_.refs_1_), channel_id=1, source_target_pairs={{0,16},{4,20},{8,24},{12,28},{16,0},{20,4},{24,8},{28,12},{1,17},{... | collective-permute-start | bytes 294920 | tf_op jit(solution)/shard_map/ppermute | solution.py:893
  171.9 19.8 %collective-permute-start.35 = (bf16[256,512]{1,0:T(8,128)(2,1)}, bf16[256,512]{1,0:T(8,128)(2,1)}, u32[]{:S(2)}, u32[]{:S(2)}) collective-permute-start(bf16[256,512]{1,0:T(8,128)(2,1)} %get-tuple-element.133.refs_3_), channel_id=1, source_target_pairs={{0,4},{4,0},{8,12},{12,8},{16,20},{20,16},{24,28},{28,24},{1,5},{5... | collective-permute-start | bytes 786440 | tf_op jit(solution)/shard_map/ppermute | solution.py:893
  176.5 10.4 %collective-permute-start.37 = (bf16[592,128]{1,0:T(8,128)(2,1)}, bf16[592,128]{1,0:T(8,128)(2,1)}, u32[]{:S(2)}, u32[]{:S(2)}) collective-permute-start(bf16[592,128]{1,0:T(8,128)(2,1)} %get-tuple-element.136), channel_id=1, source_target_pairs={{0,8},{4,12},{8,0},{12,4},{16,24},{20,28},{24,16},{28,20},{1,9},{5... | collective-permute-start | bytes 454664 | tf_op jit(solution)/shard_map/ppermute | solution.py:893
  178.6 13.2 %collective-permute-start.38 = (bf16[592,128]{1,0:T(8,128)(2,1)}, bf16[592,128]{1,0:T(8,128)(2,1)}, u32[]{:S(2)}, u32[]{:S(2)}) collective-permute-start(bf16[592,128]{1,0:T(8,128)(2,1)} %get-tuple-element.137), channel_id=1, source_target_pairs={{0,16},{4,20},{8,24},{12,28},{16,0},{20,4},{24,8},{28,12},{1,17},{... | collective-permute-start | bytes 454664 | tf_op jit(solution)/shard_map/ppermute | solution.py:893
  181.5 10.2 %collective-permute-start.39 = (bf16[592,128]{1,0:T(8,128)(2,1)}, bf16[592,128]{1,0:T(8,128)(2,1)}, u32[]{:S(2)}, u32[]{:S(2)}) collective-permute-start(bf16[592,128]{1,0:T(8,128)(2,1)} %get-tuple-element.138), channel_id=1, source_target_pairs={{0,24},{4,28},{8,16},{12,20},{16,8},{20,12},{24,0},{28,4},{1,25},{... | collective-permute-start | bytes 454664 | tf_op jit(solution)/shard_map/ppermute | solution.py:893
  184.0 18.8 %collective-permute-start.46 = (bf16[384,512]{1,0:T(8,128)(2,1)}, bf16[384,512]{1,0:T(8,128)(2,1)S(1)}, u32[]{:S(2)}, u32[]{:S(2)}) collective-permute-start(bf16[384,512]{1,0:T(8,128)(2,1)} %shard_map.312.refs_7_.refs_1_), channel_id=1, source_target_pairs={{0,4},{4,0},{8,12},{12,8},{16,20},{20,16},{24,28},{28,24},{1,5},{5... | collective-permute-start | bytes 1179656 | tf_op jit(solution)/shard_map/ppermute | solution.py:893
  193.3 9.4 %collective-permute-start.43 = (bf16[848,128]{1,0:T(8,128)(2,1)S(1)}, bf16[848,128]{1,0:T(8,128)(2,1)S(1)}, u32[]{:S(2)}, u32[]{:S(2)}) collective-permute-start(bf16[848,128]{1,0:T(8,128)(2,1)S(1)} %get-tuple-element.140), channel_id=1, source_target_pairs={{0,8},{4,12},{8,0},{12,4},{16,24},{20,28},{24,16},{28,20},{1,9},{5... | collective-permute-start | bytes 651272 | tf_op jit(solution)/shard_map/ppermute | solution.py:893
  195.7 17.5 %collective-permute-start.44 = (bf16[848,128]{1,0:T(8,128)(2,1)S(1)}, bf16[848,128]{1,0:T(8,128)(2,1)S(1)}, u32[]{:S(2)}, u32[]{:S(2)}) collective-permute-start(bf16[848,128]{1,0:T(8,128)(2,1)S(1)} %get-tuple-element.141), channel_id=1, source_target_pairs={{0,16},{4,20},{8,24},{12,28},{16,0},{20,4},{24,8},{28,12},{1,17},{... | collective-permute-start | bytes 651272 | tf_op jit(solution)/shard_map/ppermute | solution.py:893
  196.6 16.5 %collective-permute-start.45 = (bf16[848,128]{1,0:T(8,128)(2,1)S(1)}, bf16[848,128]{1,0:T(8,128)(2,1)S(1)}, u32[]{:S(2)}, u32[]{:S(2)}) collective-permute-start(bf16[848,128]{1,0:T(8,128)(2,1)S(1)} %get-tuple-element.142), channel_id=1, source_target_pairs={{0,24},{4,28},{8,16},{12,20},{16,8},{20,12},{24,0},{28,4},{1,25},{... | collective-permute-start | bytes 651272 | tf_op jit(solution)/shard_map/ppermute | solution.py:893
  214.6 11.7 %collective-permute-start.47 = (bf16[2368,128]{1,0:T(8,128)(2,1)S(1)}, bf16[2368,128]{1,0:T(8,128)(2,1)S(1)}, u32[]{:S(2)}, u32[]{:S(2)}) collective-permute-start(bf16[2368,128]{1,0:T(8,128)(2,1)S(1)} %get-tuple-element.144.refs_1_.refs_3_), channel_id=1, source_target_pairs={{0,4},{4,0},{8,12},{12,8},{16,20},{20,16},{24,28},{28,24},{1,5},{5... | collective-permute-start | bytes 1818632 | tf_op jit(solution)/shard_map/ppermute | solution.py:893
  217.0 19.7 %all-to-all-start.4 = ((bf16[32,64,128]{2,1,0:T(8,128)(2,1)}), bf16[32,64,128]{2,1,0:T(8,128)(2,1)S(1)}, u32[]{:S(2)}, u32[]{:S(2)}) async-start(bf16[32,64,128]{2,1,0:T(8,128)(2,1)} %get-tuple-element.143), calls=%async_computation.4 | async-start | bytes 1048576 | tf_op jit(solution)/shard_map/all_to_all | solution.py:1177
  (36 other events, 321.7 us)

commit v5 on v4

--- a/solution.py
+++ b/solution.py
@@ -270,16 +270,17 @@
             ref[size + 32 * index : size + 32 * (index + 1), :] = piece
 
 
-def reduce_side(ints_ref, first_ref, second_ref, x_oth_ref, x_own_ref, oth_ref, own_ref, w_ref, *small_refs):
+def reduce_side(ints_ref, first_ref, second_ref, x_oth_ref, x_own_ref, oth_ref, own_ref, w_ref, small_ref, *kept_refs):
     core = ints_ref[3]
     rows, size = w_ref.shape[0], first_ref.shape[1]
     for index, ref in ((core, first_ref), (1 - core, second_ref)):
         w_ref[:, pl.ds(pl.multiple_of(index * size, size), size)] = ref[:rows, :]
-        for small_ref in small_refs:
-            pieces = [ref[rows + 32 * piece : rows + 32 * (piece + 1), :].astype(F32) for piece in range(3)]
-            small_ref[index] = (pieces[0] + (pieces[1] + pieces[2]))[:24]
+        pieces = [ref[rows + 32 * piece : rows + 32 * (piece + 1), :].astype(F32) for piece in range(3)]
+        small_ref[index] = (pieces[0] + (pieces[1] + pieces[2]))[:24]
     oth_ref[...] = dot32(x_oth_ref[...], w_ref[...]).astype(BF16)
     own_ref[...] = dot32(x_own_ref[...], w_ref[...])
+    for ref, kept_ref in zip((x_oth_ref, x_own_ref), kept_refs):
+        kept_ref[...] = ref[...]
 
 
 def add_near(own_ref, near_ref, out_ref):
@@ -934,7 +935,7 @@
     )
     got_blocks = {bits: swap(sent_blocks[bits], bits) for bits in (2, 3, 1)}
 
-    def side_call(first, second, deps=()):
+    def side_call(first, second, frames, kept=()):
         return call(
             reduce_side,
             (
@@ -942,14 +943,15 @@
                 near((row_count, half), F32),
                 sds((chan_local, half), BF16),
                 sds((2, 24, mid_local), F32),
-            ),
-            deps=deps,
+            )
+            + kept,
             ints=ints,
-        )(first, second, x_oth, x_own)
-
-    oth_one, own_one, w_own_side, small_own = side_call(sent_blocks[0], got_blocks[1])
+        )(first, second, *frames)
+
+    kept = (near((row_count, chan_local), BF16),) * 2
+    oth_one, own_one, w_own_side, small_own, *frames = side_call(sent_blocks[0], got_blocks[1], (x_oth, x_own), kept)
     near_one = swap(oth_one, 1)
-    oth_far, own_far, w_oth_side, small_oth = side_call(got_blocks[2], got_blocks[3], (small_own,))
+    oth_far, own_far, w_oth_side, small_oth = side_call(got_blocks[2], got_blocks[3], frames)
     far_one = swap(call(add_near, near((row_count, half), BF16))(own_far, swap(oth_far, 1)), 2)
 
     w_pair = jnp.concatenate(pair(w_spatial, swap(w_spatial, 1).array), axis=2)

time: 239 us -> 238 us (level)
  no operation moved by 1% of the time
where the time goes in v5:
time: 238 us; the launch traced here: 236 us
  Pallas kernels  82.6 us (35%)
  starting transfers between devices  72.8 us (31%)
  waiting for transfers between devices  48.2 us (20%)
  blocking collectives  11.7 us (5%)
  local copies, waits for them, and re-layouts  9.62 us (4%)
  other arithmetic  7.99 us (3%)
    pallas_call x30, Pallas kernels, run(): pl.pallas_call(kernel, out_shape=outs, in_specs=[SMEM] * len(scalars) + [...  82.6 us
    ppermute x25, starting transfers between devices, swap_clip(): lax.ppermute(array, 'clip', [(i, i ^ bits) for i in range(clip_size)])  38.3 us
    ppermute x25, waiting for transfers between devices, swap_clip(): lax.ppermute(array, 'clip', [(i, i ^ bits) for i in range(clip_size)])  27.5 us
    ppermute x23, starting transfers between devices, swap(): lax.ppermute(array, 'chan', [(i, i ^ bits) for i in range(chan_size)])  16.1 us
    all_to_all x3, starting transfers between devices, share_all(): got = lax.all_to_all(sent, ('clip', 'chan'), 0, 0)  14.4 us
    all_to_all x1, blocking collectives, share_all(): got = lax.all_to_all(sent, ('clip', 'chan'), 0, 0)  11.7 us
    ppermute x23, waiting for transfers between devices, swap(): lax.ppermute(array, 'chan', [(i, i ^ bits) for i in range(chan_size)])  9.35 us
    all_to_all x1, waiting for transfers between devices, per_device(): reduce_got = lax.all_to_all(columns, ('clip', 'chan'), 0, 0)  8.22 us
  transfers between devices with their start and end apart: 52, of which 18 were waited for; matrix products, arithmetic and copies ran while one was open for 7% of the time, Pallas kernels for 29%

profile of v5, /device:TPU:0, one launch (start us, length us, event | category | flops | bytes accessed | tf_op | source)
XLA Modules:
  0.0 236.5 jit_solution(59562945696110170)
XLA Ops:
  2.5 2.9 %collective-permute-start.2 = (bf16[608,128]{1,0:T(8,128)(2,1)S(1)}, bf16[608,128]{1,0:T(8,128)(2,1)S(1)}, u32[]{:S(2)}, u32[]{:S(2)}) collective-permute-start(bf16[608,128]{1,0:T(8,128)(2,1)S(1)} %get-tuple-element.89), channel_id=1, source_target_pairs={{0,2},{1,3},{2,0},{3,1},{4,6},{5,7},{6,4},{7,5},{8,10},{9,11},{10,... | collective-permute-start | bytes 466952 | tf_op jit(solution)/shard_map/ppermute | solution.py:881
  8.1 3.1 %shard_map.289 = (bf16[784,256]{1,0:T(8,128)(2,1)S(1)}, f32[784,256]{1,0:T(8,128)S(1)}, bf16[512,256]{1,0:T(8,128)(2,1)}, f32[2,24,128]{2,1,0:T(8,128)}, bf16[78...) custom-call(s32[6]{0:T(128)S(1)} %stack.19.refs_0_, bf16[608,128]{1,0:T(8,128)(2,1)S(1)} %get-tuple-element.85.refs_1_, ...), custom_call_target="tpu_custom_call" | custom-call | tf_op jit(solution)/shard_map/pallas_call | solution.py:179
  21.1 6.5 %collective-permute-done.5.refs_3_ = bf16[784,256]{1,0:T(8,128)(2,1)S(1)} collective-permute-done((bf16[784,256]{1,0:T(8,128)(2,1)S(1)}, bf16[784,256]{1,0:T(8,128)(2,1)S(1)}, u32[]{:S(2)}, u32[]{:S(2)}) %collective-permute-start.5) | collective-permute-done | bytes 401440 | tf_op jit(solution)/shard_map/ppermute | solution.py:881
  30.9 4.9 %all-to-all-start = ((f32[32,2,256]{2,1,0:T(2,128)}), f32[32,2,256]{2,1,0:T(2,128)S(1)}, u32[]{:S(2)}, u32[]{:S(2)}) async-start(f32[32,2,256]{2,1,0:T(2,128)} %get-tuple-element.96), calls=%async_computation | async-start | bytes 131072 | tf_op jit(solution)/shard_map/all_to_all | solution.py:906
  40.7 2.5 %all-to-all-done = f32[32,2,256]{2,1,0:T(2,128)S(1)} async-done(((f32[32,2,256]{2,1,0:T(2,128)}), f32[32,2,256]{2,1,0:T(2,128)S(1)}, u32[]{:S(2)}, u32[]{:S(2)}) %all-to-all-start) | async-done | bytes 65568 | tf_op jit(solution)/shard_map/all_to_all | solution.py:906
  43.2 5.5 %shard_map.294 = (bf16[784,256]{1,0:T(8,128)(2,1)}, f32[32,2,256]{2,1,0:T(2,128)}, bf16[784,512]{1,0:T(8,128)(2,1)}) custom-call(s32[6]{0:T(128)S(1)} %stack.19.refs_0_, f32[3]{0:T(128)S(1)} %pad_maximum_fusion.2.refs_1_, bf16[784,256]{1,0:T(8,128)(2,1)} %get-tuple-element.95.refs_2_.refs_8_.refs_4_, ...), custom_call_target="tpu_custom_call" | custom-call | tf_op jit(solution)/shard_map/pallas_call | solution.py:179
  49.2 11.7 %all_to_all.25 = f32[32,2,256]{2,1,0:T(2,128)S(1)} all-to-all(f32[32,2,256]{2,1,0:T(2,128)} %get-tuple-element.100), channel_id=1, replica_groups=mesh['clip'=8,'chan'=4] {'clip','chan'}, dimensions={0} | all-to-all | bytes 131072 | tf_op jit(solution)/shard_map/all_to_all | solution.py:906
  60.9 2.2 shard_map.295
  74.0 2.6 %collective-permute-start.13 = (f32[3,512]{1,0:T(4,128)S(1)}, f32[3,512]{1,0:T(4,128)S(1)}, u32[]{:S(2)}, u32[]{:S(2)}) collective-permute-start(f32[3,512]{1,0:T(4,128)S(1)} %add.91), channel_id=1, source_target_pairs={{0,16},{4,20},{8,24},{12,28},{16,0},{20,4},{24,8},{28,12},{1,17},{... | collective-permute-start | bytes 18440 | tf_op jit(solution)/shard_map/ppermute | solution.py:894
  78.6 3.5 %collective-permute-done.14 = f32[3,512]{1,0:T(4,128)S(1)} collective-permute-done((f32[3,512]{1,0:T(4,128)S(1)}, f32[3,512]{1,0:T(4,128)S(1)}, u32[]{:S(2)}, u32[]{:S(2)}) %collective-permute-start.14) | collective-permute-done | bytes 6176 | tf_op jit(solution)/shard_map/ppermute | solution.py:894
  82.7 4.9 %shard_map.298 = (bf16[2,784,512]{2,1,0:T(8,128)(2,1)}, f32[2,784,512]{2,1,0:T(8,128)S(1)}, f32[2,512]{1,0:T(2,128)S(1)}, f32[2,512]{1,0:T(2,128)S(1)}) custom-call(s32[6]{0:T(128)S(1)} %stack.19.refs_0_, f32[3]{0:T(128)S(1)} %pad_maximum_fusion.2.refs_1_, f32[3,512]{1,0:T(4,128)} %add_add_fusion.refs_2_, f32[1,512]{1,0:T(1,128)} %bitcast.78, ...), custom_call_target="tpu_custom_call" | custom-call | tf_op jit(solution)/shard_map/pallas_call | solution.py:179
  92.7 3.0 %collective-permute-start.19 = (f32[2,512]{1,0:T(2,128)S(1)}, f32[2,512]{1,0:T(2,128)S(1)}, u32[]{:S(2)}, u32[]{:S(2)}) collective-permute-start(f32[2,512]{1,0:T(2,128)S(1)} %add.95), channel_id=1, source_target_pairs={{0,24},{4,28},{8,16},{12,20},{16,8},{20,12},{24,0},{28,4},{1,25},{... | collective-permute-start | bytes 12296 | tf_op jit(solution)/shard_map/ppermute | solution.py:894
  105.7 3.2 %shard_map.302 = (bf16[384,512]{1,0:T(8,128)(2,1)}, bf16[384,512]{1,0:T(8,128)(2,1)}) custom-call(s32[6]{0:T(128)S(1)} %stack.19.refs_0_, bf16[784,256]{1,0:T(8,128)(2,1)S(1)} %get-tuple-element.101.refs_1_, bf16[784,256]{1,0:T(8,128)(2,1)S(1)} %shard_map.296.refs_2_, bf16[784,256]{1,0:T(8,128)(2,1)S(1)} %collective-permute-done.9.refs_3_, ...), custom_call_target="tpu_custom_call" | custom-call | tf_op jit(solution)/shard_map/pallas_call | solution.py:179
  110.9 3.7 %shard_map.303.refs_11_.refs_12_ = bf16[3,1536,256]{2,1,0:T(8,128)(2,1)} custom-call(s32[6]{0:T(128)S(1)} %stack.19.refs_0_, bf16[3,1536,256]{2,1,0:T(8,128)(2,1)} %bitcast.72, bf16[9,256,128]{2,1,0:T(8,128)(2,1)S(1)} %collective-permute-done.15.refs_12_.refs_2_, bf16[9,256,128]{2,1,0:T(8,128)(2,1)S(1)} %collective-permute-done.22.refs_3_, ...), custom_call_target="tpu_custom_call" | custom-call | tf_op jit(solution)/shard_map/pallas_call | solution.py:179
  114.8 4.8 %shard_map.304 = (bf16[784,256]{1,0:T(8,128)(2,1)}, f32[32,4,256]{2,1,0:T(4,128)}, f32[32,256]{1,0:T(8,128)}) custom-call(s32[6]{0:T(128)S(1)} %stack.19.refs_0_, f32[3]{0:T(128)S(1)} %pad_maximum_fusion.2.refs_1_, f32[784,256]{1,0:T(8,128)S(1)} %get-tuple-element.107.refs_2_, bf16[784,512]{1,0:T(8,128)(2,1)S(1)} %collective-permute-done.20.refs_0_.refs_3_, ...), custom_call_target="tpu_custom_call" | custom-call | tf_op jit(solution)/shard_map/pallas_call | solution.py:179
  121.1 4.2 %all-to-all-start.2 = ((f32[32,4,256]{2,1,0:T(4,128)}), f32[32,4,256]{2,1,0:T(4,128)S(1)}, u32[]{:S(2)}, u32[]{:S(2)}) async-start(f32[32,4,256]{2,1,0:T(4,128)} %get-tuple-element.116), calls=%async_computation.2 | async-start | bytes 262144 | tf_op jit(solution)/shard_map/all_to_all | solution.py:906
  130.4 2.4 %collective-permute-start.31 = (bf16[96,512]{1,0:T(8,128)(2,1)}, bf16[96,512]{1,0:T(8,128)(2,1)}, u32[]{:S(2)}, u32[]{:S(2)}) collective-permute-start(bf16[96,512]{1,0:T(8,128)(2,1)} %get-tuple-element.129), channel_id=1, source_target_pairs={{0,16},{4,20},{8,24},{12,28},{16,0},{20,4},{24,8},{28,12},{1,17},{... | collective-permute-start | bytes 294920 | tf_op jit(solution)/shard_map/ppermute | solution.py:894
  133.5 5.8 %shard_map.306 = (bf16[784,256]{1,0:T(8,128)(2,1)}, f32[32,2,256]{2,1,0:T(2,128)}, bf16[928,128]{1,0:T(8,128)(2,1)}, bf16[304,128]{1,0:T(8,128)(2,1)}, bf16[304,...) custom-call(s32[6]{0:T(128)S(1)} %stack.19.refs_0_, f32[3]{0:T(128)S(1)} %pad_maximum_fusion.2.refs_1_, ...), custom_call_target="tpu_custom_call" | custom-call | tf_op jit(solution)/shard_map/pallas_call | solution.py:179
  140.2 5.2 %all-to-all-start.3 = ((f32[32,2,256]{2,1,0:T(2,128)}), f32[32,2,256]{2,1,0:T(2,128)S(1)}, u32[]{:S(2)}, u32[]{:S(2)}) async-start(f32[32,2,256]{2,1,0:T(2,128)} %get-tuple-element.123.refs_4_), calls=%async_computation.3 | async-start | bytes 131072 | tf_op jit(solution)/shard_map/all_to_all | solution.py:906
  149.0 8.0 %shard_map.308 = (bf16[2368,128]{1,0:T(8,128)(2,1)}, bf16[2368,128]{1,0:T(8,128)(2,1)}) custom-call(s32[6]{0:T(128)S(1)} %stack.19.refs_0_, bf16[784,512]{1,0:T(8,128)(2,1)} %get-tuple-element.121.refs_1_, bf16[928,128]{1,0:T(8,128)(2,1)} %get-tuple-element.124.refs_2_, bf16[784,512]{1,0:T(8,128)(2,1)} %collective-permute-done.25.refs_15_.refs_3_, ...), custom_call_target="tpu_custom_call" | custom-call | flops 20000000000 | tf_op jit(solution)/shard_map/pallas_call | solution.py:179
  158.4 2.7 %shard_map.309 = (bf16[784,256]{1,0:T(8,128)(2,1)}, bf16[784,256]{1,0:T(8,128)(2,1)}) custom-call(s32[6]{0:T(128)S(1)} %stack.19.refs_0_, f32[3]{0:T(128)S(1)} %pad_maximum_fusion.2.refs_1_, bf16[784,256]{1,0:T(8,128)(2,1)} %get-tuple-element.122.refs_2_, bf16[784,256]{1,0:T(8,128)(2,1)} %collective-permute-done.26.refs_3_, ...), custom_call_target="tpu_custom_call" | custom-call | flops 1000000000 | tf_op jit(solution)/shard_map/pallas_call | solution.py:179
  163.1 2.5 %collective-permute-start.41 = (bf16[96,512]{1,0:T(8,128)(2,1)}, bf16[96,512]{1,0:T(8,128)(2,1)}, u32[]{:S(2)}, u32[]{:S(2)}) collective-permute-start(bf16[96,512]{1,0:T(8,128)(2,1)} %shard_map.307.refs_7_.refs_1_), channel_id=1, source_target_pairs={{0,16},{4,20},{8,24},{12,28},{16,0},{20,4},{24,8},{28,12},{1,17},{... | collective-permute-start | bytes 294920 | tf_op jit(solution)/shard_map/ppermute | solution.py:894
  165.6 4.9 %shard_map.310 = (bf16[256,512]{1,0:T(8,128)(2,1)}, bf16[256,512]{1,0:T(8,128)(2,1)}) custom-call(s32[6]{0:T(128)S(1)} %stack.19.refs_0_, bf16[2,784,512]{2,1,0:T(8,128)(2,1)} %bitcast.68, bf16[784,256]{1,0:T(8,128)(2,1)} %get-tuple-element.132.refs_2_.refs_1_, bf16[784,256]{1,0:T(8,128)(2,1)} %get-tuple-element.133.refs_3_.refs_2_, ...), custom_call_target="tpu_custom_call" | custom-call | tf_op jit(solution)/shard_map/pallas_call | solution.py:179
  172.7 2.4 %shard_map.311 = (bf16[592,128]{1,0:T(8,128)(2,1)}, bf16[592,128]{1,0:T(8,128)(2,1)}, bf16[592,128]{1,0:T(8,128)(2,1)}, bf16[592,128]{1,0:T(8,128)(2,1)}) custom-call(s32[6]{0:T(128)S(1)} %stack.19.refs_0_, bf16[2368,128]{1,0:T(8,128)(2,1)} %get-tuple-element.138.refs_1_, bf16[2368,128]{1,0:T(8,128)(2,1)} %collective-permute-done.36.refs_2_, ...), custom_call_target="tpu_custom_call" | custom-call | tf_op jit(solution)/shard_map/pallas_call | solution.py:179
  177.2 2.9 %collective-permute-start.38 = (bf16[592,128]{1,0:T(8,128)(2,1)}, bf16[592,128]{1,0:T(8,128)(2,1)}, u32[]{:S(2)}, u32[]{:S(2)}) collective-permute-start(bf16[592,128]{1,0:T(8,128)(2,1)} %get-tuple-element.141), channel_id=1, source_target_pairs={{0,16},{4,20},{8,24},{12,28},{16,0},{20,4},{24,8},{28,12},{1,17},{... | collective-permute-start | bytes 454664 | tf_op jit(solution)/shard_map/ppermute | solution.py:894
  185.5 4.8 %collective-permute-done.38.refs_5_ = bf16[592,128]{1,0:T(8,128)(2,1)} collective-permute-done((bf16[592,128]{1,0:T(8,128)(2,1)}, bf16[592,128]{1,0:T(8,128)(2,1)}, u32[]{:S(2)}, u32[]{:S(2)}) %collective-permute-start.38) | collective-permute-done | bytes 151584 | tf_op jit(solution)/shard_map/ppermute | solution.py:894
  191.9 2.4 %collective-permute-start.43 = (bf16[848,128]{1,0:T(8,128)(2,1)S(1)}, bf16[848,128]{1,0:T(8,128)(2,1)S(1)}, u32[]{:S(2)}, u32[]{:S(2)}) collective-permute-start(bf16[848,128]{1,0:T(8,128)(2,1)S(1)} %get-tuple-element.144), channel_id=1, source_target_pairs={{0,8},{4,12},{8,0},{12,4},{16,24},{20,28},{24,16},{28,20},{1,9},{5... | collective-permute-start | bytes 651272 | tf_op jit(solution)/shard_map/ppermute | solution.py:894
  197.4 4.0 %shard_map.314.refs_6_ = f32[2,784,512]{2,1,0:T(8,128)} custom-call(s32[6]{0:T(128)S(1)} %stack.19.refs_0_, bf16[784,256]{1,0:T(8,128)(2,1)} %get-tuple-element.132.refs_2_.refs_1_, bf16[784,256]{1,0:T(8,128)(2,1)} %get-tuple-element.133.refs_3_.refs_2_, bf16[512,256]{1,0:T(8,128)(2,1)} %get-tuple-element.134.refs_3_, ...), custom_call_target="tpu_custom_call" | custom-call | tf_op jit(solution)/shard_map/pallas_call | solution.py:179
  201.4 10.4 %collective-permute-done.44.refs_3_ = bf16[848,128]{1,0:T(8,128)(2,1)S(1)} collective-permute-done((bf16[848,128]{1,0:T(8,128)(2,1)S(1)}, bf16[848,128]{1,0:T(8,128)(2,1)S(1)}, u32[]{:S(2)}, u32[]{:S(2)}) %collective-permute-start.44) | collective-permute-done | bytes 217120 | tf_op jit(solution)/shard_map/ppermute | solution.py:894
  215.6 4.1 %all-to-all-start.4 = ((bf16[32,64,128]{2,1,0:T(8,128)(2,1)}), bf16[32,64,128]{2,1,0:T(8,128)(2,1)S(1)}, u32[]{:S(2)}, u32[]{:S(2)}) async-start(bf16[32,64,128]{2,1,0:T(8,128)(2,1)} %get-tuple-element.147), calls=%async_computation.4 | async-start | bytes 1048576 | tf_op jit(solution)/shard_map/all_to_all | solution.py:1179
  220.7 2.3 shard_map.317
  227.1 8.2 %all-to-all-done.4 = bf16[32,64,128]{2,1,0:T(8,128)(2,1)S(1)} async-done(((bf16[32,64,128]{2,1,0:T(8,128)(2,1)}), bf16[32,64,128]{2,1,0:T(8,128)(2,1)S(1)}, u32[]{:S(2)}, u32[]{:S(2)}) %all-to-all-start.4) | async-done | bytes 524320 | tf_op jit(solution)/shard_map/all_to_all | solution.py:1179
  (167 shorter events, 92.4 us)
Async XLA Ops:
  0.7 17.1 %collective-permute-start.6 = (bf16[9,512,128]{2,1,0:T(8,128)(2,1)}, bf16[9,512,128]{2,1,0:T(8,128)(2,1)}, u32[]{:S(2)}, u32[]{:S(2)}) collective-permute-start(bf16[9,512,128]{2,1,0:T(8,128)(2,1)} %refs_1_.3), channel_id=1, source_target_pairs={{0,1},{1,0},{2,3},{3,2},{4,5},{5,4},{6,7},{7,6},{8,9},{9,8},{10,11... | collective-permute-start | bytes 3538952 | tf_op jit(solution)/shard_map/ppermute | solution.py:881
  16.0 11.6 %collective-permute-start.5 = (bf16[784,256]{1,0:T(8,128)(2,1)S(1)}, bf16[784,256]{1,0:T(8,128)(2,1)S(1)}, u32[]{:S(2)}, u32[]{:S(2)}) collective-permute-start(bf16[784,256]{1,0:T(8,128)(2,1)S(1)} %shard_map.291), channel_id=1, source_target_pairs={{0,2},{1,3},{2,0},{3,1},{4,6},{5,7},{6,4},{7,5},{8,10},{9,11},{10,... | collective-permute-start | bytes 1204232 | tf_op jit(solution)/shard_map/ppermute | solution.py:881
  29.1 14.1 %collective-permute-start.7 = (bf16[784,256]{1,0:T(8,128)(2,1)}, bf16[784,256]{1,0:T(8,128)(2,1)S(1)}, u32[]{:S(2)}, u32[]{:S(2)}) collective-permute-start(bf16[784,256]{1,0:T(8,128)(2,1)} %get-tuple-element.95.refs_2_.refs_8_.refs_4_), channel_id=1, source_target_pairs={{0,2},{1,3},{2,0},{3,1},{4,6},{5,7},{6,4},{7,5},{8,10},{9,11},{10,... | collective-permute-start | bytes 1204232 | tf_op jit(solution)/shard_map/ppermute | solution.py:881
  30.9 12.3 %all-to-all-start = ((f32[32,2,256]{2,1,0:T(2,128)}), f32[32,2,256]{2,1,0:T(2,128)S(1)}, u32[]{:S(2)}, u32[]{:S(2)}) async-start(f32[32,2,256]{2,1,0:T(2,128)} %get-tuple-element.96), calls=%async_computation | async-start | bytes 131072 | tf_op jit(solution)/shard_map/all_to_all | solution.py:906
  48.7 14.6 %collective-permute-start.8 = (bf16[784,256]{1,0:T(8,128)(2,1)}, bf16[784,256]{1,0:T(8,128)(2,1)S(1)}, u32[]{:S(2)}, u32[]{:S(2)}) collective-permute-start(bf16[784,256]{1,0:T(8,128)(2,1)} %get-tuple-element.99.refs_2_.refs_7_.refs_4_), channel_id=1, source_target_pairs={{0,2},{1,3},{2,0},{3,1},{4,6},{5,7},{6,4},{7,5},{8,10},{9,11},{10,... | collective-permute-start | bytes 1204232 | tf_op jit(solution)/shard_map/ppermute | solution.py:881
  65.8 16.9 %collective-permute-start.15 = (bf16[9,256,128]{2,1,0:T(8,128)(2,1)S(1)}, bf16[9,256,128]{2,1,0:T(8,128)(2,1)S(1)}, u32[]{:S(2)}, u32[]{:S(2)}) collective-permute-start(bf16[9,256,128]{2,1,0:T(8,128)(2,1)S(1)} %copy-done.11), channel_id=1, source_target_pairs={{0,2},{1,3},{2,0},{3,1},{4,6},{5,7},{6,4},{7,5},{8,10},{9,11},{10,... | collective-permute-start | bytes 1769480 | tf_op jit(solution)/shard_map/ppermute | solution.py:881
  100.5 10.4 %collective-permute-start.22 = (bf16[9,256,128]{2,1,0:T(8,128)(2,1)S(1)}, bf16[9,256,128]{2,1,0:T(8,128)(2,1)S(1)}, u32[]{:S(2)}, u32[]{:S(2)}) collective-permute-start(bf16[9,256,128]{2,1,0:T(8,128)(2,1)S(1)} %collective-permute-done.15.refs_12_.refs_2_), channel_id=1, source_target_pairs={{0,1},{1,0},{2,3},{3,2},{4,5},{5,4},{6,7},{7,6},{8,9},{9,8},{10,11... | collective-permute-start | bytes 1769480 | tf_op jit(solution)/shard_map/ppermute | solution.py:881
  101.0 32.0 %collective-permute-start.25 = (bf16[784,512]{1,0:T(8,128)(2,1)}, bf16[784,512]{1,0:T(8,128)(2,1)}, u32[]{:S(2)}, u32[]{:S(2)}) collective-permute-start(bf16[784,512]{1,0:T(8,128)(2,1)} %get-tuple-element.121.refs_1_), channel_id=1, source_target_pairs={{0,1},{1,0},{2,3},{3,2},{4,5},{5,4},{6,7},{7,6},{8,9},{9,8},{10,11... | collective-permute-start | bytes 2408456 | tf_op jit(solution)/shard_map/ppermute | solution.py:881
  103.1 11.7 %collective-permute-start.21 = (bf16[784,256]{1,0:T(8,128)(2,1)S(1)}, bf16[784,256]{1,0:T(8,128)(2,1)S(1)}, u32[]{:S(2)}, u32[]{:S(2)}) collective-permute-start(bf16[784,256]{1,0:T(8,128)(2,1)S(1)} %shard_map.301), channel_id=1, source_target_pairs={{0,2},{1,3},{2,0},{3,1},{4,6},{5,7},{6,4},{7,5},{8,10},{9,11},{10,... | collective-permute-start | bytes 1204232 | tf_op jit(solution)/shard_map/ppermute | solution.py:881
  108.9 17.7 %collective-permute-start.24 = (bf16[384,512]{1,0:T(8,128)(2,1)}, bf16[384,512]{1,0:T(8,128)(2,1)}, u32[]{:S(2)}, u32[]{:S(2)}) collective-permute-start(bf16[384,512]{1,0:T(8,128)(2,1)} %get-tuple-element.115.refs_4_), channel_id=1, source_target_pairs={{0,4},{4,0},{8,12},{12,8},{16,20},{20,16},{24,28},{28,24},{1,5},{5... | collective-permute-start | bytes 1179656 | tf_op jit(solution)/shard_map/ppermute | solution.py:894
  119.6 13.9 %collective-permute-start.23 = (bf16[784,256]{1,0:T(8,128)(2,1)}, bf16[784,256]{1,0:T(8,128)(2,1)}, u32[]{:S(2)}, u32[]{:S(2)}) collective-permute-start(bf16[784,256]{1,0:T(8,128)(2,1)} %get-tuple-element.117.refs_2_), channel_id=1, source_target_pairs={{0,2},{1,3},{2,0},{3,1},{4,6},{5,7},{6,4},{7,5},{8,10},{9,11},{10,... | collective-permute-start | bytes 1204232 | tf_op jit(solution)/shard_map/ppermute | solution.py:881
  121.1 12.4 %all-to-all-start.2 = ((f32[32,4,256]{2,1,0:T(4,128)}), f32[32,4,256]{2,1,0:T(4,128)S(1)}, u32[]{:S(2)}, u32[]{:S(2)}) async-start(f32[32,4,256]{2,1,0:T(4,128)} %get-tuple-element.116), calls=%async_computation.2 | async-start | bytes 262144 | tf_op jit(solution)/shard_map/all_to_all | solution.py:906
  128.6 11.3 %collective-permute-start.30 = (bf16[96,512]{1,0:T(8,128)(2,1)}, bf16[96,512]{1,0:T(8,128)(2,1)}, u32[]{:S(2)}, u32[]{:S(2)}) collective-permute-start(bf16[96,512]{1,0:T(8,128)(2,1)} %get-tuple-element.128), channel_id=1, source_target_pairs={{0,8},{4,12},{8,0},{12,4},{16,24},{20,28},{24,16},{28,20},{1,9},{5... | collective-permute-start | bytes 294920 | tf_op jit(solution)/shard_map/ppermute | solution.py:894
  130.4 15.0 %collective-permute-start.31 = (bf16[96,512]{1,0:T(8,128)(2,1)}, bf16[96,512]{1,0:T(8,128)(2,1)}, u32[]{:S(2)}, u32[]{:S(2)}) collective-permute-start(bf16[96,512]{1,0:T(8,128)(2,1)} %get-tuple-element.129), channel_id=1, source_target_pairs={{0,16},{4,20},{8,24},{12,28},{16,0},{20,4},{24,8},{28,12},{1,17},{... | collective-permute-start | bytes 294920 | tf_op jit(solution)/shard_map/ppermute | solution.py:894
  132.8 14.4 %collective-permute-start.32 = (bf16[96,512]{1,0:T(8,128)(2,1)}, bf16[96,512]{1,0:T(8,128)(2,1)}, u32[]{:S(2)}, u32[]{:S(2)}) collective-permute-start(bf16[96,512]{1,0:T(8,128)(2,1)} %get-tuple-element.130), channel_id=1, source_target_pairs={{0,24},{4,28},{8,16},{12,20},{16,8},{20,12},{24,0},{28,4},{1,25},{... | collective-permute-start | bytes 294920 | tf_op jit(solution)/shard_map/ppermute | solution.py:894
  139.4 9.6 %collective-permute-start.29 = (bf16[320,128]{1,0:T(8,128)(2,1)}, bf16[320,128]{1,0:T(8,128)(2,1)}, u32[]{:S(2)}, u32[]{:S(2)}) collective-permute-start(bf16[320,128]{1,0:T(8,128)(2,1)} %get-tuple-element.127), channel_id=1, source_target_pairs={{0,1},{1,0},{2,3},{3,2},{4,5},{5,4},{6,7},{7,6},{8,9},{9,8},{10,11... | collective-permute-start | bytes 245768 | tf_op jit(solution)/shard_map/ppermute | solution.py:881
  139.7 9.3 %collective-permute-start.27 = (bf16[304,128]{1,0:T(8,128)(2,1)}, bf16[304,128]{1,0:T(8,128)(2,1)}, u32[]{:S(2)}, u32[]{:S(2)}) collective-permute-start(bf16[304,128]{1,0:T(8,128)(2,1)} %get-tuple-element.125), channel_id=1, source_target_pairs={{0,1},{1,0},{2,3},{3,2},{4,5},{5,4},{6,7},{7,6},{8,9},{9,8},{10,11... | collective-permute-start | bytes 233480 | tf_op jit(solution)/shard_map/ppermute | solution.py:881
  140.2 18.2 %all-to-all-start.3 = ((f32[32,2,256]{2,1,0:T(2,128)}), f32[32,2,256]{2,1,0:T(2,128)S(1)}, u32[]{:S(2)}, u32[]{:S(2)}) async-start(f32[32,2,256]{2,1,0:T(2,128)} %get-tuple-element.123.refs_4_), calls=%async_computation.3 | async-start | bytes 131072 | tf_op jit(solution)/shard_map/all_to_all | solution.py:906
  145.4 13.0 %collective-permute-start.26 = (bf16[784,256]{1,0:T(8,128)(2,1)}, bf16[784,256]{1,0:T(8,128)(2,1)}, u32[]{:S(2)}, u32[]{:S(2)}) collective-permute-start(bf16[784,256]{1,0:T(8,128)(2,1)} %get-tuple-element.122.refs_2_), channel_id=1, source_target_pairs={{0,2},{1,3},{2,0},{3,1},{4,6},{5,7},{6,4},{7,5},{8,10},{9,11},{10,... | collective-permute-start | bytes 1204232 | tf_op jit(solution)/shard_map/ppermute | solution.py:881
  156.9 15.8 %collective-permute-start.36 = (bf16[2368,128]{1,0:T(8,128)(2,1)}, bf16[2368,128]{1,0:T(8,128)(2,1)}, u32[]{:S(2)}, u32[]{:S(2)}) collective-permute-start(bf16[2368,128]{1,0:T(8,128)(2,1)} %get-tuple-element.131.refs_10_), channel_id=1, source_target_pairs={{0,4},{4,0},{8,12},{12,8},{16,20},{20,16},{24,28},{28,24},{1,5},{5... | collective-permute-start | bytes 1818632 | tf_op jit(solution)/shard_map/ppermute | solution.py:894
  161.6 15.6 %collective-permute-start.40 = (bf16[96,512]{1,0:T(8,128)(2,1)}, bf16[96,512]{1,0:T(8,128)(2,1)}, u32[]{:S(2)}, u32[]{:S(2)}) collective-permute-start(bf16[96,512]{1,0:T(8,128)(2,1)} %shard_map.307.refs_7_.refs_1_), channel_id=1, source_target_pairs={{0,8},{4,12},{8,0},{12,4},{16,24},{20,28},{24,16},{28,20},{1,9},{5... | collective-permute-start | bytes 294920 | tf_op jit(solution)/shard_map/ppermute | solution.py:894
  163.1 17.0 %collective-permute-start.41 = (bf16[96,512]{1,0:T(8,128)(2,1)}, bf16[96,512]{1,0:T(8,128)(2,1)}, u32[]{:S(2)}, u32[]{:S(2)}) collective-permute-start(bf16[96,512]{1,0:T(8,128)(2,1)} %shard_map.307.refs_7_.refs_1_), channel_id=1, source_target_pairs={{0,16},{4,20},{8,24},{12,28},{16,0},{20,4},{24,8},{28,12},{1,17},{... | collective-permute-start | bytes 294920 | tf_op jit(solution)/shard_map/ppermute | solution.py:894
  170.5 19.8 %collective-permute-start.35 = (bf16[256,512]{1,0:T(8,128)(2,1)}, bf16[256,512]{1,0:T(8,128)(2,1)}, u32[]{:S(2)}, u32[]{:S(2)}) collective-permute-start(bf16[256,512]{1,0:T(8,128)(2,1)} %get-tuple-element.137.refs_3_), channel_id=1, source_target_pairs={{0,4},{4,0},{8,12},{12,8},{16,20},{20,16},{24,28},{28,24},{1,5},{5... | collective-permute-start | bytes 786440 | tf_op jit(solution)/shard_map/ppermute | solution.py:894
  175.1 10.4 %collective-permute-start.37 = (bf16[592,128]{1,0:T(8,128)(2,1)}, bf16[592,128]{1,0:T(8,128)(2,1)}, u32[]{:S(2)}, u32[]{:S(2)}) collective-permute-start(bf16[592,128]{1,0:T(8,128)(2,1)} %get-tuple-element.140), channel_id=1, source_target_pairs={{0,8},{4,12},{8,0},{12,4},{16,24},{20,28},{24,16},{28,20},{1,9},{5... | collective-permute-start | bytes 454664 | tf_op jit(solution)/shard_map/ppermute | solution.py:894
  177.2 13.2 %collective-permute-start.38 = (bf16[592,128]{1,0:T(8,128)(2,1)}, bf16[592,128]{1,0:T(8,128)(2,1)}, u32[]{:S(2)}, u32[]{:S(2)}) collective-permute-start(bf16[592,128]{1,0:T(8,128)(2,1)} %get-tuple-element.141), channel_id=1, source_target_pairs={{0,16},{4,20},{8,24},{12,28},{16,0},{20,4},{24,8},{28,12},{1,17},{... | collective-permute-start | bytes 454664 | tf_op jit(solution)/shard_map/ppermute | solution.py:894
  180.1 10.2 %collective-permute-start.39 = (bf16[592,128]{1,0:T(8,128)(2,1)}, bf16[592,128]{1,0:T(8,128)(2,1)}, u32[]{:S(2)}, u32[]{:S(2)}) collective-permute-start(bf16[592,128]{1,0:T(8,128)(2,1)} %get-tuple-element.142), channel_id=1, source_target_pairs={{0,24},{4,28},{8,16},{12,20},{16,8},{20,12},{24,0},{28,4},{1,25},{... | collective-permute-start | bytes 454664 | tf_op jit(solution)/shard_map/ppermute | solution.py:894
  182.6 18.8 %collective-permute-start.46 = (bf16[384,512]{1,0:T(8,128)(2,1)}, bf16[384,512]{1,0:T(8,128)(2,1)S(1)}, u32[]{:S(2)}, u32[]{:S(2)}) collective-permute-start(bf16[384,512]{1,0:T(8,128)(2,1)} %shard_map.312.refs_7_.refs_1_), channel_id=1, source_target_pairs={{0,4},{4,0},{8,12},{12,8},{16,20},{20,16},{24,28},{28,24},{1,5},{5... | collective-permute-start | bytes 1179656 | tf_op jit(solution)/shard_map/ppermute | solution.py:894
  191.9 9.5 %collective-permute-start.43 = (bf16[848,128]{1,0:T(8,128)(2,1)S(1)}, bf16[848,128]{1,0:T(8,128)(2,1)S(1)}, u32[]{:S(2)}, u32[]{:S(2)}) collective-permute-start(bf16[848,128]{1,0:T(8,128)(2,1)S(1)} %get-tuple-element.144), channel_id=1, source_target_pairs={{0,8},{4,12},{8,0},{12,4},{16,24},{20,28},{24,16},{28,20},{1,9},{5... | collective-permute-start | bytes 651272 | tf_op jit(solution)/shard_map/ppermute | solution.py:894
  194.3 17.5 %collective-permute-start.44 = (bf16[848,128]{1,0:T(8,128)(2,1)S(1)}, bf16[848,128]{1,0:T(8,128)(2,1)S(1)}, u32[]{:S(2)}, u32[]{:S(2)}) collective-permute-start(bf16[848,128]{1,0:T(8,128)(2,1)S(1)} %get-tuple-element.145), channel_id=1, source_target_pairs={{0,16},{4,20},{8,24},{12,28},{16,0},{20,4},{24,8},{28,12},{1,17},{... | collective-permute-start | bytes 651272 | tf_op jit(solution)/shard_map/ppermute | solution.py:894
  195.3 16.5 %collective-permute-start.45 = (bf16[848,128]{1,0:T(8,128)(2,1)S(1)}, bf16[848,128]{1,0:T(8,128)(2,1)S(1)}, u32[]{:S(2)}, u32[]{:S(2)}) collective-permute-start(bf16[848,128]{1,0:T(8,128)(2,1)S(1)} %get-tuple-element.146), channel_id=1, source_target_pairs={{0,24},{4,28},{8,16},{12,20},{16,8},{20,12},{24,0},{28,4},{1,25},{... | collective-permute-start | bytes 651272 | tf_op jit(solution)/shard_map/ppermute | solution.py:894
  213.2 11.7 %collective-permute-start.47 = (bf16[2368,128]{1,0:T(8,128)(2,1)S(1)}, bf16[2368,128]{1,0:T(8,128)(2,1)S(1)}, u32[]{:S(2)}, u32[]{:S(2)}) collective-permute-start(bf16[2368,128]{1,0:T(8,128)(2,1)S(1)} %get-tuple-element.148.refs_1_.refs_3_), channel_id=1, source_target_pairs={{0,4},{4,0},{8,12},{12,8},{16,20},{20,16},{24,28},{28,24},{1,5},{5... | collective-permute-start | bytes 1818632 | tf_op jit(solution)/shard_map/ppermute | solution.py:894
  215.6 19.7 %all-to-all-start.4 = ((bf16[32,64,128]{2,1,0:T(8,128)(2,1)}), bf16[32,64,128]{2,1,0:T(8,128)(2,1)S(1)}, u32[]{:S(2)}, u32[]{:S(2)}) async-start(bf16[32,64,128]{2,1,0:T(8,128)(2,1)} %get-tuple-element.147), calls=%async_computation.4 | async-start | bytes 1048576 | tf_op jit(solution)/shard_map/all_to_all | solution.py:1179
  (36 other events, 320.4 us)
